TPU v7x, 256 devices: a whole 4x4x8 slice. The times are simulated.
256 devices in a mesh: lon: 8 (over y, x_hi), lat: 16 (over z, core), batch: 2 (over x_lo).
Axes of the slice: x: 4 (x_hi: 2, x_lo: 2; x = x_hi * 2 + x_lo), y: 4, z: 8, core: 2. Of those that a mesh axis runs over, the one named last changes fastest.
Arguments:
- fields: bfloat16 [576, 384, 512], P(('batch', 'lat'), 'lon'), parts along dimension 0, may hold values from -6 to 6
- grad_out: bfloat16 [576, 384, 512], P(('batch', 'lat'), 'lon'), parts along dimension 0, may hold values from -6 to 6
- layernorm_gain: float32 [512], replicated, may hold values from 0.1 to 1.9
- qkv_weight: bfloat16 [512, 1536], replicated, may hold values from -0.25 to 0.25
- proj_weight: bfloat16 [512, 512], replicated, may hold values from -0.25 to 0.25
- bias_table: float32 [8, 253], replicated, may hold values from -4 to 350
- sea_mask: int32 [576, 384], P(('batch', 'lat'), 'lon'), parts along dimension 0, may hold values from 0 to 1
Outputs:
- updated: bfloat16 [576, 384, 512], P(('batch', 'lat'), 'lon'), parts along dimension 0
- grad_in: bfloat16 [576, 384, 512], P(('batch', 'lat'), 'lon'), parts along dimension 0
- grad_gain: float32 [1024], P('batch'), parts along dimension 0
- grad_bias: float32 [16, 253], P('batch'), parts along dimension 0
- grad_qkv: float32 [1024, 1536], P(('batch', 'lon', 'lat')), parts along dimension 0
- grad_proj: float32 [1024, 512], P(('batch', 'lon', 'lat')), parts along dimension 0
There are 2 independent parts, one for each index of `batch`. A program takes and returns all parts, laid end to end along the dimension named above; an argument that names none is the same for every part. Nothing has to cross between parts.
All inputs are finite; a program needn't handle non-finite values.
Results may differ from a plain program's by a relative error of at most 0.0093.
Values may be sent and summed in bfloat16 or wider, within the bound.
A program may use at most 128 MiB of HBM per device.

v0:
```python
import jax
import jax.numpy as jnp
import numpy as np
from jax import lax
from jax.sharding import PartitionSpec as P

HEADS = 8
HEAD_DIM = 64
WIN_LAT = 6
WIN_LON = 12


def shifted(x, axis, by):
    devices = lax.axis_size(axis)
    return lax.ppermute(x, axis, [(i, (i + by) % devices) for i in range(devices)])


def relative_index():
    places = np.arange(WIN_LAT * WIN_LON)
    row_of = places // WIN_LON
    col_of = places % WIN_LON
    return (row_of[:, None] - row_of[None, :] + WIN_LAT - 1) * (2 * WIN_LON - 1) + (
        col_of[:, None] - col_of[None, :] + WIN_LON - 1
    )


def contract(form, left, right):
    return jnp.einsum(form, left, right, preferred_element_type=jnp.float32)


def window_forward(
    windows_x, window_sea, window_class, layernorm_gain, qkv_weight, proj_weight, position_bias
):
    win_count, tokens, model_width = windows_x.shape
    score_scale = HEAD_DIM ** (-0.5)
    fields32 = windows_x.astype(jnp.float32)
    average = jnp.mean(fields32, axis=-1, keepdims=True)
    mean_removed = fields32 - average
    inverse_deviation = lax.rsqrt(
        jnp.mean(mean_removed * mean_removed, axis=-1, keepdims=True) + 1e-05
    )
    standardized_input = mean_removed * inverse_deviation
    normalized_input = (standardized_input * layernorm_gain).astype(jnp.bfloat16)
    packed = contract("btc,cf->btf", normalized_input, qkv_weight).astype(jnp.bfloat16)
    head_parts = packed.reshape(win_count, tokens, 3, HEADS, HEAD_DIM)
    query_rows = head_parts[:, :, 0]
    key_portion = head_parts[:, :, 1]
    value_rows = head_parts[:, :, 2]
    scores = (
        contract("bqhd,bkhd->bhqk", query_rows, key_portion) * score_scale + position_bias[None]
    )
    allowed = window_class[:, None, :, None] == window_class[:, None, None, :]
    scores = jnp.where(allowed, scores, -1000000000.0)
    attention_weights = jax.nn.softmax(scores, axis=-1)
    rounded_values = attention_weights.astype(jnp.bfloat16)
    attended_tokens = (
        contract("bhqk,bkhd->bqhd", rounded_values, value_rows)
        .astype(jnp.bfloat16)
        .reshape(win_count, tokens, model_width)
    )
    projected = contract("btc,cd->btd", attended_tokens, proj_weight)
    ocean_weight = window_sea.astype(jnp.float32)[..., None]
    sublayer_output = (fields32 + ocean_weight * projected).astype(jnp.bfloat16)
    return (
        sublayer_output,
        (
            standardized_input,
            inverse_deviation,
            normalized_input,
            query_rows,
            key_portion,
            value_rows,
            attention_weights,
            rounded_values,
            attended_tokens,
            ocean_weight,
        ),
    )


def window_backward(saved_residuals, window_dy, layernorm_gain, qkv_weight, proj_weight):
    (
        standardized_input,
        inverse_deviation,
        normalized_input,
        query_rows,
        key_portion,
        value_rows,
        attention_weights,
        rounded_values,
        attended_tokens,
        ocean_weight,
    ) = saved_residuals
    win_count, tokens, model_width = normalized_input.shape
    score_scale = HEAD_DIM ** (-0.5)
    dy_float = window_dy.astype(jnp.float32)
    grad_z = (ocean_weight * dy_float).astype(jnp.bfloat16)
    grad_mixed = contract("btd,cd->btc", grad_z, proj_weight).astype(jnp.bfloat16)
    grad_heads = grad_mixed.reshape(win_count, tokens, HEADS, HEAD_DIM)
    grad_probs = contract("bqhd,bkhd->bhqk", grad_heads, value_rows)
    grad_values = contract("bhqk,bqhd->bkhd", rounded_values, grad_heads).astype(jnp.bfloat16)
    grad_scores = attention_weights * (
        grad_probs - jnp.sum(attention_weights * grad_probs, axis=-1, keepdims=True)
    )
    scaled = (grad_scores * score_scale).astype(jnp.bfloat16)
    grad_query = contract("bhqk,bkhd->bqhd", scaled, key_portion).astype(jnp.bfloat16)
    grad_keys = contract("bhqk,bqhd->bkhd", scaled, query_rows).astype(jnp.bfloat16)
    grad_packed = jnp.stack([grad_query, grad_keys, grad_values], axis=2).reshape(
        win_count, tokens, 3 * model_width
    )
    gradient_normalized = contract("btf,cf->btc", grad_packed, qkv_weight)
    gain_product = jnp.sum(gradient_normalized * standardized_input, axis=(0, 1))
    gradient_standardized = gradient_normalized * layernorm_gain
    inner_product = (
        gradient_standardized
        - jnp.mean(gradient_standardized, axis=-1, keepdims=True)
        - standardized_input
        * jnp.mean(gradient_standardized * standardized_input, axis=-1, keepdims=True)
    )
    grad_fields = (dy_float + inverse_deviation * inner_product).astype(jnp.bfloat16)
    bias_term = jnp.sum(grad_scores, axis=0)
    return (grad_fields, grad_packed, grad_z, gain_product, bias_term)


def frame_windows(grid):
    lat_wins = grid.shape[0] // WIN_LAT
    lon_wins = grid.shape[1] // WIN_LON
    shaped = grid.reshape(lat_wins, WIN_LAT, lon_wins, WIN_LON, grid.shape[2]).transpose(
        0, 2, 1, 3, 4
    )
    return shaped.reshape(lat_wins * lon_wins, WIN_LAT * WIN_LON, grid.shape[2])


def frame_grid(windows, row_count, col_count):
    lat_wins = row_count // WIN_LAT
    lon_wins = col_count // WIN_LON
    shaped = windows.reshape(lat_wins, lon_wins, WIN_LAT, WIN_LON, windows.shape[-1]).transpose(
        0, 2, 1, 3, 4
    )
    return shaped.reshape(row_count, col_count, windows.shape[-1])


def transposed_product(left, right):
    return lax.dot_general(
        left, right, (((0,), (0,)), ((), ())), preferred_element_type=jnp.float32
    )


def on_device(fields, grad_out, layernorm_gain, qkv_weight, proj_weight, bias_table, sea_mask):
    row_count, col_count, model_width = fields.shape
    half_lat = WIN_LAT // 2
    half_lon = WIN_LON // 2
    sea_flag = sea_mask.astype(jnp.bfloat16)[..., None]
    at_end = lax.axis_index("lat") == lax.axis_size("lat") - 1
    wrap_side = jnp.logical_and(at_end, jnp.arange(row_count) >= row_count - half_lat).astype(
        jnp.int32
    )
    side_grid = jnp.broadcast_to(wrap_side[:, None, None], (row_count, col_count, 1))
    rel_index = relative_index()
    position_bias = bias_table[:, rel_index]
    lon_in = shifted((fields[:, :half_lon], sea_flag[:, :half_lon]), "lon", -1)
    lon_x = jnp.concatenate([fields[:, half_lon:], lon_in[0]], axis=1)
    lon_flag = jnp.concatenate([sea_flag[:, half_lon:], lon_in[1]], axis=1)
    lat_in = shifted((lon_x[:half_lat], lon_flag[:half_lat]), "lat", -1)
    frame_x = jnp.concatenate([lon_x[half_lat:], lat_in[0]], axis=0)
    frame_flag = jnp.concatenate([lon_flag[half_lat:], lat_in[1]], axis=0)
    windows_x = frame_windows(frame_x)
    window_sea = frame_windows(frame_flag)[..., 0].astype(jnp.int32)
    window_class = window_sea + 2 * frame_windows(side_grid)[..., 0]
    picked = None
    out_windows, saved_residuals = window_forward(
        windows_x, window_sea, window_class, layernorm_gain, qkv_weight, proj_weight, position_bias
    )
    frame_out, saved_residuals, picked = (
        frame_grid(out_windows, row_count, col_count),
        saved_residuals,
        picked,
    )
    out_lat = shifted(frame_out[row_count - half_lat :], "lat", 1)
    lat_out = jnp.concatenate([out_lat, frame_out[: row_count - half_lat]], axis=0)
    out_lon = shifted(lat_out[:, col_count - half_lon :], "lon", 1)
    updated = jnp.concatenate([out_lon, lat_out[:, : col_count - half_lon]], axis=1)
    dy_lon = shifted(grad_out[:, :half_lon], "lon", -1)
    lon_dy = jnp.concatenate([grad_out[:, half_lon:], dy_lon], axis=1)
    dy_lat = shifted(lon_dy[:half_lat], "lat", -1)
    frame_dy = jnp.concatenate([lon_dy[half_lat:], dy_lat], axis=0)
    windows_dy = frame_windows(frame_dy)
    dx_windows, grad_packed, grad_z, gain_product, bias_term = window_backward(
        saved_residuals, windows_dy, layernorm_gain, qkv_weight, proj_weight
    )
    frame_dx, grad_packed, grad_z, gain_product, bias_term = (
        frame_grid(dx_windows, row_count, col_count),
        grad_packed,
        grad_z,
        gain_product,
        bias_term,
    )
    dx_lat = shifted(frame_dx[row_count - half_lat :], "lat", 1)
    lat_dx = jnp.concatenate([dx_lat, frame_dx[: row_count - half_lat]], axis=0)
    dx_lon = shifted(lat_dx[:, col_count - half_lon :], "lon", 1)
    grad_in = jnp.concatenate([dx_lon, lat_dx[:, : col_count - half_lon]], axis=1)
    normed_flat = saved_residuals[2].reshape(-1, model_width)
    mixed_flat = saved_residuals[8].reshape(-1, model_width)
    packed_flat = grad_packed.reshape(-1, 3 * model_width)
    grad_z_flat = grad_z.reshape(-1, model_width)
    bias_local = (
        jnp.zeros((HEADS, bias_table.shape[1]), jnp.float32)
        .at[:, rel_index.reshape(-1)]
        .add(bias_term.reshape(HEADS, -1))
    )
    share = model_width // lax.axis_size(("lon", "lat"))
    full_qkv = transposed_product(normed_flat, packed_flat)
    full_proj = transposed_product(mixed_flat, grad_z_flat)
    sum_qkv, sum_proj, grad_gain, grad_bias = lax.psum(
        (full_qkv, full_proj, gain_product, bias_local), ("lon", "lat")
    )
    first_row = lax.axis_index(("lon", "lat")) * share
    grad_qkv = lax.dynamic_slice_in_dim(sum_qkv, first_row, share, 0)
    grad_proj = lax.dynamic_slice_in_dim(sum_proj, first_row, share, 0)
    return (updated, grad_in, grad_gain, grad_bias, grad_qkv, grad_proj)


def solution(mesh):
    placed = (
        P(("batch", "lat"), "lon", None),
        P(("batch", "lat"), "lon", None),
        P(),
        P(),
        P(),
        P(),
        P(("batch", "lat"), "lon"),
    )
    return jax.shard_map(
        on_device,
        mesh=mesh,
        in_specs=placed,
        out_specs=(
            P(("batch", "lat"), "lon", None),
            P(("batch", "lat"), "lon", None),
            P("batch"),
            P("batch", None),
            P(("batch", "lon", "lat"), None),
            P(("batch", "lon", "lat"), None),
        ),
        check_vma=False,
    )
```

profile of v0, /device:TPU:2, one launch (start us, length us, event | category | flops | bytes accessed | tf_op | source)
XLA Modules:
  0.0 1470.5 jit_solution(4595077272491530499)
XLA Ops:
  8.1 4.6 collective-permute-start.2
  22.5 10.6 gather_fusion
  33.1 3.2 copy.94
  37.1 4.5 collective-permute-start.3
  59.7 3.3 multiply_convert_fusion.2
  66.4 3.5 copy.98
  72.5 3.2 convolution_convert_fusion.5
  78.1 3.1 convolution_convert_fusion
  81.3 7.6 reshape.187
  88.8 5.0 fusion.60
  93.9 3.8 copy.120
  97.7 3.8 copy.119
  101.5 4.0 copy.121
  105.6 6.3 fusion.62
  111.8 4.5 convolution_convert_fusion.4
  121.5 8.1 fusion.24
  129.6 8.0 fusion.21
  147.3 5.7 pad_maximum_fusion
  153.0 8.7 copy.104
  161.6 3.8 copy.110
  165.5 3.7 reshape_reshape.7
  169.2 8.0 reshape_reshape.6
  177.2 3.3 fusion.73
  180.5 4.7 fusion.72
  185.2 7.8 reshape.192
  193.0 3.1 add_convert_fusion.1
  204.9 4.0 multiply_reduce_fusion.2
  215.2 6.9 fusion.63
  226.9 30.9 %scatter_custom_fusion = f32[8,253]{0,1:T(8,128)S(1)} fusion(s32[5184]{0:T(1024)S(1)} %copy-done.13, f32[5184,8]{1,0:T(8,128)} %copy.107, f32[]{:T(128)} %constant.21.clone.1), kind=kCustom, calls=%fused_computation.73 | custom fusion | flops 41472 | bytes 8608 | tf_op jit(solution)/shard_map/scatter-add | solution.py:209
  257.8 648.4 %all-reduce = (f32[512]{0:T(512)}, f32[8,253]{0,1:T(8,128)S(1)}) all-reduce(f32[512]{0:T(512)S(1)} %get-tuple-element.30, f32[8,253]{0,1:T(8,128)S(1)} %scatter_custom_fusion), channel_id=1, replica_groups=mesh['lon'=8,'lat'=16,'batch'=2] {'lon','lat'}, use_global_device_ids=true, to_apply=%region_8.9 | all-reduce | flops 2536 | bytes 20288 | tf_op jit(solution)/shard_map/psum | solution.py:214
  908.6 8.0 collective-permute-done.5
  920.9 539.6 %all-reduce.4.cloned.1.call-done = (f32[512,1536]{1,0:T(8,128)}, f32[512,512]{1,0:T(8,128)}) async-done(((f32[512,1536]{1,0:T(8,128)}, f32[512,512]{1,0:T(8,128)}), (f32[512,1536]{1,0:T(8,128)}, f32[512,512]{1,0:T(8,128)})) %all-reduce.4.cloned.1.call-update) | async-done | bytes 4194320 | tf_op jit(solution)/shard_map/psum | solution.py:214
  (122 shorter events, 82.1 us)
Async XLA Ops:
  7.2 71.0 %copy-start = (bf16[512,1536]{1,0:T(8,128)(2,1)S(1)}, bf16[512,1536]{1,0:T(8,128)(2,1)}, u32[]{:S(2)}) copy-start(bf16[512,1536]{1,0:T(8,128)(2,1)} %param.14) | copy-start | bytes 4718596
  7.2 1453.4 %all-reduce.4.cloned.1.call-start = ((), (), s32[]{:S(2)}) async-start(), calls=%async_computation | async-start | bytes 8388608 | tf_op jit(solution)/shard_map/psum | solution.py:214
  7.2 13.9 copy-start.11
  8.1 28.2 %collective-permute-start.2 = (bf16[18,6,1]{1,0,2:T(8,128)(2,1)S(1)}, bf16[18,6,1]{1,0,2:T(8,128)(2,1)}, u32[]{:S(2)}, u32[]{:S(2)}) collective-permute-start(bf16[18,6,1]{1,0,2:T(8,128)(2,1)S(1)} %bitcast.106), channel_id=1, source_target_pairs={{0,224},{32,0},{64,32},{96,64},{128,96},{160,128},{192,160},{224,1... | collective-permute-start | bytes 656 | tf_op jit(solution)/shard_map/ppermute | solution.py:15
  14.3 33.4 %collective-permute-start.6 = (bf16[18,6,512]{2,1,0:T(8,128)(2,1)}, bf16[18,6,512]{2,1,0:T(8,128)(2,1)}, u32[]{:S(2)}, u32[]{:S(2)}) collective-permute-start(bf16[18,6,512]{2,1,0:T(8,128)(2,1)} %slice.85), channel_id=1, source_target_pairs={{0,224},{32,0},{64,32},{96,64},{128,96},{160,128},{192,160},{224,1... | collective-permute-start | bytes 331784 | tf_op jit(solution)/shard_map/ppermute | solution.py:15
  17.2 26.7 %collective-permute-start = (bf16[18,6,512]{2,1,0:T(8,128)(2,1)}, bf16[18,6,512]{2,1,0:T(8,128)(2,1)}, u32[]{:S(2)}, u32[]{:S(2)}) collective-permute-start(bf16[18,6,512]{2,1,0:T(8,128)(2,1)} %slice.70), channel_id=1, source_target_pairs={{0,224},{32,0},{64,32},{96,64},{128,96},{160,128},{192,160},{224,1... | collective-permute-start | bytes 331784 | tf_op jit(solution)/shard_map/ppermute | solution.py:15
  19.6 1.9 copy-start.13
  37.1 5.8 collective-permute-start.3
  44.7 7.2 collective-permute-start.1
  49.0 7.5 collective-permute-start.7
  53.6 2.4 copy-start.1
  55.7 1.2 copy-start.10
  57.9 1.8 copy-start.14
  59.7 3.3 copy-start.2
  101.5 4.0 copy-start.12
  111.8 4.5 copy-start.5
  111.8 4.5 copy-start.15
  111.8 4.5 copy-start.16
  116.3 2.2 copy-start.6
  177.2 3.3 copy-start.4
  204.4 4.5 copy-start.3
  204.4 702.5 %collective-permute-start.4 = (bf16[3,48,512]{2,1,0:T(8,128)(2,1)}, bf16[3,48,512]{2,1,0:T(8,128)(2,1)}, u32[]{:S(2)}, u32[]{:S(2)}) collective-permute-start(bf16[3,48,512]{2,1,0:T(8,128)(2,1)} %slice.103), channel_id=1, source_target_pairs={{0,2},{2,4},{4,6},{6,8},{8,10},{10,12},{12,14},{14,16},{16,18},{18... | collective-permute-start | bytes 442376 | tf_op jit(solution)/shard_map/ppermute | solution.py:15
  214.2 1.0 copy-start.8
  215.0 7.1 copy-start.7
  215.0 692.7 %collective-permute-start.8 = (bf16[3,48,512]{2,1,0:T(8,128)(2,1)}, bf16[3,48,512]{2,1,0:T(8,128)(2,1)}, u32[]{:S(2)}, u32[]{:S(2)}) collective-permute-start(bf16[3,48,512]{2,1,0:T(8,128)(2,1)} %slice.107), channel_id=1, source_target_pairs={{0,2},{2,4},{4,6},{6,8},{8,10},{10,12},{12,14},{14,16},{16,18},{18... | collective-permute-start | bytes 442376 | tf_op jit(solution)/shard_map/ppermute | solution.py:15
  222.1 1.2 copy-start.9
  907.6 8.9 collective-permute-start.5
  908.5 10.2 collective-permute-start.9
Sparse Core Ops, SparseCore 0:
  185.3 1275.2 all-reduce.3
where the time goes:
time: 1480 us; the launch traced here: 1470 us
  blocking collectives  648 us (44%)
  waiting for transfers between devices  548 us (37%)
  local copies, waits for them, and re-layouts  121 us (8%)
  other arithmetic  68.1 us (5%)
  matrix products  53.3 us (4%)
  starting transfers between devices  16.5 us (1%)
  between operations  14.8 us (1%)
    psum x1, blocking collectives, on_device(): lax.psum((full_qkv, full_proj, gain_product, bias_local), ('lon', 'lat'))  648 us
    psum x1, waiting for transfers between devices, on_device(): lax.psum((full_qkv, full_proj, gain_product, bias_local), ('lon', 'lat'))  540 us
    dot_general x9, matrix products, contract(): return jnp.einsum(form, left, right, preferred_element_type=jnp.float32)  39.1 us
    scatter-add x1, other arithmetic, on_device(): bias_local = jnp.zeros((HEADS, bias_table.shape[1]), jnp.float32).at[:, r...  30.9 us
  transfers between devices with their start and end apart: 11, of which 3 were waited for; matrix products, arithmetic and copies ran while one was open for 7% of the time, Pallas kernels for 0%

commit v1 on v0

v1 whole, which is shorter than its diff:
```python
import functools

import jax
import jax.numpy as jnp
import numpy as np
from jax import lax
from jax.experimental import pallas as pl
from jax.experimental.pallas import tpu as pltpu
from jax.sharding import PartitionSpec as P

MESH = pl.DeviceIdType.MESH
F32 = jnp.float32
BF16 = jnp.bfloat16
C = 512
HEADS = 8
PAIRS = 4
WIN_LAT = 6
WIN_LON = 12
HALF_LAT = 3
HALF_LON = 6
T = 72
TP = 80
SLOTS = 9
ROWS = SLOTS * TP
RP = 768
REL = 253
X0, D0, M0, FW = 0, 512, 1024, 1152
EPS = 1e-5


def nn(a, b, **kw):
    return lax.dot_general(a, b, (((1,), (0,)), ((), ())), preferred_element_type=F32, **kw)


def nt(a, b, **kw):
    return lax.dot_general(a, b, (((1,), (1,)), ((), ())), preferred_element_type=F32, **kw)


def tn(a, b, **kw):
    return lax.dot_general(a, b, (((0,), (0,)), ((), ())), preferred_element_type=F32, **kw)


def pad_rows(v, rows):
    return jnp.concatenate([v, jnp.zeros((rows - v.shape[0], v.shape[1]), v.dtype)], axis=0)


def kernel(dims, cols, *refs):
    ny, nx, nz = dims
    nlon, nlat = ny * nx, 2 * nz
    nxz = nx * nz
    lat_dev, lon_dev = 18, 48
    wrows, wcols = lat_dev // WIN_LAT, lon_dev // WIN_LON
    nwin = wrows * wcols
    half = C // 2
    ysz = half // ny
    share = ysz // nxz
    nchunk = len(cols)

    it = iter(refs)
    take = lambda n=None: next(it) if n is None else [next(it) for _ in range(n)]
    x_ref, dy_ref, mask_ref, gain_ref, wqkv, wproj, table, perm, selr, self_ = take(10)
    upd, gin, gain_out, bias_out, gqkv, gproj = take(6)
    frame, win, colf, colsend, colrecv, rowsend, rowrecv, cornrecv = take(8)
    idx = take()
    tb, bias2, madd, xhat, invd, normed, gz, gm, packed, mixed, ntp, mtp, probs, dp3, gnacc, bacc = take(16)
    res, of, tmp = take(3)
    ocs, ors, ocr, orr, occ = take(5)
    chunks = [take(7) for _ in range(nchunk)]
    sm, smc, smy, smx = take(4)
    hs, hr, os_, or_, as_, ar, ys, yr, xs, xr, ss, sr = take(12)

    lon = lax.axis_index("lon")
    lat = lax.axis_index("lat")
    y, xh = lon // nx, lon % nx
    z, core = lat // 2, lat % 2

    def dev(a, b):
        return {"lon": a, "lat": b}

    partner = dev(lon, z * 2 + (1 - core))
    ypeer = [dev(((y + d) % ny) * nx + xh, lat) for d in range(1, ny)]
    xzd = [(a, b) for a in range(nx) for b in range(nz) if (a, b) != (0, 0)]
    xzpeer = [dev(y * nx + (xh + a) % nx, ((z + b) % nz) * 2 + core) for a, b in xzd]
    west, east = (lon + nlon - 1) % nlon, (lon + 1) % nlon
    north, south = (lat + nlat - 1) % nlat, (lat + 1) % nlat
    back = [dev(west, lat), dev(lon, north), dev(west, north)]
    forth = [dev(east, lat), dev(lon, south), dev(east, south)]

    barrier = pltpu.get_barrier_semaphore()
    everyone = [partner] + ypeer + xzpeer + back + forth
    for d in everyone:
        pl.semaphore_signal(barrier, inc=1, device_id=d, device_id_type=MESH)

    sends = []

    def send(src, dst, ssem, rsem, d):
        copy = pltpu.make_async_remote_copy(
            src_ref=src, dst_ref=dst, send_sem=ssem, recv_sem=rsem, device_id=d, device_id_type=MESH
        )
        copy.start()
        sends.append(copy)
        return copy

    lane_row = lax.broadcasted_iota(jnp.int32, (lat_dev, lat_dev * 128), 1) // 128
    pick = (lane_row == lax.broadcasted_iota(jnp.int32, (lat_dev, lat_dev * 128), 0)).astype(F32)
    sea = tn(mask_ref[...].astype(F32), pick)
    for r in range(lat_dev):
        frame[r, 0:lon_dev, X0 : X0 + C] = x_ref[r].astype(F32)
        frame[r, 0:lon_dev, D0 : D0 + C] = dy_ref[r].astype(F32)
        frame[r, 0:lon_dev, M0:FW] = sea[:, 128 * r : 128 * r + 128]
    colf[96:112, :] = jnp.zeros((16, FW), F32)
    for r in range(lat_dev):
        colf[6 * r : 6 * r + 6, :] = frame[r, 0:HALF_LON, :]
    colsend[...] = colf[...].astype(BF16)
    for r in range(HALF_LAT):
        rowsend[r] = frame[r, 0:lon_dev, :].astype(BF16)
    pl.semaphore_wait(barrier, len(everyone))
    halo = [
        send(colsend, colrecv, hs.at[0], hr.at[0], back[0]),
        send(rowsend, rowrecv, hs.at[1], hr.at[1], back[1]),
        send(colsend.at[0:32], cornrecv, hs.at[2], hr.at[2], back[2]),
    ]

    tb[...] = jnp.zeros_like(tb)
    tb[:, 0:REL] = table[...]
    hi = lax.Precision.HIGHEST
    for h in range(HEADS):
        line = jnp.broadcast_to(tb[h : h + 1, :], (128, 256))
        rolled = pltpu.roll(pltpu.roll(line, 2, 1), 128, 1, stride=1, stride_axis=0)
        both = nt(nn(selr[...], rolled[:, 0:128], precision=hi), selr[...], precision=hi)
        bias2[h // 2, TP * (h % 2) : TP * (h % 2) + TP, :] = both[0:TP]

    halo[0].wait_recv()
    colf[...] = colrecv[...].astype(F32)
    for r in range(lat_dev):
        frame[r, lon_dev : lon_dev + HALF_LON, :] = colf[6 * r : 6 * r + 6, :]
    halo[2].wait_recv()
    colf[0:32, :] = cornrecv[...].astype(F32)
    for r in range(HALF_LAT):
        frame[lat_dev + r, lon_dev : lon_dev + HALF_LON, :] = colf[6 * r : 6 * r + 6, :]
    halo[1].wait_recv()
    for r in range(HALF_LAT):
        frame[lat_dev + r, 0:lon_dev, :] = rowrecv[r].astype(F32)

    for w in range(nwin):
        wr, wc = w // wcols, w % wcols
        win[w, T:TP, :] = jnp.zeros((TP - T, FW), F32)
        for i in range(WIN_LAT):
            c0 = HALF_LON + WIN_LON * wc
            win[w, WIN_LON * i : WIN_LON * i + WIN_LON, :] = frame[
                HALF_LAT + WIN_LAT * wr + i, c0 : c0 + WIN_LON, :
            ]

    active = [(jnp.max(win[w, :, M0:FW]) > 0.5).astype(jnp.int32) for w in range(nwin)]
    total = functools.reduce(lambda a, b: a + b, active)
    place, seen = [], jnp.int32(0)
    for w in range(nwin):
        place.append(jnp.where(active[w] > 0, seen, total + (w - seen)))
        seen = seen + active[w]
    for k in range(SLOTS):
        slot = jnp.int32(0)
        for w in range(nwin):
            slot = slot + jnp.where(place[w] == k, w, 0)
        idx[k] = slot

    at_end = (lat == nlat - 1).astype(F32)
    gain = gain_ref[...]
    zero_tail = jnp.zeros((RP - ROWS, C), BF16)
    normed[ROWS:RP, :] = zero_tail
    gz[ROWS:RP, :] = zero_tail
    mixed[ROWS:RP, :] = zero_tail
    for p in range(PAIRS):
        dp3[p, ROWS:RP, :] = jnp.zeros((RP - ROWS, 384), BF16)

    def rows_of(k):
        return pl.ds(pl.multiple_of(k * TP, TP), TP)

    def ln_step(k, carry):
        w = idx[k]
        x = win[w, :, X0 : X0 + C]
        mean = jnp.mean(x, axis=1, keepdims=True)
        xc = x - mean
        inv = lax.rsqrt(jnp.mean(xc * xc, axis=1, keepdims=True) + EPS)
        hat = xc * inv
        rows = rows_of(k)
        xhat[rows, :] = hat
        invd[rows, :] = jnp.broadcast_to(inv, (TP, 128))
        normed[rows, :] = (hat * gain).astype(BF16)
        m = win[w, :, M0:FW]
        gz[rows, :] = (win[w, :, D0 : D0 + C] * jnp.concatenate([m] * 4, axis=1)).astype(BF16)
        keys = jnp.transpose(pad_rows(m, 128))[0:TP, :]
        side_a = lax.broadcasted_iota(jnp.int32, (TP, 128), 0) >= T // 2
        side_b = lax.broadcasted_iota(jnp.int32, (TP, 128), 1) >= T // 2
        apart = jnp.where(side_a != side_b, 1.0, 0.0)
        wrap = at_end * jnp.where(w >= nwin - wcols, 1.0, 0.0)
        open_ = keys * (1.0 - apart * wrap)
        madd[k] = (open_ - 1.0) * 1e9
        return carry

    lax.fori_loop(0, SLOTS, ln_step, 0)

    packed[...] = nn(normed[0:ROWS, :], wqkv[...]).astype(BF16)
    gm[...] = nt(gz[0:ROWS, :], wproj[...]).astype(BF16)
    ntp[...] = nt(perm[...], normed[...]).astype(BF16)

    lane = lax.broadcasted_iota(jnp.int32, (TP, 128), 1)
    low = lane < 64
    one_lo = jnp.where(low, 1.0, 0.0).astype(BF16)
    one_hi = jnp.where(low, 0.0, 1.0).astype(BF16)
    q_lo = jnp.where(low, 0.125, 0.0).astype(BF16)
    q_hi = jnp.where(low, 0.0, 0.125).astype(BF16)

    def attend(k, carry):
        rows = rows_of(k)
        add = madd[k]
        add2 = jnp.concatenate([add, add], axis=0)
        scores = []
        for p in range(PAIRS):
            q = packed[rows, 128 * p : 128 * p + 128]
            kk = pad_rows(packed[rows, C + 128 * p : C + 128 * p + 128], 128)
            q2 = jnp.concatenate([q * q_lo, q * q_hi], axis=0)
            scores.append(nt(q2, kk) + bias2[p] + add2)
        weights = []
        for p in range(PAIRS):
            s = scores[p]
            e = jnp.exp(s - jnp.max(s, axis=1, keepdims=True))
            weights.append(e * (1.0 / jnp.sum(e, axis=1, keepdims=True)))
        for p in range(PAIRS):
            probs[k * PAIRS + p] = weights[p]
            v = pad_rows(packed[rows, 2 * C + 128 * p : 2 * C + 128 * p + 128], 128)
            mix = nn(weights[p].astype(BF16), v)
            mixed[rows, 128 * p : 128 * p + 128] = jnp.where(low, mix[0:TP], mix[TP : 2 * TP]).astype(BF16)
        return carry

    lax.fori_loop(0, SLOTS, attend, 0)

    def chunk_start(c, lhs, rhs):
        asend, arecv, own = chunks[c][0:3]
        right = rhs[...]
        other = pl.multiple_of((1 - core) * half, half)
        mine = pl.multiple_of(core * half, half)
        asend[...] = nn(lhs[pl.ds(other, half), :], right).astype(BF16)
        copy = send(asend, arecv, as_.at[c], ar.at[c], partner)
        own[...] = nn(lhs[pl.ds(mine, half), :], right)
        return [copy]

    def chunk_y(c, copies):
        asend, arecv, own, ysend, yrecv = chunks[c][0:5]
        copies[0].wait_recv()
        s = own[...] + arecv[...].astype(F32)
        own[...] = s
        ysend[...] = s.astype(BF16)
        out = []
        for d in range(1, ny):
            start = pl.multiple_of(((y + d) % ny) * ysz, ysz)
            out.append(
                send(ysend.at[pl.ds(start, ysz)], yrecv.at[d - 1], ys.at[c, d - 1], yr.at[c, d - 1], ypeer[d - 1])
            )
        return out

    def chunk_x(c, copies):
        own, ysend, yrecv, xsend, xrecv = chunks[c][2:7]
        s = own[pl.ds(pl.multiple_of(y * ysz, ysz), ysz), :]
        for d in range(1, ny):
            copies[d - 1].wait_recv()
            s = s + yrecv[d - 1].astype(F32)
        for j in range(nxz):
            xsend[j] = s[share * j : share * j + share]
        out = []
        for i, (a, b) in enumerate(xzd):
            j = ((xh + a) % nx) * nz + (z + b) % nz
            out.append(send(xsend.at[j], xrecv.at[i], xs.at[c, i], xr.at[c, i], xzpeer[i]))
        return out

    def chunk_end(c, copies):
        xsend, xrecv = chunks[c][5:7]
        s = xsend[xh * nz + z]
        for i, copy in enumerate(copies):
            copy.wait_recv()
            s = s + xrecv[i]
        if c == 0:
            gproj[...] = s
        else:
            p = c - 1
            for part in range(3):
                gqkv[:, C * part + 128 * p : C * part + 128 * p + 128] = s[:, 128 * part : 128 * part + 128]

    def window_back(o, lane0):
        for w in range(nwin):
            wr, wc = w // wcols, w % wcols
            got = res[jnp.minimum(place[w], SLOTS - 1)]
            tmp[...] = jnp.where(place[w] < SLOTS, got, win[w, :, lane0 : lane0 + C])
            for i in range(WIN_LAT):
                c0 = HALF_LON + WIN_LON * wc
                of[o, HALF_LAT + WIN_LAT * wr + i, c0 : c0 + WIN_LON, :] = tmp[
                    WIN_LON * i : WIN_LON * i + WIN_LON, :
                ]
        colf[0:112, 0:C] = jnp.zeros((112, C), F32)
        for r in range(HALF_LAT, lat_dev):
            colf[6 * r : 6 * r + 6, 0:C] = of[o, r, lon_dev : lon_dev + HALF_LON, :]
        ocs[o, 0:112] = colf[0:112, 0:C].astype(BF16)
        for r in range(HALF_LAT):
            colf[6 * r : 6 * r + 6, 0:C] = of[o, lat_dev + r, lon_dev : lon_dev + HALF_LON, :]
            ors[o, r] = of[o, lat_dev + r, 0:lon_dev, :].astype(BF16)
        ocs[o, 112:144] = colf[0:32, 0:C].astype(BF16)
        return [
            send(ocs.at[o, 0:112], ocr.at[o], os_.at[o, 0], or_.at[o, 0], forth[0]),
            send(ors.at[o], orr.at[o], os_.at[o, 1], or_.at[o, 1], forth[1]),
            send(ocs.at[o, 112:144], occ.at[o], os_.at[o, 2], or_.at[o, 2], forth[2]),
        ]

    def finish(o, copies, out):
        copies[1].wait_recv()
        for r in range(HALF_LAT):
            of[o, r, 0:lon_dev, :] = orr[o, r].astype(F32)
        copies[0].wait_recv()
        colf[0:112, 0:C] = ocr[o].astype(F32)
        for r in range(HALF_LAT, lat_dev):
            of[o, r, 0:HALF_LON, :] = colf[6 * r : 6 * r + 6, 0:C]
        copies[2].wait_recv()
        colf[0:32, 0:C] = occ[o].astype(F32)
        for r in range(HALF_LAT):
            of[o, r, 0:HALF_LON, :] = colf[6 * r : 6 * r + 6, 0:C]
        for r in range(lat_dev):
            out[r] = of[o, r, 0:lon_dev, :].astype(BF16)

    mtp[...] = nt(perm[...], mixed[...]).astype(BF16)
    st = {}
    st[0] = chunk_start(0, mtp, gz)

    gnacc[...] = nn(mixed[0:ROWS, :], wproj[...])

    def updated_step(k, carry):
        w = idx[k]
        m = win[w, :, M0:FW]
        res[k] = win[w, :, X0 : X0 + C] + jnp.concatenate([m] * 4, axis=1) * gnacc[rows_of(k), :]
        return carry

    lax.fori_loop(0, SLOTS, updated_step, 0)
    out_copies = [window_back(0, X0), None]

    def backward(p):
        bacc[p] = jnp.zeros((2 * TP, 128), F32)

        def step(i, carry):
            ks = [3 * i + j for j in range(3)]
            d2s, dps, q2s, kps = [], [], [], []
            for k in ks:
                rows = rows_of(k)
                d = gm[rows, 128 * p : 128 * p + 128]
                d2s.append(jnp.concatenate([d * one_lo, d * one_hi], axis=0))
                q = packed[rows, 128 * p : 128 * p + 128]
                q2s.append(jnp.concatenate([q * q_lo, q * q_hi], axis=0))
                kps.append(pad_rows(packed[rows, C + 128 * p : C + 128 * p + 128], 128))
                v = pad_rows(packed[rows, 2 * C + 128 * p : 2 * C + 128 * p + 128], 128)
                dps.append(nt(d2s[-1], v))
            dss, dvs = [], []
            for j, k in enumerate(ks):
                pr = probs[k * PAIRS + p]
                t = pr * dps[j]
                dss.append(t - pr * jnp.sum(t, axis=1, keepdims=True))
                dvs.append(tn(pr.astype(BF16), d2s[j]))
            bacc[p] += dss[0] + dss[1] + dss[2]
            for j, k in enumerate(ks):
                rows = rows_of(k)
                ds = dss[j].astype(BF16)
                dq2 = nn(ds, kps[j])
                dq = jnp.where(low, dq2[0:TP], dq2[TP : 2 * TP]) * 0.125
                dk = tn(ds, q2s[j])
                dp3[p, rows, 0:128] = dq.astype(BF16)
                dp3[p, rows, 128:256] = dk[0:TP].astype(BF16)
                dp3[p, rows, 256:384] = dvs[j][0:TP].astype(BF16)
            return carry

        lax.fori_loop(0, SLOTS // 3, step, 0)

    def weight_pair(p):
        return jnp.concatenate([wqkv[:, C * part + 128 * p : C * part + 128 * p + 128] for part in range(3)], axis=1)

    def grad_normed(p):
        g = nt(dp3[p, 0:ROWS, :], weight_pair(p))
        gnacc[...] = g if p == 0 else gnacc[...] + g

    for p in range(PAIRS):
        backward(p)
        st[p + 1] = chunk_start(p + 1, ntp, dp3.at[p])
        if p >= 0:
            st[p] = chunk_y(p, st[p])
        if p >= 1:
            st[p - 1] = chunk_x(p - 1, st[p - 1])
        grad_normed(p)

    sm[...] = jnp.zeros_like(sm)
    for h in range(HEADS):
        g = pad_rows(bacc[h // 2, TP * (h % 2) : TP * (h % 2) + TP, :], 128)
        spread = nn(tn(self_[...], g, precision=hi), selr[...], precision=hi)
        wide = jnp.concatenate([spread, jnp.zeros((128, 128), F32)], axis=1)
        sm[h : h + 1, :] = jnp.sum(pltpu.roll(wide, 0, 1, stride=1, stride_axis=0), axis=0, keepdims=True)

    st[4] = chunk_y(4, st[4])
    st[3] = chunk_x(3, st[3])

    def norm_back(k, total):
        w = idx[k]
        rows = rows_of(k)
        gn = gnacc[rows, :]
        hat = xhat[rows, :]
        g = gn * gain
        prod = g * hat
        inner = g - jnp.mean(g, axis=1, keepdims=True) - hat * jnp.mean(prod, axis=1, keepdims=True)
        inv = jnp.concatenate([invd[rows, :]] * 4, axis=1)
        res[k] = win[w, :, D0 : D0 + C] + inv * inner
        return total + jnp.sum(gn * hat, axis=0, keepdims=True)

    gsum = lax.fori_loop(0, SLOTS, norm_back, jnp.zeros((1, C), F32))
    sm[8:9, :] = gsum[:, 0:256]
    sm[9:10, :] = gsum[:, 256:512]
    sma = send(sm, smc, ss.at[0], sr.at[0], partner)
    out_copies[1] = window_back(1, D0)

    st[4] = chunk_x(4, st[4])
    sma.wait_recv()
    smy[y] = sm[...] + smc[...]
    smys = [send(smy.at[y], smy.at[y], ss.at[d], sr.at[d], ypeer[d - 1]) for d in range(1, ny)]
    finish(0, out_copies[0], upd)
    for c in range(nchunk - 1):
        chunk_end(c, st[c])
    for copy in smys:
        copy.wait_recv()
    acc = smy[0]
    for j in range(1, ny):
        acc = acc + smy[j]
    here = xh * nz + z
    smx[here] = acc
    smxs = [send(smx.at[here], smx.at[here], ss.at[ny + i], sr.at[ny + i], xzpeer[i]) for i in range(len(xzd))]
    finish(1, out_copies[1], gin)
    chunk_end(nchunk - 1, st[nchunk - 1])
    for copy in smxs:
        copy.wait_recv()
    acc = smx[0]
    for j in range(1, nxz):
        acc = acc + smx[j]
    bias_out[...] = acc[0:HEADS, 0:REL]
    gain_out[:, 0:256] = acc[8:9, :]
    gain_out[:, 256:512] = acc[9:10, :]
    for copy in sends:
        copy.wait_send()


def constants(ny, nx, nz):
    share = C // (ny * nx * nz * 2)
    perm = np.zeros((C, C), np.float32)
    for core in range(2):
        for y in range(ny):
            for xh in range(nx):
                for z in range(nz):
                    to = (((core * ny + y) * nx + xh) * nz + z) * share
                    start = (((y * nx + xh) * nz + z) * 2 + core) * share
                    perm[to + np.arange(share), start + np.arange(share)] = 1
    a = np.arange(T)
    pa = (a // WIN_LON) * (2 * WIN_LON - 1) + a % WIN_LON
    selr = np.zeros((128, 128), np.float32)
    selr[a, 126 - pa] = 1
    self_ = np.zeros((128, 128), np.float32)
    self_[a, pa] = 1
    return perm, selr, self_


def solution(mesh):
    nlon, nlat = mesh.shape["lon"], mesh.shape["lat"]
    nx, nz = 2, nlat // 2
    ny = nlon // nx
    nxz = nx * nz
    half = C // 2
    ysz = half // ny
    share = ysz // nxz
    cols = [C] + [384] * PAIRS
    lat_dev, lon_dev = 18, 48
    nwin = 12
    vm = pltpu.VMEM
    dma = lambda *s: pltpu.SemaphoreType.DMA(s)
    perm, selr, self_ = constants(ny, nx, nz)

    def on_device(fields, grad_out, layernorm_gain, qkv_weight, proj_weight, bias_table, sea_mask):
        scratch = [
            vm((lat_dev + 3, 56, FW), F32),
            vm((nwin, TP, FW), F32),
            vm((112, FW), F32),
            vm((112, FW), BF16),
            vm((112, FW), BF16),
            vm((3, lon_dev, FW), BF16),
            vm((3, lon_dev, FW), BF16),
            vm((32, FW), BF16),
            pltpu.SMEM((16,), jnp.int32),
            vm((HEADS, 256), F32),
            vm((PAIRS, 2 * TP, 128), F32),
            vm((SLOTS, TP, 128), F32),
            vm((ROWS, C), F32),
            vm((ROWS, 128), F32),
            vm((RP, C), BF16),
            vm((RP, C), BF16),
            vm((ROWS, C), BF16),
            vm((ROWS, 3 * C), BF16),
            vm((RP, C), BF16),
            vm((C, RP), BF16),
            vm((C, RP), BF16),
            vm((SLOTS * PAIRS, 2 * TP, 128), F32),
            vm((PAIRS, RP, 384), BF16),
            vm((ROWS, C), F32),
            vm((PAIRS, 2 * TP, 128), F32),
            vm((SLOTS, TP, C), F32),
            vm((2, lat_dev + 3, 56, C), F32),
            vm((TP, C), F32),
            vm((2, 144, C), BF16),
            vm((2, 3, lon_dev, C), BF16),
            vm((2, 112, C), BF16),
            vm((2, 3, lon_dev, C), BF16),
            vm((2, 32, C), BF16),
        ]
        for n in cols:
            scratch += [
                vm((half, n), BF16),
                vm((half, n), BF16),
                vm((half, n), F32),
                vm((half, n), BF16),
                vm((ny - 1, ysz, n), BF16),
                vm((nxz, share, n), F32),
                vm((nxz - 1, share, n), F32),
            ]
        scratch += [vm((16, 256), F32), vm((16, 256), F32), vm((ny, 16, 256), F32), vm((nxz, 16, 256), F32)]
        nc = len(cols)
        small = ny + nxz - 1
        scratch += [
            dma(3), dma(3), dma(2, 3), dma(2, 3), dma(nc), dma(nc), dma(nc, ny - 1), dma(nc, ny - 1),
            dma(nc, nxz - 1), dma(nc, nxz - 1), dma(small), dma(small),
        ]
        whole = pl.BlockSpec(memory_space=vm)
        outs = pl.pallas_call(
            functools.partial(kernel, (ny, nx, nz), cols),
            out_shape=(
                jax.ShapeDtypeStruct((lat_dev, lon_dev, C), BF16),
                jax.ShapeDtypeStruct((lat_dev, lon_dev, C), BF16),
                jax.ShapeDtypeStruct((1, C), F32),
                jax.ShapeDtypeStruct((HEADS, REL), F32),
                jax.ShapeDtypeStruct((share, 3 * C), F32),
                jax.ShapeDtypeStruct((share, C), F32),
            ),
            in_specs=[whole] * 10,
            out_specs=(whole,) * 6,
            scratch_shapes=scratch,
            compiler_params=pltpu.CompilerParams(
                collective_id=0, has_side_effects=True, vmem_limit_bytes=60 * 1024 * 1024
            ),
        )(
            fields, grad_out, sea_mask, layernorm_gain.reshape(1, C), qkv_weight, proj_weight, bias_table,
            jnp.asarray(perm, BF16), jnp.asarray(selr, F32), jnp.asarray(self_, F32),
        )
        updated, grad_in, grad_gain, grad_bias, grad_qkv, grad_proj = outs
        return (updated, grad_in, grad_gain.reshape(C), grad_bias, grad_qkv, grad_proj)

    grid = P(("batch", "lat"), "lon", None)
    return jax.shard_map(
        on_device,
        mesh=mesh,
        in_specs=(grid, grid, P(), P(), P(), P(), P(("batch", "lat"), "lon")),
        out_specs=(
            grid,
            grid,
            P("batch"),
            P("batch", None),
            P(("batch", "lon", "lat"), None),
            P(("batch", "lon", "lat"), None),
        ),
        check_vma=False,
    )
```

time: 1480 us -> 82.7 us (0.06)
  the two profiles are of different devices: /device:TPU:2 before, /device:TPU:4 now
where the time goes in v1:
time: 82.7 us; the launch traced here: 82.6 us
  Pallas kernels  76.4 us (92%)
  local copies, waits for them, and re-layouts  5.53 us (7%)
    pallas_call x1, Pallas kernels, on_device(): pl.pallas_call(functools.partial(kernel, (ny, nx, nz), cols), out_shape=(...  76.4 us
    unnamed x16, local copies, waits for them, and re-layouts  5.53 us

profile of v1, /device:TPU:4, one launch (start us, length us, event | category | flops | bytes accessed | tf_op | source)
XLA Modules:
  0.0 82.6 jit_solution(9863489224001622064)
XLA Ops:
  0.6 76.4 %shard_map.145 = (bf16[18,48,512]{2,1,0:T(8,128)(2,1)}, bf16[18,48,512]{2,1,0:T(8,128)(2,1)}, f32[1,512]{1,0:T(1,128)}, f32[8,253]{1,0:T(8,128)}, f32[4,1536]{1,0:T(4,128)}, /*index=5*/f32[4,512]{1,0:T(4,128)}) custom-call(bf16[18,48,512]{2,1,0:T(8,128)(2,1)} %refs_0_.1, bf16[18,48,512]{2,1,0:T(8,128)(2,1)} %refs_1_.1, s32[18,48]{1,0:T(8,128)} %refs_2_.1, ...), custom_call_target="tpu_custom_call" | custom-call | tf_op jit(solution)/shard_map/pallas_call | solution.py:538
  77.0 0.0 copy-start
  77.0 0.0 copy-start.4
  77.0 0.0 copy-start.3
  77.0 0.0 copy-start.1
  77.0 0.0 copy-start.2
  77.1 2.2 %copy.22 = bf16[18,48,512]{2,1,0:T(8,128)(2,1)} copy(bf16[18,48,512]{2,1,0:T(8,128)(2,1)} %get-tuple-element.24) | data formatting | bytes 1769472
  79.3 0.0 copy-done
  79.3 0.9 %copy.23 = bf16[18,48,512]{2,1,0:T(8,128)(2,1)} copy(bf16[18,48,512]{2,1,0:T(8,128)(2,1)S(1)} %copy-done) | data formatting | bytes 1769472
  80.2 0.0 copy-done.4
  80.2 0.6 copy.24
  80.8 0.0 copy-done.3
  80.8 0.6 copy.25
  81.4 0.0 copy-done.1
  81.4 0.6 copy.26
  82.0 0.0 copy-done.2
  82.0 0.6 copy.27
Async XLA Ops:
  77.0 2.3 %copy-start = (bf16[18,48,512]{2,1,0:T(8,128)(2,1)S(1)}, bf16[18,48,512]{2,1,0:T(8,128)(2,1)}, u32[]{:S(2)}) copy-start(bf16[18,48,512]{2,1,0:T(8,128)(2,1)} %get-tuple-element.25) | copy-start | bytes 2654212
  77.0 3.2 %copy-start.4 = (f32[1,512]{1,0:T(1,128)S(1)}, f32[1,512]{1,0:T(1,128)}, u32[]{:S(2)}) copy-start(f32[1,512]{1,0:T(1,128)} %get-tuple-element.14) | copy-start | bytes 6148
  77.0 3.7 %copy-start.3 = (f32[8,253]{1,0:T(8,128)S(1)}, f32[8,253]{1,0:T(8,128)}, u32[]{:S(2)}) copy-start(f32[8,253]{1,0:T(8,128)} %get-tuple-element.27) | copy-start | bytes 24292
  77.0 4.3 %copy-start.1 = (f32[4,1536]{1,0:T(4,128)S(1)}, f32[4,1536]{1,0:T(4,128)}, u32[]{:S(2)}) copy-start(f32[4,1536]{1,0:T(4,128)} %get-tuple-element.28) | copy-start | bytes 73732
  77.0 4.9 %copy-start.2 = (f32[4,512]{1,0:T(4,128)S(1)}, f32[4,512]{1,0:T(4,128)}, u32[]{:S(2)}) copy-start(f32[4,512]{1,0:T(4,128)} %get-tuple-element.29) | copy-start | bytes 24580

commit v2 on v1

--- a/solution.py
+++ b/solution.py
@@ -24,7 +24,9 @@
 ROWS = SLOTS * TP
 RP = 768
 REL = 253
-X0, D0, M0, FW = 0, 512, 1024, 1152
+X0, M0, D0, FW = 0, 512, 640, 1152
+XW, DW = 640, 512
+EARLY = 3
 EPS = 1e-5
 
 
@@ -60,13 +62,14 @@
     take = lambda n=None: next(it) if n is None else [next(it) for _ in range(n)]
     x_ref, dy_ref, mask_ref, gain_ref, wqkv, wproj, table, perm, selr, self_ = take(10)
     upd, gin, gain_out, bias_out, gqkv, gproj = take(6)
-    frame, win, colf, colsend, colrecv, rowsend, rowrecv, cornrecv = take(8)
+    frame, win, colf = take(3)
+    halos = [take(5) for _ in range(2)]
     idx = take()
     tb, bias2, madd, xhat, invd, normed, gz, gm, packed, mixed, ntp, mtp, probs, dp3, gnacc, bacc = take(16)
-    res, of, tmp = take(3)
+    res, of = take(2)
     ocs, ors, ocr, orr, occ = take(5)
     chunks = [take(7) for _ in range(nchunk)]
-    sm, smc, smy, smx = take(4)
+    sums = [take(4) for _ in range(2)]
     hs, hr, os_, or_, as_, ar, ys, yr, xs, xr, ss, sr = take(12)
 
     lon = lax.axis_index("lon")
@@ -104,22 +107,49 @@
     lane_row = lax.broadcasted_iota(jnp.int32, (lat_dev, lat_dev * 128), 1) // 128
     pick = (lane_row == lax.broadcasted_iota(jnp.int32, (lat_dev, lat_dev * 128), 0)).astype(F32)
     sea = tn(mask_ref[...].astype(F32), pick)
+    colf[96:112, :] = jnp.zeros((16, FW), F32)
+
+    def halo_pack(h, lanes):
+        colsend, colrecv, rowsend, rowrecv, cornrecv = halos[h]
+        for r in range(lat_dev):
+            colf[6 * r : 6 * r + 6, lanes] = frame[r, 0:HALF_LON, lanes]
+        colsend[...] = colf[:, lanes].astype(BF16)
+        for r in range(HALF_LAT):
+            rowsend[r] = frame[r, 0:lon_dev, lanes].astype(BF16)
+
+    def halo_send(h):
+        colsend, colrecv, rowsend, rowrecv, cornrecv = halos[h]
+        return [
+            send(colsend, colrecv, hs.at[h, 0], hr.at[h, 0], back[0]),
+            send(rowsend, rowrecv, hs.at[h, 1], hr.at[h, 1], back[1]),
+            send(colsend.at[0:32], cornrecv, hs.at[h, 2], hr.at[h, 2], back[2]),
+        ]
+
+    def halo_land(h, lanes, copies):
+        colsend, colrecv, rowsend, rowrecv, cornrecv = halos[h]
+        copies[1].wait_recv()
+        for r in range(HALF_LAT):
+            frame[lat_dev + r, 0:lon_dev, lanes] = rowrecv[r].astype(F32)
+        copies[2].wait_recv()
+        colf[0:32, lanes] = cornrecv[...].astype(F32)
+        for r in range(HALF_LAT):
+            frame[lat_dev + r, lon_dev : lon_dev + HALF_LON, lanes] = colf[6 * r : 6 * r + 6, lanes]
+        copies[0].wait_recv()
+        colf[:, lanes] = colrecv[...].astype(F32)
+        for r in range(lat_dev):
+            frame[r, lon_dev : lon_dev + HALF_LON, lanes] = colf[6 * r : 6 * r + 6, lanes]
+
+    xlanes, dlanes = slice(X0, X0 + XW), slice(D0, D0 + DW)
     for r in range(lat_dev):
         frame[r, 0:lon_dev, X0 : X0 + C] = x_ref[r].astype(F32)
+        frame[r, 0:lon_dev, M0 : M0 + 128] = sea[:, 128 * r : 128 * r + 128]
+    halo_pack(0, xlanes)
+    pl.semaphore_wait(barrier, len(everyone))
+    xcopies = halo_send(0)
+    for r in range(lat_dev):
         frame[r, 0:lon_dev, D0 : D0 + C] = dy_ref[r].astype(F32)
-        frame[r, 0:lon_dev, M0:FW] = sea[:, 128 * r : 128 * r + 128]
-    colf[96:112, :] = jnp.zeros((16, FW), F32)
-    for r in range(lat_dev):
-        colf[6 * r : 6 * r + 6, :] = frame[r, 0:HALF_LON, :]
-    colsend[...] = colf[...].astype(BF16)
-    for r in range(HALF_LAT):
-        rowsend[r] = frame[r, 0:lon_dev, :].astype(BF16)
-    pl.semaphore_wait(barrier, len(everyone))
-    halo = [
-        send(colsend, colrecv, hs.at[0], hr.at[0], back[0]),
-        send(rowsend, rowrecv, hs.at[1], hr.at[1], back[1]),
-        send(colsend.at[0:32], cornrecv, hs.at[2], hr.at[2], back[2]),
-    ]
+    halo_pack(1, dlanes)
+    dcopies = halo_send(1)
 
     tb[...] = jnp.zeros_like(tb)
     tb[:, 0:REL] = table[...]
@@ -127,50 +157,53 @@
     for h in range(HEADS):
         line = jnp.broadcast_to(tb[h : h + 1, :], (128, 256))
         rolled = pltpu.roll(pltpu.roll(line, 2, 1), 128, 1, stride=1, stride_axis=0)
-        both = nt(nn(selr[...], rolled[:, 0:128], precision=hi), selr[...], precision=hi)
+        both = nt(nt(selr[...], rolled[:, 0:128], precision=hi), selr[...], precision=hi)
         bias2[h // 2, TP * (h % 2) : TP * (h % 2) + TP, :] = both[0:TP]
 
-    halo[0].wait_recv()
-    colf[...] = colrecv[...].astype(F32)
-    for r in range(lat_dev):
-        frame[r, lon_dev : lon_dev + HALF_LON, :] = colf[6 * r : 6 * r + 6, :]
-    halo[2].wait_recv()
-    colf[0:32, :] = cornrecv[...].astype(F32)
-    for r in range(HALF_LAT):
-        frame[lat_dev + r, lon_dev : lon_dev + HALF_LON, :] = colf[6 * r : 6 * r + 6, :]
-    halo[1].wait_recv()
-    for r in range(HALF_LAT):
-        frame[lat_dev + r, 0:lon_dev, :] = rowrecv[r].astype(F32)
-
-    for w in range(nwin):
-        wr, wc = w // wcols, w % wcols
-        win[w, T:TP, :] = jnp.zeros((TP - T, FW), F32)
-        for i in range(WIN_LAT):
-            c0 = HALF_LON + WIN_LON * wc
-            win[w, WIN_LON * i : WIN_LON * i + WIN_LON, :] = frame[
-                HALF_LAT + WIN_LAT * wr + i, c0 : c0 + WIN_LON, :
-            ]
-
-    active = [(jnp.max(win[w, :, M0:FW]) > 0.5).astype(jnp.int32) for w in range(nwin)]
-    total = functools.reduce(lambda a, b: a + b, active)
-    place, seen = [], jnp.int32(0)
-    for w in range(nwin):
-        place.append(jnp.where(active[w] > 0, seen, total + (w - seen)))
-        seen = seen + active[w]
-    for k in range(SLOTS):
-        slot = jnp.int32(0)
-        for w in range(nwin):
-            slot = slot + jnp.where(place[w] == k, w, 0)
-        idx[k] = slot
-
-    at_end = (lat == nlat - 1).astype(F32)
-    gain = gain_ref[...]
     zero_tail = jnp.zeros((RP - ROWS, C), BF16)
     normed[ROWS:RP, :] = zero_tail
     gz[ROWS:RP, :] = zero_tail
     mixed[ROWS:RP, :] = zero_tail
     for p in range(PAIRS):
         dp3[p, ROWS:RP, :] = jnp.zeros((RP - ROWS, 384), BF16)
+    for w in range(nwin):
+        win[w, T:TP, :] = jnp.zeros((TP - T, FW), F32)
+
+    def cut(w, lanes):
+        wr, wc = w // wcols, w % wcols
+        c0 = HALF_LON + WIN_LON * wc
+        for i in range(WIN_LAT):
+            win[w, WIN_LON * i : WIN_LON * i + WIN_LON, lanes] = frame[
+                HALF_LAT + WIN_LAT * wr + i, c0 : c0 + WIN_LON, lanes
+            ]
+
+    def holds_sea(w):
+        return (jnp.max(win[w, :, M0 : M0 + 128]) > 0.5).astype(jnp.int32)
+
+    def ranks(flags, counted):
+        total = jnp.int32(0)
+        for f, c in zip(flags, counted):
+            total = total + f * c
+        out, on, off = [], jnp.int32(0), total
+        for f, c in zip(flags, counted):
+            out.append(jnp.where(f > 0, on, off))
+            on = on + f * c
+            off = off + (1 - f) * c
+        return out
+
+    def slot_window(k, places):
+        slot = jnp.int32(0)
+        for w, at in places:
+            slot = slot + jnp.where(at == k, w, 0)
+        idx[k] = slot
+
+    inner = [w for w in range(nwin) if w // wcols < wrows - 1 and w % wcols < wcols - 1]
+    outer = [w for w in range(nwin) if w not in inner]
+    active = [None] * nwin
+    place = [None] * nwin
+
+    at_end = (lat == nlat - 1).astype(F32)
+    gain = gain_ref[...]
 
     def rows_of(k):
         return pl.ds(pl.multiple_of(k * TP, TP), TP)
@@ -186,22 +219,19 @@
         xhat[rows, :] = hat
         invd[rows, :] = jnp.broadcast_to(inv, (TP, 128))
         normed[rows, :] = (hat * gain).astype(BF16)
-        m = win[w, :, M0:FW]
-        gz[rows, :] = (win[w, :, D0 : D0 + C] * jnp.concatenate([m] * 4, axis=1)).astype(BF16)
-        keys = jnp.transpose(pad_rows(m, 128))[0:TP, :]
-        side_a = lax.broadcasted_iota(jnp.int32, (TP, 128), 0) >= T // 2
-        side_b = lax.broadcasted_iota(jnp.int32, (TP, 128), 1) >= T // 2
+        keys = win[w, :, M0 : M0 + 128]
+        side_b = lax.broadcasted_iota(jnp.int32, (TP, 128), 0) >= T // 2
+        side_a = lax.broadcasted_iota(jnp.int32, (TP, 128), 1) >= T // 2
         apart = jnp.where(side_a != side_b, 1.0, 0.0)
         wrap = at_end * jnp.where(w >= nwin - wcols, 1.0, 0.0)
-        open_ = keys * (1.0 - apart * wrap)
-        madd[k] = (open_ - 1.0) * 1e9
+        madd[k] = (keys * (1.0 - apart * wrap) - 1.0) * 1e9
         return carry
 
-    lax.fori_loop(0, SLOTS, ln_step, 0)
-
-    packed[...] = nn(normed[0:ROWS, :], wqkv[...]).astype(BF16)
-    gm[...] = nt(gz[0:ROWS, :], wproj[...]).astype(BF16)
-    ntp[...] = nt(perm[...], normed[...]).astype(BF16)
+    def dy_step(k, carry):
+        w = idx[k]
+        m = win[w, :, M0 : M0 + 128]
+        gz[rows_of(k), :] = (win[w, :, D0 : D0 + C] * jnp.concatenate([m] * 4, axis=1)).astype(BF16)
+        return carry
 
     lane = lax.broadcasted_iota(jnp.int32, (TP, 128), 1)
     low = lane < 64
@@ -210,29 +240,69 @@
     q_lo = jnp.where(low, 0.125, 0.0).astype(BF16)
     q_hi = jnp.where(low, 0.0, 0.125).astype(BF16)
 
+    def both_heads(v, lo, hi_):
+        return jnp.concatenate([v * lo, v * hi_], axis=0)
+
+    def join_heads(v):
+        return jnp.where(low, v[0:TP], v[TP : 2 * TP])
+
+    def per_head(v):
+        return v.reshape(2, TP, 128)
+
     def attend(k, carry):
         rows = rows_of(k)
         add = madd[k]
         add2 = jnp.concatenate([add, add], axis=0)
         scores = []
         for p in range(PAIRS):
-            q = packed[rows, 128 * p : 128 * p + 128]
-            kk = pad_rows(packed[rows, C + 128 * p : C + 128 * p + 128], 128)
-            q2 = jnp.concatenate([q * q_lo, q * q_hi], axis=0)
-            scores.append(nt(q2, kk) + bias2[p] + add2)
-        weights = []
+            q = pad_rows(packed[rows, 128 * p : 128 * p + 128], 128)
+            k2 = both_heads(packed[rows, C + 128 * p : C + 128 * p + 128], q_lo, q_hi)
+            scores.append(nt(k2, q) + bias2[p] + add2)
         for p in range(PAIRS):
-            s = scores[p]
+            s = per_head(scores[p])
             e = jnp.exp(s - jnp.max(s, axis=1, keepdims=True))
-            weights.append(e * (1.0 / jnp.sum(e, axis=1, keepdims=True)))
-        for p in range(PAIRS):
-            probs[k * PAIRS + p] = weights[p]
-            v = pad_rows(packed[rows, 2 * C + 128 * p : 2 * C + 128 * p + 128], 128)
-            mix = nn(weights[p].astype(BF16), v)
-            mixed[rows, 128 * p : 128 * p + 128] = jnp.where(low, mix[0:TP], mix[TP : 2 * TP]).astype(BF16)
+            pr = (e * (1.0 / jnp.sum(e, axis=1, keepdims=True))).reshape(2 * TP, 128)
+            probs[k * PAIRS + p] = pr
+            v2 = both_heads(packed[rows, 2 * C + 128 * p : 2 * C + 128 * p + 128], one_lo, one_hi)
+            mixed[rows, 128 * p : 128 * p + 128] = tn(pr.astype(BF16), v2)[0:TP].astype(BF16)
         return carry
 
-    lax.fori_loop(0, SLOTS, attend, 0)
+    def forward(first, last):
+        lax.fori_loop(first, last, ln_step, 0)
+        rows = slice(first * TP, last * TP)
+        packed[rows, :] = nn(normed[rows, :], wqkv[...]).astype(BF16)
+        lax.fori_loop(first, last, attend, 0)
+
+    for w in inner:
+        cut(w, slice(0, FW))
+        active[w] = holds_sea(w)
+    inner_rank = ranks([active[w] for w in inner], [1] * len(inner))
+    for k in range(EARLY):
+        slot_window(k, list(zip(inner, inner_rank)))
+    forward(0, EARLY)
+
+    halo_land(0, xlanes, xcopies)
+    for w in outer:
+        cut(w, xlanes)
+        active[w] = holds_sea(w)
+    rest = [jnp.int32(1)] * nwin
+    for w, at in zip(inner, inner_rank):
+        rest[w] = (at >= EARLY).astype(jnp.int32)
+    late_rank = ranks(active, rest)
+    for w in range(nwin):
+        place[w] = late_rank[w] + EARLY
+    for w, at in zip(inner, inner_rank):
+        place[w] = jnp.where(at < EARLY, at, place[w])
+    for k in range(EARLY, SLOTS):
+        slot_window(k, list(enumerate(place)))
+    forward(EARLY, SLOTS)
+
+    halo_land(1, dlanes, dcopies)
+    for w in outer:
+        cut(w, dlanes)
+    lax.fori_loop(0, SLOTS, dy_step, 0)
+    gm[...] = nt(gz[0:ROWS, :], wproj[...]).astype(BF16)
+    ntp[...] = nt(perm[...], normed[...]).astype(BF16)
 
     def chunk_start(c, lhs, rhs):
         asend, arecv, own = chunks[c][0:3]
@@ -288,13 +358,13 @@
     def window_back(o, lane0):
         for w in range(nwin):
             wr, wc = w // wcols, w % wcols
-            got = res[jnp.minimum(place[w], SLOTS - 1)]
-            tmp[...] = jnp.where(place[w] < SLOTS, got, win[w, :, lane0 : lane0 + C])
+            slot = jnp.minimum(place[w], SLOTS - 1)
             for i in range(WIN_LAT):
                 c0 = HALF_LON + WIN_LON * wc
-                of[o, HALF_LAT + WIN_LAT * wr + i, c0 : c0 + WIN_LON, :] = tmp[
-                    WIN_LON * i : WIN_LON * i + WIN_LON, :
-                ]
+                at = slice(WIN_LON * i, WIN_LON * i + WIN_LON)
+                of[o, HALF_LAT + WIN_LAT * wr + i, c0 : c0 + WIN_LON, :] = jnp.where(
+                    place[w] < SLOTS, res[slot, at, :], win[w, at, lane0 : lane0 + C]
+                )
         colf[0:112, 0:C] = jnp.zeros((112, C), F32)
         for r in range(HALF_LAT, lat_dev):
             colf[6 * r : 6 * r + 6, 0:C] = of[o, r, lon_dev : lon_dev + HALF_LON, :]
@@ -332,7 +402,7 @@
 
     def updated_step(k, carry):
         w = idx[k]
-        m = win[w, :, M0:FW]
+        m = win[w, :, M0 : M0 + 128]
         res[k] = win[w, :, X0 : X0 + C] + jnp.concatenate([m] * 4, axis=1) * gnacc[rows_of(k), :]
         return carry
 
@@ -344,32 +414,30 @@
 
         def step(i, carry):
             ks = [3 * i + j for j in range(3)]
-            d2s, dps, q2s, kps = [], [], [], []
+            ds_, dps = [], []
             for k in ks:
                 rows = rows_of(k)
-                d = gm[rows, 128 * p : 128 * p + 128]
-                d2s.append(jnp.concatenate([d * one_lo, d * one_hi], axis=0))
-                q = packed[rows, 128 * p : 128 * p + 128]
-                q2s.append(jnp.concatenate([q * q_lo, q * q_hi], axis=0))
-                kps.append(pad_rows(packed[rows, C + 128 * p : C + 128 * p + 128], 128))
-                v = pad_rows(packed[rows, 2 * C + 128 * p : 2 * C + 128 * p + 128], 128)
-                dps.append(nt(d2s[-1], v))
+                ds_.append(pad_rows(gm[rows, 128 * p : 128 * p + 128], 128))
+                v2 = both_heads(packed[rows, 2 * C + 128 * p : 2 * C + 128 * p + 128], one_lo, one_hi)
+                dps.append(nt(v2, ds_[-1]))
             dss, dvs = [], []
             for j, k in enumerate(ks):
                 pr = probs[k * PAIRS + p]
                 t = pr * dps[j]
-                dss.append(t - pr * jnp.sum(t, axis=1, keepdims=True))
-                dvs.append(tn(pr.astype(BF16), d2s[j]))
+                dot = jnp.sum(per_head(t), axis=1, keepdims=True)
+                dss.append((per_head(t) - per_head(pr) * dot).reshape(2 * TP, 128))
+                dvs.append(nn(pr.astype(BF16), ds_[j]))
             bacc[p] += dss[0] + dss[1] + dss[2]
             for j, k in enumerate(ks):
                 rows = rows_of(k)
                 ds = dss[j].astype(BF16)
-                dq2 = nn(ds, kps[j])
-                dq = jnp.where(low, dq2[0:TP], dq2[TP : 2 * TP]) * 0.125
-                dk = tn(ds, q2s[j])
-                dp3[p, rows, 0:128] = dq.astype(BF16)
-                dp3[p, rows, 128:256] = dk[0:TP].astype(BF16)
-                dp3[p, rows, 256:384] = dvs[j][0:TP].astype(BF16)
+                q = pad_rows(packed[rows, 128 * p : 128 * p + 128], 128)
+                k2 = both_heads(packed[rows, C + 128 * p : C + 128 * p + 128], q_lo, q_hi)
+                dk2 = nn(ds, q)
+                dq = tn(ds, k2)
+                dp3[p, rows, 0:128] = dq[0:TP].astype(BF16)
+                dp3[p, rows, 128:256] = (join_heads(dk2) * 0.125).astype(BF16)
+                dp3[p, rows, 256:384] = join_heads(dvs[j]).astype(BF16)
             return carry
 
         lax.fori_loop(0, SLOTS // 3, step, 0)
@@ -390,15 +458,47 @@
             st[p - 1] = chunk_x(p - 1, st[p - 1])
         grad_normed(p)
 
-    sm[...] = jnp.zeros_like(sm)
+    def sum_core(g):
+        sm, smc = sums[g][0:2]
+        return send(sm, smc, ss.at[g, 0], sr.at[g, 0], partner)
+
+    def sum_y(g, copy):
+        sm, smc, smy, smx = sums[g]
+        copy.wait_recv()
+        smy[y] = sm[...] + smc[...]
+        return [
+            send(smy.at[y], smy.at[y], ss.at[g, d], sr.at[g, d], ypeer[d - 1]) for d in range(1, ny)
+        ]
+
+    def sum_xz(g, copies):
+        sm, smc, smy, smx = sums[g]
+        for copy in copies:
+            copy.wait_recv()
+        acc = smy[0]
+        for j in range(1, ny):
+            acc = acc + smy[j]
+        here = xh * nz + z
+        smx[here] = acc
+        return [
+            send(smx.at[here], smx.at[here], ss.at[g, ny + i], sr.at[g, ny + i], xzpeer[i])
+            for i in range(len(xzd))
+        ]
+
+    def sum_end(g, copies):
+        smx = sums[g][3]
+        for copy in copies:
+            copy.wait_recv()
+        acc = smx[0]
+        for j in range(1, nxz):
+            acc = acc + smx[j]
+        return acc
+
     for h in range(HEADS):
         g = pad_rows(bacc[h // 2, TP * (h % 2) : TP * (h % 2) + TP, :], 128)
-        spread = nn(tn(self_[...], g, precision=hi), selr[...], precision=hi)
+        spread = tn(self_[...], tn(g, selr[...], precision=hi), precision=hi)
         wide = jnp.concatenate([spread, jnp.zeros((128, 128), F32)], axis=1)
-        sm[h : h + 1, :] = jnp.sum(pltpu.roll(wide, 0, 1, stride=1, stride_axis=0), axis=0, keepdims=True)
-
-    st[4] = chunk_y(4, st[4])
-    st[3] = chunk_x(3, st[3])
+        sums[0][0][h : h + 1, :] = jnp.sum(pltpu.roll(wide, 0, 1, stride=1, stride_axis=0), axis=0, keepdims=True)
+    bias_copies = sum_core(0)
 
     def norm_back(k, total):
         w = idx[k]
@@ -407,44 +507,45 @@
         hat = xhat[rows, :]
         g = gn * gain
         prod = g * hat
-        inner = g - jnp.mean(g, axis=1, keepdims=True) - hat * jnp.mean(prod, axis=1, keepdims=True)
+        mid = g - jnp.mean(g, axis=1, keepdims=True) - hat * jnp.mean(prod, axis=1, keepdims=True)
         inv = jnp.concatenate([invd[rows, :]] * 4, axis=1)
-        res[k] = win[w, :, D0 : D0 + C] + inv * inner
+        res[k] = win[w, :, D0 : D0 + C] + inv * mid
         return total + jnp.sum(gn * hat, axis=0, keepdims=True)
 
     gsum = lax.fori_loop(0, SLOTS, norm_back, jnp.zeros((1, C), F32))
-    sm[8:9, :] = gsum[:, 0:256]
-    sm[9:10, :] = gsum[:, 256:512]
-    sma = send(sm, smc, ss.at[0], sr.at[0], partner)
+    sums[1][0][...] = jnp.zeros((8, 128), F32)
+    for j in range(4):
+        sums[1][0][j : j + 1, :] = gsum[:, 128 * j : 128 * j + 128]
+    gain_copies = sum_core(1)
+    st[4] = chunk_y(4, st[4])
     out_copies[1] = window_back(1, D0)
 
+    st[3] = chunk_x(3, st[3])
+    bias_copies = sum_y(0, bias_copies)
+    gain_copies = sum_y(1, gain_copies)
     st[4] = chunk_x(4, st[4])
-    sma.wait_recv()
-    smy[y] = sm[...] + smc[...]
-    smys = [send(smy.at[y], smy.at[y], ss.at[d], sr.at[d], ypeer[d - 1]) for d in range(1, ny)]
+    bias_copies = sum_xz(0, bias_copies)
+    gain_copies = sum_xz(1, gain_copies)
     finish(0, out_copies[0], upd)
     for c in range(nchunk - 1):
         chunk_end(c, st[c])
-    for copy in smys:
-        copy.wait_recv()
-    acc = smy[0]
-    for j in range(1, ny):
-        acc = acc + smy[j]
-    here = xh * nz + z
-    smx[here] = acc
-    smxs = [send(smx.at[here], smx.at[here], ss.at[ny + i], sr.at[ny + i], xzpeer[i]) for i in range(len(xzd))]
     finish(1, out_copies[1], gin)
+    bias_out[...] = sum_end(0, bias_copies)[:, 0:REL]
     chunk_end(nchunk - 1, st[nchunk - 1])
-    for copy in smxs:
-        copy.wait_recv()
-    acc = smx[0]
-    for j in range(1, nxz):
-        acc = acc + smx[j]
-    bias_out[...] = acc[0:HEADS, 0:REL]
-    gain_out[:, 0:256] = acc[8:9, :]
-    gain_out[:, 256:512] = acc[9:10, :]
+    acc = sum_end(1, gain_copies)
+    for j in range(4):
+        gain_out[:, 128 * j : 128 * j + 128] = acc[j : j + 1, :]
     for copy in sends:
         copy.wait_send()
+
+
+def hand_over(*refs):
+    sem = refs[12]
+    copies = [pltpu.make_async_copy(refs[i], refs[6 + i], sem.at[i]) for i in range(6)]
+    for copy in copies:
+        copy.start()
+    for copy in copies:
+        copy.wait()
 
 
 def constants(ny, nx, nz):
@@ -486,11 +587,16 @@
             vm((lat_dev + 3, 56, FW), F32),
             vm((nwin, TP, FW), F32),
             vm((112, FW), F32),
-            vm((112, FW), BF16),
-            vm((112, FW), BF16),
-            vm((3, lon_dev, FW), BF16),
-            vm((3, lon_dev, FW), BF16),
-            vm((32, FW), BF16),
+        ]
+        for wide in (XW, DW):
+            scratch += [
+                vm((112, wide), BF16),
+                vm((112, wide), BF16),
+                vm((3, lon_dev, wide), BF16),
+                vm((3, lon_dev, wide), BF16),
+                vm((32, wide), BF16),
+            ]
+        scratch += [
             pltpu.SMEM((16,), jnp.int32),
             vm((HEADS, 256), F32),
             vm((PAIRS, 2 * TP, 128), F32),
@@ -510,7 +616,6 @@
             vm((PAIRS, 2 * TP, 128), F32),
             vm((SLOTS, TP, C), F32),
             vm((2, lat_dev + 3, 56, C), F32),
-            vm((TP, C), F32),
             vm((2, 144, C), BF16),
             vm((2, 3, lon_dev, C), BF16),
             vm((2, 112, C), BF16),
@@ -527,24 +632,26 @@
                 vm((nxz, share, n), F32),
                 vm((nxz - 1, share, n), F32),
             ]
-        scratch += [vm((16, 256), F32), vm((16, 256), F32), vm((ny, 16, 256), F32), vm((nxz, 16, 256), F32)]
+        for sm in ((8, 256), (8, 128)):
+            scratch += [vm(sm, F32), vm(sm, F32), vm((ny,) + sm, F32), vm((nxz,) + sm, F32)]
         nc = len(cols)
         small = ny + nxz - 1
         scratch += [
-            dma(3), dma(3), dma(2, 3), dma(2, 3), dma(nc), dma(nc), dma(nc, ny - 1), dma(nc, ny - 1),
-            dma(nc, nxz - 1), dma(nc, nxz - 1), dma(small), dma(small),
+            dma(2, 3), dma(2, 3), dma(2, 3), dma(2, 3), dma(nc), dma(nc), dma(nc, ny - 1), dma(nc, ny - 1),
+            dma(nc, nxz - 1), dma(nc, nxz - 1), dma(2, small), dma(2, small),
         ]
         whole = pl.BlockSpec(memory_space=vm)
+        shapes = (
+            jax.ShapeDtypeStruct((lat_dev, lon_dev, C), BF16),
+            jax.ShapeDtypeStruct((lat_dev, lon_dev, C), BF16),
+            jax.ShapeDtypeStruct((1, C), F32),
+            jax.ShapeDtypeStruct((HEADS, REL), F32),
+            jax.ShapeDtypeStruct((share, 3 * C), F32),
+            jax.ShapeDtypeStruct((share, C), F32),
+        )
         outs = pl.pallas_call(
             functools.partial(kernel, (ny, nx, nz), cols),
-            out_shape=(
-                jax.ShapeDtypeStruct((lat_dev, lon_dev, C), BF16),
-                jax.ShapeDtypeStruct((lat_dev, lon_dev, C), BF16),
-                jax.ShapeDtypeStruct((1, C), F32),
-                jax.ShapeDtypeStruct((HEADS, REL), F32),
-                jax.ShapeDtypeStruct((share, 3 * C), F32),
-                jax.ShapeDtypeStruct((share, C), F32),
-            ),
+            out_shape=shapes,
             in_specs=[whole] * 10,
             out_specs=(whole,) * 6,
             scratch_shapes=scratch,
@@ -555,6 +662,15 @@
             fields, grad_out, sea_mask, layernorm_gain.reshape(1, C), qkv_weight, proj_weight, bias_table,
             jnp.asarray(perm, BF16), jnp.asarray(selr, F32), jnp.asarray(self_, F32),
         )
+        anywhere = pl.BlockSpec(memory_space=pl.ANY)
+        outs = pl.pallas_call(
+            hand_over,
+            out_shape=shapes,
+            in_specs=[anywhere] * 6,
+            out_specs=(anywhere,) * 6,
+            scratch_shapes=[dma(6)],
+            compiler_params=pltpu.CompilerParams(vmem_limit_bytes=60 * 1024 * 1024),
+        )(*outs)
         updated, grad_in, grad_gain, grad_bias, grad_qkv, grad_proj = outs
         return (updated, grad_in, grad_gain.reshape(C), grad_bias, grad_qkv, grad_proj)
 

time: 82.7 us -> 124 us (1.50)
  Pallas kernels: 76.4 us -> 123 us
  local copies, waits for them, and re-layouts: 5.53 us -> 0 us
    pallas_call x1 -> x2, Pallas kernels: 76.4 us -> 123 us  [the longest x1 66.5 us: on_device(): pl.pallas_call(functools.partial(kernel, (ny, nx, nz), cols), out_shape=s...]
    unnamed x16 -> x0, local copies, waits for them, and re-layouts: 5.53 us -> none
where the time goes in v2:
time: 124 us; the launch traced here: 123 us
  Pallas kernels  123 us (99%)
    pallas_call x1, Pallas kernels, on_device(): pl.pallas_call(functools.partial(kernel, (ny, nx, nz), cols), out_shape=s...  66.5 us
    pallas_call x1, Pallas kernels, on_device(): pl.pallas_call(hand_over, out_shape=shapes, in_specs=[anywhere] * 6, out_...  56.1 us

profile of v2, /device:TPU:4, one launch (start us, length us, event | category | flops | bytes accessed | tf_op | source)
XLA Modules:
  0.0 123.4 jit_solution(14781165243755458772)
XLA Ops:
  0.6 66.5 %shard_map.145 = (bf16[18,48,512]{2,1,0:T(8,128)(2,1)}, bf16[18,48,512]{2,1,0:T(8,128)(2,1)}, f32[1,512]{1,0:T(1,128)}, f32[8,253]{1,0:T(8,128)}, f32[4,1536]{1,0:T(4,128)}, /*index=5*/f32[4,512]{1,0:T(4,128)}) custom-call(bf16[18,48,512]{2,1,0:T(8,128)(2,1)} %refs_0_.1, bf16[18,48,512]{2,1,0:T(8,128)(2,1)} %refs_1_.1, s32[18,48]{1,0:T(8,128)} %refs_2_.1, ...), custom_call_target="tpu_custom_call" | custom-call | tf_op jit(solution)/shard_map/pallas_call | solution.py:652
  67.2 56.1 %shard_map.146 = (bf16[18,48,512]{2,1,0:T(8,128)(2,1)}, bf16[18,48,512]{2,1,0:T(8,128)(2,1)}, f32[1,512]{1,0:T(1,128)}, f32[8,253]{1,0:T(8,128)}, f32[4,1536]{1,0:T(4,128)}, /*index=5*/f32[4,512]{1,0:T(4,128)}) custom-call(bf16[18,48,512]{2,1,0:T(8,128)(2,1)} %get-tuple-element.18.refs_0_, bf16[18,48,512]{2,1,0:T(8,128)(2,1)} %get-tuple-element.19.refs_1_, ...), custom_call_target="tpu_custom_call" | custom-call | tf_op jit(solution)/shard_map/pallas_call | solution.py:666

commit v3 on v2

--- a/solution.py
+++ b/solution.py
@@ -60,8 +60,12 @@
 
     it = iter(refs)
     take = lambda n=None: next(it) if n is None else [next(it) for _ in range(n)]
-    x_ref, dy_ref, mask_ref, gain_ref, wqkv, wproj, table, perm, selr, self_ = take(10)
-    upd, gin, gain_out, bias_out, gqkv, gproj = take(6)
+    given = take(11)
+    results = take(6)
+    held = take(11)
+    x_ref, mask_ref, dy_ref, table, self_, selft, selrt, gain_ref, wqkv, wproj, perm = held
+    staged = take(6)
+    upd, gin, gain_out, bias_out, gqkv, gproj = staged
     frame, win, colf = take(3)
     halos = [take(5) for _ in range(2)]
     idx = take()
@@ -71,6 +75,7 @@
     chunks = [take(7) for _ in range(nchunk)]
     sums = [take(4) for _ in range(2)]
     hs, hr, os_, or_, as_, ar, ys, yr, xs, xr, ss, sr = take(12)
+    ins, outs = take(2)
 
     lon = lax.axis_index("lon")
     lat = lax.axis_index("lat")
@@ -94,6 +99,11 @@
     for d in everyone:
         pl.semaphore_signal(barrier, inc=1, device_id=d, device_id_type=MESH)
 
+    loads = [pltpu.make_async_copy(a, b, ins.at[i]) for i, (a, b) in enumerate(zip(given, held))]
+    for load in loads:
+        load.start()
+
+    stores = [pltpu.make_async_copy(a, b, outs.at[i]) for i, (a, b) in enumerate(zip(staged, results))]
     sends = []
 
     def send(src, dst, ssem, rsem, d):
@@ -106,6 +116,7 @@
 
     lane_row = lax.broadcasted_iota(jnp.int32, (lat_dev, lat_dev * 128), 1) // 128
     pick = (lane_row == lax.broadcasted_iota(jnp.int32, (lat_dev, lat_dev * 128), 0)).astype(F32)
+    loads[1].wait()
     sea = tn(mask_ref[...].astype(F32), pick)
     colf[96:112, :] = jnp.zeros((16, FW), F32)
 
@@ -140,25 +151,41 @@
             frame[r, lon_dev : lon_dev + HALF_LON, lanes] = colf[6 * r : 6 * r + 6, lanes]
 
     xlanes, dlanes = slice(X0, X0 + XW), slice(D0, D0 + DW)
+    loads[0].wait()
     for r in range(lat_dev):
         frame[r, 0:lon_dev, X0 : X0 + C] = x_ref[r].astype(F32)
         frame[r, 0:lon_dev, M0 : M0 + 128] = sea[:, 128 * r : 128 * r + 128]
     halo_pack(0, xlanes)
     pl.semaphore_wait(barrier, len(everyone))
     xcopies = halo_send(0)
+    loads[2].wait()
     for r in range(lat_dev):
         frame[r, 0:lon_dev, D0 : D0 + C] = dy_ref[r].astype(F32)
     halo_pack(1, dlanes)
     dcopies = halo_send(1)
 
+    def pieces(v, n):
+        out = []
+        for i in range(n):
+            part = v.astype(BF16)
+            out.append(part)
+            if i < n - 1:
+                v = v - part.astype(F32)
+        return out
+
+    for i in range(3, 11):
+        loads[i].wait()
     tb[...] = jnp.zeros_like(tb)
     tb[:, 0:REL] = table[...]
-    hi = lax.Precision.HIGHEST
+    shifted = []
     for h in range(HEADS):
         line = jnp.broadcast_to(tb[h : h + 1, :], (128, 256))
-        rolled = pltpu.roll(pltpu.roll(line, 2, 1), 128, 1, stride=1, stride_axis=0)
-        both = nt(nt(selr[...], rolled[:, 0:128], precision=hi), selr[...], precision=hi)
-        bias2[h // 2, TP * (h % 2) : TP * (h % 2) + TP, :] = both[0:TP]
+        shifted.append(pltpu.roll(pltpu.roll(line, 2, 1), 128, 1, stride=1, stride_axis=0)[:, 0:128])
+    by_query = sum(nn(v, selft[...]) for v in pieces(jnp.concatenate(shifted, axis=0), 3))
+    by_query = jnp.concatenate([by_query[128 * h : 128 * h + 128] for h in range(HEADS)], axis=1)
+    whole_bias = sum(nn(self_[0:TP, :], v) for v in pieces(by_query, 3))
+    for p in range(PAIRS):
+        bias2[p] = whole_bias[:, 256 * p : 256 * p + 256]
 
     zero_tail = jnp.zeros((RP - ROWS, C), BF16)
     normed[ROWS:RP, :] = zero_tail
@@ -207,6 +234,14 @@
 
     def rows_of(k):
         return pl.ds(pl.multiple_of(k * TP, TP), TP)
+
+    def by_three(step):
+        def body(i, carry):
+            for j in range(3):
+                carry = step(3 * i + j, carry)
+            return carry
+
+        return body
 
     def ln_step(k, carry):
         w = idx[k]
@@ -240,35 +275,33 @@
     q_lo = jnp.where(low, 0.125, 0.0).astype(BF16)
     q_hi = jnp.where(low, 0.0, 0.125).astype(BF16)
 
-    def both_heads(v, lo, hi_):
-        return jnp.concatenate([v * lo, v * hi_], axis=0)
-
-    def join_heads(v):
-        return jnp.where(low, v[0:TP], v[TP : 2 * TP])
-
-    def per_head(v):
-        return v.reshape(2, TP, 128)
+    def both_heads(v, lo, hi):
+        return jnp.concatenate([pad_rows(v * lo, 128), pad_rows(v * hi, 128)], axis=0)
+
+    def own_head(v):
+        return jnp.transpose(jnp.concatenate([v[0:64, 0:128], v[64:128, 128:256]], axis=0))[0:TP]
 
     def attend(k, carry):
         rows = rows_of(k)
         add = madd[k]
-        add2 = jnp.concatenate([add, add], axis=0)
+        add2 = jnp.concatenate([add, add], axis=1)
         scores = []
         for p in range(PAIRS):
-            q = pad_rows(packed[rows, 128 * p : 128 * p + 128], 128)
-            k2 = both_heads(packed[rows, C + 128 * p : C + 128 * p + 128], q_lo, q_hi)
-            scores.append(nt(k2, q) + bias2[p] + add2)
+            q2 = both_heads(packed[rows, 128 * p : 128 * p + 128], q_lo, q_hi)
+            scores.append(nt(packed[rows, C + 128 * p : C + 128 * p + 128], q2) + bias2[p] + add2)
+        mixes = []
         for p in range(PAIRS):
-            s = per_head(scores[p])
-            e = jnp.exp(s - jnp.max(s, axis=1, keepdims=True))
-            pr = (e * (1.0 / jnp.sum(e, axis=1, keepdims=True))).reshape(2 * TP, 128)
+            s = scores[p]
+            e = jnp.exp(s - jnp.max(s, axis=0, keepdims=True))
+            pr = e * (1.0 / jnp.sum(e, axis=0, keepdims=True))
             probs[k * PAIRS + p] = pr
-            v2 = both_heads(packed[rows, 2 * C + 128 * p : 2 * C + 128 * p + 128], one_lo, one_hi)
-            mixed[rows, 128 * p : 128 * p + 128] = tn(pr.astype(BF16), v2)[0:TP].astype(BF16)
+            mixes.append(tn(packed[rows, 2 * C + 128 * p : 2 * C + 128 * p + 128], pr.astype(BF16)))
+        for p in range(PAIRS):
+            mixed[rows, 128 * p : 128 * p + 128] = own_head(mixes[p]).astype(BF16)
         return carry
 
     def forward(first, last):
-        lax.fori_loop(first, last, ln_step, 0)
+        lax.fori_loop(first // 3, last // 3, by_three(ln_step), 0)
         rows = slice(first * TP, last * TP)
         packed[rows, :] = nn(normed[rows, :], wqkv[...]).astype(BF16)
         lax.fori_loop(first, last, attend, 0)
@@ -300,7 +333,7 @@
     halo_land(1, dlanes, dcopies)
     for w in outer:
         cut(w, dlanes)
-    lax.fori_loop(0, SLOTS, dy_step, 0)
+    lax.fori_loop(0, SLOTS // 3, by_three(dy_step), 0)
     gm[...] = nt(gz[0:ROWS, :], wproj[...]).astype(BF16)
     ntp[...] = nt(perm[...], normed[...]).astype(BF16)
 
@@ -406,38 +439,36 @@
         res[k] = win[w, :, X0 : X0 + C] + jnp.concatenate([m] * 4, axis=1) * gnacc[rows_of(k), :]
         return carry
 
-    lax.fori_loop(0, SLOTS, updated_step, 0)
+    lax.fori_loop(0, SLOTS // 3, by_three(updated_step), 0)
     out_copies = [window_back(0, X0), None]
 
     def backward(p):
-        bacc[p] = jnp.zeros((2 * TP, 128), F32)
+        bacc[p] = jnp.zeros((TP, 256), F32)
 
         def step(i, carry):
             ks = [3 * i + j for j in range(3)]
-            ds_, dps = [], []
+            d2s, dps = [], []
             for k in ks:
                 rows = rows_of(k)
-                ds_.append(pad_rows(gm[rows, 128 * p : 128 * p + 128], 128))
-                v2 = both_heads(packed[rows, 2 * C + 128 * p : 2 * C + 128 * p + 128], one_lo, one_hi)
-                dps.append(nt(v2, ds_[-1]))
+                d2s.append(both_heads(gm[rows, 128 * p : 128 * p + 128], one_lo, one_hi))
+                dps.append(nt(packed[rows, 2 * C + 128 * p : 2 * C + 128 * p + 128], d2s[-1]))
             dss, dvs = [], []
             for j, k in enumerate(ks):
                 pr = probs[k * PAIRS + p]
                 t = pr * dps[j]
-                dot = jnp.sum(per_head(t), axis=1, keepdims=True)
-                dss.append((per_head(t) - per_head(pr) * dot).reshape(2 * TP, 128))
-                dvs.append(nn(pr.astype(BF16), ds_[j]))
+                dss.append(t - pr * jnp.sum(t, axis=0, keepdims=True))
+                dvs.append(nn(pr.astype(BF16), d2s[j]))
             bacc[p] += dss[0] + dss[1] + dss[2]
+            dqs = []
             for j, k in enumerate(ks):
                 rows = rows_of(k)
                 ds = dss[j].astype(BF16)
-                q = pad_rows(packed[rows, 128 * p : 128 * p + 128], 128)
-                k2 = both_heads(packed[rows, C + 128 * p : C + 128 * p + 128], q_lo, q_hi)
-                dk2 = nn(ds, q)
-                dq = tn(ds, k2)
-                dp3[p, rows, 0:128] = dq[0:TP].astype(BF16)
-                dp3[p, rows, 128:256] = (join_heads(dk2) * 0.125).astype(BF16)
-                dp3[p, rows, 256:384] = join_heads(dvs[j]).astype(BF16)
+                q2 = both_heads(packed[rows, 128 * p : 128 * p + 128], q_lo, q_hi)
+                dqs.append(tn(packed[rows, C + 128 * p : C + 128 * p + 128], ds))
+                dp3[p, rows, 128:256] = nn(ds, q2).astype(BF16)
+                dp3[p, rows, 256:384] = dvs[j].astype(BF16)
+            for j, k in enumerate(ks):
+                dp3[p, rows_of(k), 0:128] = (own_head(dqs[j]) * 0.125).astype(BF16)
             return carry
 
         lax.fori_loop(0, SLOTS // 3, step, 0)
@@ -493,13 +524,6 @@
             acc = acc + smx[j]
         return acc
 
-    for h in range(HEADS):
-        g = pad_rows(bacc[h // 2, TP * (h % 2) : TP * (h % 2) + TP, :], 128)
-        spread = tn(self_[...], tn(g, selr[...], precision=hi), precision=hi)
-        wide = jnp.concatenate([spread, jnp.zeros((128, 128), F32)], axis=1)
-        sums[0][0][h : h + 1, :] = jnp.sum(pltpu.roll(wide, 0, 1, stride=1, stride_axis=0), axis=0, keepdims=True)
-    bias_copies = sum_core(0)
-
     def norm_back(k, total):
         w = idx[k]
         rows = rows_of(k)
@@ -512,40 +536,68 @@
         res[k] = win[w, :, D0 : D0 + C] + inv * mid
         return total + jnp.sum(gn * hat, axis=0, keepdims=True)
 
-    gsum = lax.fori_loop(0, SLOTS, norm_back, jnp.zeros((1, C), F32))
+    gsum = lax.fori_loop(0, SLOTS // 3, by_three(norm_back), jnp.zeros((1, C), F32))
     sums[1][0][...] = jnp.zeros((8, 128), F32)
     for j in range(4):
         sums[1][0][j : j + 1, :] = gsum[:, 128 * j : 128 * j + 128]
     gain_copies = sum_core(1)
     st[4] = chunk_y(4, st[4])
     out_copies[1] = window_back(1, D0)
-
     st[3] = chunk_x(3, st[3])
+
+    stacked = jnp.concatenate([bacc[h // 2, :, 128 * (h % 2) : 128 * (h % 2) + 128] for h in range(HEADS)], axis=0)
+    by_place = sum(nn(v, self_[...]) for v in pieces(stacked, 2))
+    by_place = jnp.concatenate([by_place[TP * h : TP * h + TP] for h in range(HEADS)], axis=1)
+    spread = sum(nn(selrt[:, 0:TP], v) for v in pieces(by_place, 2))
+    for h in range(HEADS):
+        wide = jnp.concatenate([spread[:, 128 * h : 128 * h + 128], jnp.zeros((128, 128), F32)], axis=1)
+        sums[0][0][h : h + 1, :] = jnp.sum(pltpu.roll(wide, 0, 1, stride=1, stride_axis=0), axis=0, keepdims=True)
+    bias_copies = sum_core(0)
+
+    st[4] = chunk_x(4, st[4])
     bias_copies = sum_y(0, bias_copies)
     gain_copies = sum_y(1, gain_copies)
-    st[4] = chunk_x(4, st[4])
+    finish(0, out_copies[0], upd)
+    stores[0].start()
     bias_copies = sum_xz(0, bias_copies)
     gain_copies = sum_xz(1, gain_copies)
-    finish(0, out_copies[0], upd)
     for c in range(nchunk - 1):
         chunk_end(c, st[c])
     finish(1, out_copies[1], gin)
+    stores[1].start()
     bias_out[...] = sum_end(0, bias_copies)[:, 0:REL]
     chunk_end(nchunk - 1, st[nchunk - 1])
     acc = sum_end(1, gain_copies)
     for j in range(4):
         gain_out[:, 128 * j : 128 * j + 128] = acc[j : j + 1, :]
+    for store in stores[2:]:
+        store.start()
     for copy in sends:
         copy.wait_send()
+    for store in stores:
+        store.wait()
 
 
 def hand_over(*refs):
-    sem = refs[12]
-    copies = [pltpu.make_async_copy(refs[i], refs[6 + i], sem.at[i]) for i in range(6)]
-    for copy in copies:
-        copy.start()
-    for copy in copies:
-        copy.wait()
+    arrived, left = refs[18:20]
+    steps = []
+    for i in range(6):
+        rows = refs[i].shape[0]
+        size = 3 if i < 2 else rows
+        steps += [(i, pl.ds(start, size)) for start in range(0, rows, size)]
+    fetches = [
+        pltpu.make_async_copy(refs[i].at[at], refs[12 + i].at[at], arrived.at[n]) for n, (i, at) in enumerate(steps)
+    ]
+    stores = [
+        pltpu.make_async_copy(refs[12 + i].at[at], refs[6 + i].at[at], left.at[n]) for n, (i, at) in enumerate(steps)
+    ]
+    for fetch in fetches:
+        fetch.start()
+    for fetch, store in zip(fetches, stores):
+        fetch.wait()
+        store.start()
+    for store in stores:
+        store.wait()
 
 
 def constants(ny, nx, nz):
@@ -560,11 +612,11 @@
                     perm[to + np.arange(share), start + np.arange(share)] = 1
     a = np.arange(T)
     pa = (a // WIN_LON) * (2 * WIN_LON - 1) + a % WIN_LON
-    selr = np.zeros((128, 128), np.float32)
-    selr[a, 126 - pa] = 1
+    selrt = np.zeros((128, 128), np.float32)
+    selrt[126 - pa, a] = 1
     self_ = np.zeros((128, 128), np.float32)
     self_[a, pa] = 1
-    return perm, selr, self_
+    return perm, self_, self_.T, selrt
 
 
 def solution(mesh):
@@ -580,10 +632,32 @@
     nwin = 12
     vm = pltpu.VMEM
     dma = lambda *s: pltpu.SemaphoreType.DMA(s)
-    perm, selr, self_ = constants(ny, nx, nz)
+    perm, self_, selft, selrt = (jnp.asarray(v, BF16) for v in constants(ny, nx, nz))
 
     def on_device(fields, grad_out, layernorm_gain, qkv_weight, proj_weight, bias_table, sea_mask):
+        shapes = (
+            jax.ShapeDtypeStruct((lat_dev, lon_dev, C), BF16),
+            jax.ShapeDtypeStruct((lat_dev, lon_dev, C), BF16),
+            jax.ShapeDtypeStruct((1, C), F32),
+            jax.ShapeDtypeStruct((HEADS, REL), F32),
+            jax.ShapeDtypeStruct((share, 3 * C), F32),
+            jax.ShapeDtypeStruct((share, C), F32),
+        )
         scratch = [
+            vm((lat_dev, lon_dev, C), BF16),
+            vm((lat_dev, lon_dev), jnp.int32),
+            vm((lat_dev, lon_dev, C), BF16),
+            vm((HEADS, REL), F32),
+            vm((128, 128), BF16),
+            vm((128, 128), BF16),
+            vm((128, 128), BF16),
+            vm((1, C), F32),
+            vm((C, 3 * C), BF16),
+            vm((C, C), BF16),
+            vm((C, C), BF16),
+        ]
+        scratch += [vm(v.shape, v.dtype) for v in shapes]
+        scratch += [
             vm((lat_dev + 3, 56, FW), F32),
             vm((nwin, TP, FW), F32),
             vm((112, FW), F32),
@@ -599,7 +673,7 @@
         scratch += [
             pltpu.SMEM((16,), jnp.int32),
             vm((HEADS, 256), F32),
-            vm((PAIRS, 2 * TP, 128), F32),
+            vm((PAIRS, TP, 256), F32),
             vm((SLOTS, TP, 128), F32),
             vm((ROWS, C), F32),
             vm((ROWS, 128), F32),
@@ -610,10 +684,10 @@
             vm((RP, C), BF16),
             vm((C, RP), BF16),
             vm((C, RP), BF16),
-            vm((SLOTS * PAIRS, 2 * TP, 128), F32),
+            vm((SLOTS * PAIRS, TP, 256), F32),
             vm((PAIRS, RP, 384), BF16),
             vm((ROWS, C), F32),
-            vm((PAIRS, 2 * TP, 128), F32),
+            vm((PAIRS, TP, 256), F32),
             vm((SLOTS, TP, C), F32),
             vm((2, lat_dev + 3, 56, C), F32),
             vm((2, 144, C), BF16),
@@ -638,37 +712,28 @@
         small = ny + nxz - 1
         scratch += [
             dma(2, 3), dma(2, 3), dma(2, 3), dma(2, 3), dma(nc), dma(nc), dma(nc, ny - 1), dma(nc, ny - 1),
-            dma(nc, nxz - 1), dma(nc, nxz - 1), dma(2, small), dma(2, small),
+            dma(nc, nxz - 1), dma(nc, nxz - 1), dma(2, small), dma(2, small), dma(11), dma(6),
         ]
-        whole = pl.BlockSpec(memory_space=vm)
-        shapes = (
-            jax.ShapeDtypeStruct((lat_dev, lon_dev, C), BF16),
-            jax.ShapeDtypeStruct((lat_dev, lon_dev, C), BF16),
-            jax.ShapeDtypeStruct((1, C), F32),
-            jax.ShapeDtypeStruct((HEADS, REL), F32),
-            jax.ShapeDtypeStruct((share, 3 * C), F32),
-            jax.ShapeDtypeStruct((share, C), F32),
-        )
+        anywhere = pl.BlockSpec(memory_space=pl.ANY)
         outs = pl.pallas_call(
             functools.partial(kernel, (ny, nx, nz), cols),
             out_shape=shapes,
-            in_specs=[whole] * 10,
-            out_specs=(whole,) * 6,
+            in_specs=[anywhere] * 11,
+            out_specs=(anywhere,) * 6,
             scratch_shapes=scratch,
             compiler_params=pltpu.CompilerParams(
                 collective_id=0, has_side_effects=True, vmem_limit_bytes=60 * 1024 * 1024
             ),
         )(
-            fields, grad_out, sea_mask, layernorm_gain.reshape(1, C), qkv_weight, proj_weight, bias_table,
-            jnp.asarray(perm, BF16), jnp.asarray(selr, F32), jnp.asarray(self_, F32),
+            fields, sea_mask, grad_out, bias_table, self_, selft, selrt,
+            layernorm_gain.reshape(1, C), qkv_weight, proj_weight, perm,
         )
-        anywhere = pl.BlockSpec(memory_space=pl.ANY)
         outs = pl.pallas_call(
             hand_over,
             out_shape=shapes,
             in_specs=[anywhere] * 6,
             out_specs=(anywhere,) * 6,
-            scratch_shapes=[dma(6)],
+            scratch_shapes=[vm(v.shape, v.dtype) for v in shapes] + [dma(16), dma(16)],
             compiler_params=pltpu.CompilerParams(vmem_limit_bytes=60 * 1024 * 1024),
         )(*outs)
         updated, grad_in, grad_gain, grad_bias, grad_qkv, grad_proj = outs

time: 124 us -> 69.7 us (0.56)
  Pallas kernels: 123 us -> 68.1 us
    pallas_call x1, Pallas kernels: 56.1 us -> 2.49 us  [on_device(): pl.pallas_call(hand_over, out_shape=shapes, in_specs=[anywhere] * 6, out_...]
where the time goes in v3:
time: 69.7 us; the launch traced here: 68.9 us
  Pallas kernels  68.1 us (98%)
  between operations  0.82 us (1%)
    pallas_call x1, Pallas kernels, on_device(): pl.pallas_call(functools.partial(kernel, (ny, nx, nz), cols), out_shape=s...  65.6 us
    pallas_call x1, Pallas kernels, on_device(): pl.pallas_call(hand_over, out_shape=shapes, in_specs=[anywhere] * 6, out_...  2.49 us

profile of v3, /device:TPU:4, one launch (start us, length us, event | category | flops | bytes accessed | tf_op | source)
XLA Modules:
  0.0 68.9 jit_solution(11955396736707528663)
XLA Ops:
  0.6 65.6 %shard_map.154 = (bf16[18,48,512]{2,1,0:T(8,128)(2,1)}, bf16[18,48,512]{2,1,0:T(8,128)(2,1)}, f32[1,512]{1,0:T(1,128)}, f32[8,253]{1,0:T(8,128)}, f32[4,1536]{1,0:T(4,128)}, /*index=5*/f32[4,512]{1,0:T(4,128)}) custom-call(bf16[18,48,512]{2,1,0:T(8,128)(2,1)} %refs_0_.1, s32[18,48]{1,0:T(8,128)} %refs_1_.1, bf16[18,48,512]{2,1,0:T(8,128)(2,1)} %refs_2_.1, ...), custom_call_target="tpu_custom_call" | custom-call | tf_op jit(solution)/shard_map/pallas_call | solution.py:718
  66.2 2.5 %shard_map.155 = (bf16[18,48,512]{2,1,0:T(8,128)(2,1)}, bf16[18,48,512]{2,1,0:T(8,128)(2,1)}, f32[1,512]{1,0:T(1,128)}, f32[8,253]{1,0:T(8,128)}, f32[4,1536]{1,0:T(4,128)}, /*index=5*/f32[4,512]{1,0:T(4,128)}) custom-call(bf16[18,48,512]{2,1,0:T(8,128)(2,1)} %get-tuple-element.18.refs_0_, bf16[18,48,512]{2,1,0:T(8,128)(2,1)} %get-tuple-element.19.refs_1_, ...), custom_call_target="tpu_custom_call" | custom-call | tf_op jit(solution)/shard_map/pallas_call | solution.py:731

commit v4 on v3

--- a/solution.py
+++ b/solution.py
@@ -25,7 +25,6 @@
 RP = 768
 REL = 253
 X0, M0, D0, FW = 0, 512, 640, 1152
-XW, DW = 640, 512
 EARLY = 3
 EPS = 1e-5
 
@@ -68,13 +67,15 @@
     upd, gin, gain_out, bias_out, gqkv, gproj = staged
     frame, win, colf = take(3)
     halos = [take(5) for _ in range(2)]
+    masks = take(3)
     idx = take()
     tb, bias2, madd, xhat, invd, normed, gz, gm, packed, mixed, ntp, mtp, probs, dp3, gnacc, bacc = take(16)
     res, of = take(2)
     ocs, ors, ocr, orr, occ = take(5)
-    chunks = [take(7) for _ in range(nchunk)]
-    sums = [take(4) for _ in range(2)]
-    hs, hr, os_, or_, as_, ar, ys, yr, xs, xr, ss, sr = take(12)
+    chunks = [take(8) for _ in range(nchunk)]
+    groups = [take(2) for _ in range(2)]
+    sums = take(6)
+    hs, hr, ms, mr, os_, or_, as_, ar, ys, yr, xs, xr, zs, zr, ss, sr = take(16)
     ins, outs = take(2)
 
     lon = lax.axis_index("lon")
@@ -87,15 +88,15 @@
 
     partner = dev(lon, z * 2 + (1 - core))
     ypeer = [dev(((y + d) % ny) * nx + xh, lat) for d in range(1, ny)]
-    xzd = [(a, b) for a in range(nx) for b in range(nz) if (a, b) != (0, 0)]
-    xzpeer = [dev(y * nx + (xh + a) % nx, ((z + b) % nz) * 2 + core) for a, b in xzd]
+    xpeer = dev(y * nx + (1 - xh), lat)
+    zpeer = [dev(lon, ((z + d) % nz) * 2 + core) for d in range(1, nz)]
     west, east = (lon + nlon - 1) % nlon, (lon + 1) % nlon
     north, south = (lat + nlat - 1) % nlat, (lat + 1) % nlat
     back = [dev(west, lat), dev(lon, north), dev(west, north)]
     forth = [dev(east, lat), dev(lon, south), dev(east, south)]
 
     barrier = pltpu.get_barrier_semaphore()
-    everyone = [partner] + ypeer + xzpeer + back + forth
+    everyone = [partner, xpeer] + ypeer + zpeer + back + forth
     for d in everyone:
         pl.semaphore_signal(barrier, inc=1, device_id=d, device_id_type=MESH)
 
@@ -116,8 +117,12 @@
 
     lane_row = lax.broadcasted_iota(jnp.int32, (lat_dev, lat_dev * 128), 1) // 128
     pick = (lane_row == lax.broadcasted_iota(jnp.int32, (lat_dev, lat_dev * 128), 0)).astype(F32)
+
+    def spread_mask(ref):
+        return tn(ref[...].astype(F32), pick)
+
     loads[1].wait()
-    sea = tn(mask_ref[...].astype(F32), pick)
+    sea = spread_mask(mask_ref)
     colf[96:112, :] = jnp.zeros((16, FW), F32)
 
     def halo_pack(h, lanes):
@@ -150,13 +155,14 @@
         for r in range(lat_dev):
             frame[r, lon_dev : lon_dev + HALF_LON, lanes] = colf[6 * r : 6 * r + 6, lanes]
 
-    xlanes, dlanes = slice(X0, X0 + XW), slice(D0, D0 + DW)
+    xlanes, dlanes = slice(X0, X0 + C), slice(D0, D0 + C)
     loads[0].wait()
     for r in range(lat_dev):
         frame[r, 0:lon_dev, X0 : X0 + C] = x_ref[r].astype(F32)
         frame[r, 0:lon_dev, M0 : M0 + 128] = sea[:, 128 * r : 128 * r + 128]
     halo_pack(0, xlanes)
     pl.semaphore_wait(barrier, len(everyone))
+    mcopies = [send(mask_ref, masks[i], ms.at[i], mr.at[i], back[i]) for i in range(3)]
     xcopies = halo_send(0)
     loads[2].wait()
     for r in range(lat_dev):
@@ -314,9 +320,21 @@
         slot_window(k, list(zip(inner, inner_rank)))
     forward(0, EARLY)
 
+    mlanes = slice(M0, M0 + 128)
+    for copy in mcopies:
+        copy.wait_recv()
+    sea = spread_mask(masks[0])
+    for r in range(lat_dev):
+        frame[r, lon_dev : lon_dev + HALF_LON, mlanes] = sea[0:HALF_LON, 128 * r : 128 * r + 128]
+    sea = spread_mask(masks[1])
+    for r in range(HALF_LAT):
+        frame[lat_dev + r, 0:lon_dev, mlanes] = sea[:, 128 * r : 128 * r + 128]
+    sea = spread_mask(masks[2])
+    for r in range(HALF_LAT):
+        frame[lat_dev + r, lon_dev : lon_dev + HALF_LON, mlanes] = sea[0:HALF_LON, 128 * r : 128 * r + 128]
     halo_land(0, xlanes, xcopies)
     for w in outer:
-        cut(w, xlanes)
+        cut(w, slice(X0, M0 + 128))
         active[w] = holds_sea(w)
     rest = [jnp.int32(1)] * nwin
     for w, at in zip(inner, inner_rank):
@@ -362,34 +380,54 @@
         return out
 
     def chunk_x(c, copies):
-        own, ysend, yrecv, xsend, xrecv = chunks[c][2:7]
+        own, ysend, yrecv, xsend, xrecv, xown = chunks[c][2:8]
         s = own[pl.ds(pl.multiple_of(y * ysz, ysz), ysz), :]
         for d in range(1, ny):
             copies[d - 1].wait_recv()
             s = s + yrecv[d - 1].astype(F32)
-        for j in range(nxz):
-            xsend[j] = s[share * j : share * j + share]
-        out = []
-        for i, (a, b) in enumerate(xzd):
-            j = ((xh + a) % nx) * nz + (z + b) % nz
-            out.append(send(xsend.at[j], xrecv.at[i], xs.at[c, i], xr.at[c, i], xzpeer[i]))
-        return out
-
-    def chunk_end(c, copies):
-        xsend, xrecv = chunks[c][5:7]
-        s = xsend[xh * nz + z]
+        top, low_half = s[0 : ysz // 2], s[ysz // 2 : ysz]
+        first = xh == 0
+        xsend[...] = jnp.where(first, low_half, top).astype(BF16)
+        xown[...] = jnp.where(first, top, low_half)
+        return [send(xsend, xrecv, xs.at[c], xr.at[c], xpeer)]
+
+    def chunk_z(c, copies):
+        xsend, xrecv, xown = chunks[c][5:8]
+        zsend = groups[0 if c < 4 else 1][0]
+        start = sum(cols[:c]) if c < 4 else 0
+        copies[0].wait_recv()
+        s = xown[...] + xrecv[...].astype(F32)
+        for j in range(nz):
+            zsend[j, :, start : start + cols[c]] = s[share * j : share * j + share]
+
+    def group_send(g):
+        zsend, zrecv = groups[g]
+        return [
+            send(zsend.at[(z + d) % nz], zrecv.at[d - 1], zs.at[g, d - 1], zr.at[g, d - 1], zpeer[d - 1])
+            for d in range(1, nz)
+        ]
+
+    def group_end(g, copies):
+        zsend, zrecv = groups[g]
+        s = zsend[z]
         for i, copy in enumerate(copies):
             copy.wait_recv()
-            s = s + xrecv[i]
-        if c == 0:
-            gproj[...] = s
-        else:
-            p = c - 1
-            for part in range(3):
-                gqkv[:, C * part + 128 * p : C * part + 128 * p + 128] = s[:, 128 * part : 128 * part + 128]
+            s = s + zrecv[i]
+        start = 0
+        for c in range(nchunk):
+            if (c < 4) != (g == 0):
+                continue
+            if c == 0:
+                gproj[...] = s[:, 0:C]
+            else:
+                p = c - 1
+                for part in range(3):
+                    at = start + 128 * part
+                    gqkv[:, C * part + 128 * p : C * part + 128 * p + 128] = s[:, at : at + 128]
+            start += cols[c]
 
     def window_back(o, lane0):
-        for w in range(nwin):
+        def place_window(w):
             wr, wc = w // wcols, w % wcols
             slot = jnp.minimum(place[w], SLOTS - 1)
             for i in range(WIN_LAT):
@@ -398,19 +436,29 @@
                 of[o, HALF_LAT + WIN_LAT * wr + i, c0 : c0 + WIN_LON, :] = jnp.where(
                     place[w] < SLOTS, res[slot, at, :], win[w, at, lane0 : lane0 + C]
                 )
-        colf[0:112, 0:C] = jnp.zeros((112, C), F32)
+
+        for w in range(wcols - 1, nwin, wcols):
+            place_window(w)
+        colf[0 : 6 * HALF_LAT, 0:C] = jnp.zeros((6 * HALF_LAT, C), F32)
         for r in range(HALF_LAT, lat_dev):
             colf[6 * r : 6 * r + 6, 0:C] = of[o, r, lon_dev : lon_dev + HALF_LON, :]
         ocs[o, 0:112] = colf[0:112, 0:C].astype(BF16)
         for r in range(HALF_LAT):
             colf[6 * r : 6 * r + 6, 0:C] = of[o, lat_dev + r, lon_dev : lon_dev + HALF_LON, :]
-            ors[o, r] = of[o, lat_dev + r, 0:lon_dev, :].astype(BF16)
         ocs[o, 112:144] = colf[0:32, 0:C].astype(BF16)
-        return [
+        copies = [
             send(ocs.at[o, 0:112], ocr.at[o], os_.at[o, 0], or_.at[o, 0], forth[0]),
-            send(ors.at[o], orr.at[o], os_.at[o, 1], or_.at[o, 1], forth[1]),
             send(ocs.at[o, 112:144], occ.at[o], os_.at[o, 2], or_.at[o, 2], forth[2]),
         ]
+        for w in range(nwin - wcols, nwin - 1):
+            place_window(w)
+        for r in range(HALF_LAT):
+            ors[o, r] = of[o, lat_dev + r, 0:lon_dev, :].astype(BF16)
+        copies.insert(1, send(ors.at[o], orr.at[o], os_.at[o, 1], or_.at[o, 1], forth[1]))
+        for w in range(nwin - wcols):
+            if w % wcols < wcols - 1:
+                place_window(w)
+        return copies
 
     def finish(o, copies, out):
         copies[1].wait_recv()
@@ -483,46 +531,13 @@
     for p in range(PAIRS):
         backward(p)
         st[p + 1] = chunk_start(p + 1, ntp, dp3.at[p])
-        if p >= 0:
-            st[p] = chunk_y(p, st[p])
+        st[p] = chunk_y(p, st[p])
         if p >= 1:
             st[p - 1] = chunk_x(p - 1, st[p - 1])
+        if p >= 2:
+            chunk_z(p - 2, st[p - 2])
         grad_normed(p)
-
-    def sum_core(g):
-        sm, smc = sums[g][0:2]
-        return send(sm, smc, ss.at[g, 0], sr.at[g, 0], partner)
-
-    def sum_y(g, copy):
-        sm, smc, smy, smx = sums[g]
-        copy.wait_recv()
-        smy[y] = sm[...] + smc[...]
-        return [
-            send(smy.at[y], smy.at[y], ss.at[g, d], sr.at[g, d], ypeer[d - 1]) for d in range(1, ny)
-        ]
-
-    def sum_xz(g, copies):
-        sm, smc, smy, smx = sums[g]
-        for copy in copies:
-            copy.wait_recv()
-        acc = smy[0]
-        for j in range(1, ny):
-            acc = acc + smy[j]
-        here = xh * nz + z
-        smx[here] = acc
-        return [
-            send(smx.at[here], smx.at[here], ss.at[g, ny + i], sr.at[g, ny + i], xzpeer[i])
-            for i in range(len(xzd))
-        ]
-
-    def sum_end(g, copies):
-        smx = sums[g][3]
-        for copy in copies:
-            copy.wait_recv()
-        acc = smx[0]
-        for j in range(1, nxz):
-            acc = acc + smx[j]
-        return acc
+    st[4] = chunk_y(4, st[4])
 
     def norm_back(k, total):
         w = idx[k]
@@ -537,11 +552,6 @@
         return total + jnp.sum(gn * hat, axis=0, keepdims=True)
 
     gsum = lax.fori_loop(0, SLOTS // 3, by_three(norm_back), jnp.zeros((1, C), F32))
-    sums[1][0][...] = jnp.zeros((8, 128), F32)
-    for j in range(4):
-        sums[1][0][j : j + 1, :] = gsum[:, 128 * j : 128 * j + 128]
-    gain_copies = sum_core(1)
-    st[4] = chunk_y(4, st[4])
     out_copies[1] = window_back(1, D0)
     st[3] = chunk_x(3, st[3])
 
@@ -551,25 +561,45 @@
     spread = sum(nn(selrt[:, 0:TP], v) for v in pieces(by_place, 2))
     for h in range(HEADS):
         wide = jnp.concatenate([spread[:, 128 * h : 128 * h + 128], jnp.zeros((128, 128), F32)], axis=1)
-        sums[0][0][h : h + 1, :] = jnp.sum(pltpu.roll(wide, 0, 1, stride=1, stride_axis=0), axis=0, keepdims=True)
-    bias_copies = sum_core(0)
-
+        sums[0][h : h + 1, 0:256] = jnp.sum(pltpu.roll(wide, 0, 1, stride=1, stride_axis=0), axis=0, keepdims=True)
+    sm, smc, smy, sma, smx, smz = sums
+    sm[4:8, 256:384] = jnp.zeros((4, 128), F32)
+    for j in range(4):
+        sm[j : j + 1, 256:384] = gsum[:, 128 * j : 128 * j + 128]
+    copy = send(sm, smc, ss.at[0], sr.at[0], partner)
+    chunk_z(2, st[2])
+    chunk_z(3, st[3])
+    group0 = group_send(0)
     st[4] = chunk_x(4, st[4])
-    bias_copies = sum_y(0, bias_copies)
-    gain_copies = sum_y(1, gain_copies)
+    copy.wait_recv()
+    smy[y] = sm[...] + smc[...]
+    copies = [send(smy.at[y], smy.at[y], ss.at[d], sr.at[d], ypeer[d - 1]) for d in range(1, ny)]
     finish(0, out_copies[0], upd)
     stores[0].start()
-    bias_copies = sum_xz(0, bias_copies)
-    gain_copies = sum_xz(1, gain_copies)
-    for c in range(nchunk - 1):
-        chunk_end(c, st[c])
+    chunk_z(4, st[4])
+    group1 = group_send(1)
+    for copy in copies:
+        copy.wait_recv()
+    acc = smy[0]
+    for j in range(1, ny):
+        acc = acc + smy[j]
+    sma[...] = acc
+    copy = send(sma, smx, ss.at[ny], sr.at[ny], xpeer)
+    group_end(0, group0)
+    copy.wait_recv()
+    smz[z] = sma[...] + smx[...]
+    copies = [send(smz.at[z], smz.at[z], ss.at[ny + d], sr.at[ny + d], zpeer[d - 1]) for d in range(1, nz)]
     finish(1, out_copies[1], gin)
     stores[1].start()
-    bias_out[...] = sum_end(0, bias_copies)[:, 0:REL]
-    chunk_end(nchunk - 1, st[nchunk - 1])
-    acc = sum_end(1, gain_copies)
+    group_end(1, group1)
+    for copy in copies:
+        copy.wait_recv()
+    acc = smz[0]
+    for j in range(1, nz):
+        acc = acc + smz[j]
+    bias_out[...] = acc[:, 0:REL]
     for j in range(4):
-        gain_out[:, 128 * j : 128 * j + 128] = acc[j : j + 1, :]
+        gain_out[:, 128 * j : 128 * j + 128] = acc[j : j + 1, 256:384]
     for store in stores[2:]:
         store.start()
     for copy in sends:
@@ -662,7 +692,7 @@
             vm((nwin, TP, FW), F32),
             vm((112, FW), F32),
         ]
-        for wide in (XW, DW):
+        for wide in (C, C):
             scratch += [
                 vm((112, wide), BF16),
                 vm((112, wide), BF16),
@@ -670,6 +700,7 @@
                 vm((3, lon_dev, wide), BF16),
                 vm((32, wide), BF16),
             ]
+        scratch += [vm((lat_dev, lon_dev), jnp.int32)] * 3
         scratch += [
             pltpu.SMEM((16,), jnp.int32),
             vm((HEADS, 256), F32),
@@ -703,16 +734,19 @@
                 vm((half, n), F32),
                 vm((half, n), BF16),
                 vm((ny - 1, ysz, n), BF16),
-                vm((nxz, share, n), F32),
-                vm((nxz - 1, share, n), F32),
+                vm((ysz // 2, n), BF16),
+                vm((ysz // 2, n), BF16),
+                vm((ysz // 2, n), F32),
             ]
-        for sm in ((8, 256), (8, 128)):
-            scratch += [vm(sm, F32), vm(sm, F32), vm((ny,) + sm, F32), vm((nxz,) + sm, F32)]
+        for n in (sum(cols[:4]), cols[4]):
+            scratch += [vm((nz, share, n), F32), vm((nz - 1, share, n), F32)]
+        sm = (8, 384)
+        scratch += [vm(sm, F32), vm(sm, F32), vm((ny,) + sm, F32), vm(sm, F32), vm(sm, F32), vm((nz,) + sm, F32)]
         nc = len(cols)
-        small = ny + nxz - 1
+        small = ny + nz
         scratch += [
-            dma(2, 3), dma(2, 3), dma(2, 3), dma(2, 3), dma(nc), dma(nc), dma(nc, ny - 1), dma(nc, ny - 1),
-            dma(nc, nxz - 1), dma(nc, nxz - 1), dma(2, small), dma(2, small), dma(11), dma(6),
+            dma(2, 3), dma(2, 3), dma(3), dma(3), dma(2, 3), dma(2, 3), dma(nc), dma(nc), dma(nc, ny - 1),
+            dma(nc, ny - 1), dma(nc), dma(nc), dma(2, nz - 1), dma(2, nz - 1), dma(small), dma(small), dma(11), dma(6),
         ]
         anywhere = pl.BlockSpec(memory_space=pl.ANY)
         outs = pl.pallas_call(

time: 69.7 us -> 67.1 us (0.963)
  Pallas kernels: 68.1 us -> 65.6 us
    pallas_call x1, Pallas kernels: 65.6 us -> 63.1 us  [on_device(): pl.pallas_call(functools.partial(kernel, (ny, nx, nz), cols), out_shape=s...]
where the time goes in v4:
time: 67.1 us; the launch traced here: 66.4 us
  Pallas kernels  65.6 us (98%)
  between operations  0.8 us (1%)
    pallas_call x1, Pallas kernels, on_device(): pl.pallas_call(functools.partial(kernel, (ny, nx, nz), cols), out_shape=s...  63.1 us
    pallas_call x1, Pallas kernels, on_device(): pl.pallas_call(hand_over, out_shape=shapes, in_specs=[anywhere] * 6, out_...  2.49 us

profile of v4, /device:TPU:4, one launch (start us, length us, event | category | flops | bytes accessed | tf_op | source)
XLA Modules:
  0.0 66.4 jit_solution(14331541541180600052)
XLA Ops:
  0.6 63.1 %shard_map.154 = (bf16[18,48,512]{2,1,0:T(8,128)(2,1)}, bf16[18,48,512]{2,1,0:T(8,128)(2,1)}, f32[1,512]{1,0:T(1,128)}, f32[8,253]{1,0:T(8,128)}, f32[4,1536]{1,0:T(4,128)}, /*index=5*/f32[4,512]{1,0:T(4,128)}) custom-call(bf16[18,48,512]{2,1,0:T(8,128)(2,1)} %refs_0_.1, s32[18,48]{1,0:T(8,128)} %refs_1_.1, bf16[18,48,512]{2,1,0:T(8,128)(2,1)} %refs_2_.1, ...), custom_call_target="tpu_custom_call" | custom-call | tf_op jit(solution)/shard_map/pallas_call | solution.py:752
  63.7 2.5 %shard_map.155 = (bf16[18,48,512]{2,1,0:T(8,128)(2,1)}, bf16[18,48,512]{2,1,0:T(8,128)(2,1)}, f32[1,512]{1,0:T(1,128)}, f32[8,253]{1,0:T(8,128)}, f32[4,1536]{1,0:T(4,128)}, /*index=5*/f32[4,512]{1,0:T(4,128)}) custom-call(bf16[18,48,512]{2,1,0:T(8,128)(2,1)} %get-tuple-element.18.refs_0_, bf16[18,48,512]{2,1,0:T(8,128)(2,1)} %get-tuple-element.19.refs_1_, ...), custom_call_target="tpu_custom_call" | custom-call | tf_op jit(solution)/shard_map/pallas_call | solution.py:765

commit v5 on v4

--- a/solution.py
+++ b/solution.py
@@ -69,7 +69,7 @@
     halos = [take(5) for _ in range(2)]
     masks = take(3)
     idx = take()
-    tb, bias2, madd, xhat, invd, normed, gz, gm, packed, mixed, ntp, mtp, probs, dp3, gnacc, bacc = take(16)
+    tb, bias2, madd, xhat, invd, normed, gz, gm, packed, mixed, ntp, mtp, probs, probs16, dv, dqk, gnacc, bacc = take(18)
     res, of = take(2)
     ocs, ors, ocr, orr, occ = take(5)
     chunks = [take(8) for _ in range(nchunk)]
@@ -197,8 +197,9 @@
     normed[ROWS:RP, :] = zero_tail
     gz[ROWS:RP, :] = zero_tail
     mixed[ROWS:RP, :] = zero_tail
+    dv[ROWS:RP, :] = zero_tail
     for p in range(PAIRS):
-        dp3[p, ROWS:RP, :] = jnp.zeros((RP - ROWS, 384), BF16)
+        dqk[p, ROWS:RP, :] = jnp.zeros((RP - ROWS, 256), BF16)
     for w in range(nwin):
         win[w, T:TP, :] = jnp.zeros((TP - T, FW), F32)
 
@@ -284,8 +285,11 @@
     def both_heads(v, lo, hi):
         return jnp.concatenate([pad_rows(v * lo, 128), pad_rows(v * hi, 128)], axis=0)
 
-    def own_head(v):
-        return jnp.transpose(jnp.concatenate([v[0:64, 0:128], v[64:128, 128:256]], axis=0))[0:TP]
+    def stack_heads(v, lo, hi):
+        return jnp.concatenate([v * lo, v * hi], axis=0)
+
+    def lanes_to_rows(v):
+        return jnp.concatenate([v[:, 0:128], v[:, 128:256]], axis=0)
 
     def attend(k, carry):
         rows = rows_of(k)
@@ -295,15 +299,15 @@
         for p in range(PAIRS):
             q2 = both_heads(packed[rows, 128 * p : 128 * p + 128], q_lo, q_hi)
             scores.append(nt(packed[rows, C + 128 * p : C + 128 * p + 128], q2) + bias2[p] + add2)
-        mixes = []
         for p in range(PAIRS):
             s = scores[p]
             e = jnp.exp(s - jnp.max(s, axis=0, keepdims=True))
             pr = e * (1.0 / jnp.sum(e, axis=0, keepdims=True))
             probs[k * PAIRS + p] = pr
-            mixes.append(tn(packed[rows, 2 * C + 128 * p : 2 * C + 128 * p + 128], pr.astype(BF16)))
-        for p in range(PAIRS):
-            mixed[rows, 128 * p : 128 * p + 128] = own_head(mixes[p]).astype(BF16)
+            pr16 = pr.astype(BF16)
+            probs16[k * PAIRS + p] = pr16
+            v2 = stack_heads(packed[rows, 2 * C + 128 * p : 2 * C + 128 * p + 128], one_lo, one_hi)
+            mixed[rows, 128 * p : 128 * p + 128] = tn(lanes_to_rows(pr16), v2)[0:TP].astype(BF16)
         return carry
 
     def forward(first, last):
@@ -393,8 +397,8 @@
 
     def chunk_z(c, copies):
         xsend, xrecv, xown = chunks[c][5:8]
-        zsend = groups[0 if c < 4 else 1][0]
-        start = sum(cols[:c]) if c < 4 else 0
+        zsend = groups[0 if c < 5 else 1][0]
+        start = sum(cols[:c]) if c < 5 else 0
         copies[0].wait_recv()
         s = xown[...] + xrecv[...].astype(F32)
         for j in range(nz):
@@ -415,15 +419,17 @@
             s = s + zrecv[i]
         start = 0
         for c in range(nchunk):
-            if (c < 4) != (g == 0):
+            if (c < 5) != (g == 0):
                 continue
+            part = s[:, start : start + cols[c]]
             if c == 0:
-                gproj[...] = s[:, 0:C]
+                gproj[...] = part
+            elif c == 1:
+                gqkv[:, 2 * C : 3 * C] = part
             else:
-                p = c - 1
-                for part in range(3):
-                    at = start + 128 * part
-                    gqkv[:, C * part + 128 * p : C * part + 128 * p + 128] = s[:, at : at + 128]
+                p = c - 2
+                gqkv[:, 128 * p : 128 * p + 128] = part[:, 0:128]
+                gqkv[:, C + 128 * p : C + 128 * p + 128] = part[:, 128:256]
             start += cols[c]
 
     def window_back(o, lane0):
@@ -479,6 +485,16 @@
     st = {}
     st[0] = chunk_start(0, mtp, gz)
 
+    def value_step(k, carry):
+        rows = rows_of(k)
+        for p in range(PAIRS):
+            d2 = both_heads(gm[rows, 128 * p : 128 * p + 128], one_lo, one_hi)
+            dv[rows, 128 * p : 128 * p + 128] = nn(probs16[k * PAIRS + p], d2).astype(BF16)
+        return carry
+
+    lax.fori_loop(0, SLOTS // 3, by_three(value_step), 0)
+    st[1] = chunk_start(1, ntp, dv)
+
     gnacc[...] = nn(mixed[0:ROWS, :], wproj[...])
 
     def updated_step(k, carry):
@@ -489,55 +505,49 @@
 
     lax.fori_loop(0, SLOTS // 3, by_three(updated_step), 0)
     out_copies = [window_back(0, X0), None]
+    gnacc[...] = nt(dv[0:ROWS, :], wqkv[:, 2 * C : 3 * C])
+    st[0] = chunk_y(0, st[0])
 
     def backward(p):
         bacc[p] = jnp.zeros((TP, 256), F32)
 
         def step(i, carry):
             ks = [3 * i + j for j in range(3)]
-            d2s, dps = [], []
+            dps = []
             for k in ks:
                 rows = rows_of(k)
-                d2s.append(both_heads(gm[rows, 128 * p : 128 * p + 128], one_lo, one_hi))
-                dps.append(nt(packed[rows, 2 * C + 128 * p : 2 * C + 128 * p + 128], d2s[-1]))
-            dss, dvs = [], []
+                d2 = both_heads(gm[rows, 128 * p : 128 * p + 128], one_lo, one_hi)
+                dps.append(nt(packed[rows, 2 * C + 128 * p : 2 * C + 128 * p + 128], d2))
+            dss = []
             for j, k in enumerate(ks):
                 pr = probs[k * PAIRS + p]
                 t = pr * dps[j]
                 dss.append(t - pr * jnp.sum(t, axis=0, keepdims=True))
-                dvs.append(nn(pr.astype(BF16), d2s[j]))
             bacc[p] += dss[0] + dss[1] + dss[2]
-            dqs = []
             for j, k in enumerate(ks):
                 rows = rows_of(k)
                 ds = dss[j].astype(BF16)
                 q2 = both_heads(packed[rows, 128 * p : 128 * p + 128], q_lo, q_hi)
-                dqs.append(tn(packed[rows, C + 128 * p : C + 128 * p + 128], ds))
-                dp3[p, rows, 128:256] = nn(ds, q2).astype(BF16)
-                dp3[p, rows, 256:384] = dvs[j].astype(BF16)
-            for j, k in enumerate(ks):
-                dp3[p, rows_of(k), 0:128] = (own_head(dqs[j]) * 0.125).astype(BF16)
+                k2 = stack_heads(packed[rows, C + 128 * p : C + 128 * p + 128], q_lo, q_hi)
+                dqk[p, rows, 0:128] = tn(lanes_to_rows(ds), k2)[0:TP].astype(BF16)
+                dqk[p, rows, 128:256] = nn(ds, q2).astype(BF16)
             return carry
 
         lax.fori_loop(0, SLOTS // 3, step, 0)
 
-    def weight_pair(p):
-        return jnp.concatenate([wqkv[:, C * part + 128 * p : C * part + 128 * p + 128] for part in range(3)], axis=1)
-
     def grad_normed(p):
-        g = nt(dp3[p, 0:ROWS, :], weight_pair(p))
-        gnacc[...] = g if p == 0 else gnacc[...] + g
+        weight = jnp.concatenate([wqkv[:, C * i + 128 * p : C * i + 128 * p + 128] for i in range(2)], axis=1)
+        gnacc[...] += nt(dqk[p, 0:ROWS, :], weight)
 
     for p in range(PAIRS):
         backward(p)
-        st[p + 1] = chunk_start(p + 1, ntp, dp3.at[p])
-        st[p] = chunk_y(p, st[p])
+        st[p + 2] = chunk_start(p + 2, ntp, dqk.at[p])
+        st[p + 1] = chunk_y(p + 1, st[p + 1])
+        st[p] = chunk_x(p, st[p])
         if p >= 1:
-            st[p - 1] = chunk_x(p - 1, st[p - 1])
-        if p >= 2:
-            chunk_z(p - 2, st[p - 2])
+            chunk_z(p - 1, st[p - 1])
         grad_normed(p)
-    st[4] = chunk_y(4, st[4])
+    st[5] = chunk_y(5, st[5])
 
     def norm_back(k, total):
         w = idx[k]
@@ -553,7 +563,7 @@
 
     gsum = lax.fori_loop(0, SLOTS // 3, by_three(norm_back), jnp.zeros((1, C), F32))
     out_copies[1] = window_back(1, D0)
-    st[3] = chunk_x(3, st[3])
+    st[4] = chunk_x(4, st[4])
 
     stacked = jnp.concatenate([bacc[h // 2, :, 128 * (h % 2) : 128 * (h % 2) + 128] for h in range(HEADS)], axis=0)
     by_place = sum(nn(v, self_[...]) for v in pieces(stacked, 2))
@@ -567,16 +577,16 @@
     for j in range(4):
         sm[j : j + 1, 256:384] = gsum[:, 128 * j : 128 * j + 128]
     copy = send(sm, smc, ss.at[0], sr.at[0], partner)
-    chunk_z(2, st[2])
     chunk_z(3, st[3])
+    chunk_z(4, st[4])
     group0 = group_send(0)
-    st[4] = chunk_x(4, st[4])
+    st[5] = chunk_x(5, st[5])
     copy.wait_recv()
     smy[y] = sm[...] + smc[...]
     copies = [send(smy.at[y], smy.at[y], ss.at[d], sr.at[d], ypeer[d - 1]) for d in range(1, ny)]
     finish(0, out_copies[0], upd)
     stores[0].start()
-    chunk_z(4, st[4])
+    chunk_z(5, st[5])
     group1 = group_send(1)
     for copy in copies:
         copy.wait_recv()
@@ -657,7 +667,7 @@
     half = C // 2
     ysz = half // ny
     share = ysz // nxz
-    cols = [C] + [384] * PAIRS
+    cols = [C, C] + [256] * PAIRS
     lat_dev, lon_dev = 18, 48
     nwin = 12
     vm = pltpu.VMEM
@@ -716,7 +726,9 @@
             vm((C, RP), BF16),
             vm((C, RP), BF16),
             vm((SLOTS * PAIRS, TP, 256), F32),
-            vm((PAIRS, RP, 384), BF16),
+            vm((SLOTS * PAIRS, TP, 256), BF16),
+            vm((RP, C), BF16),
+            vm((PAIRS, RP, 256), BF16),
             vm((ROWS, C), F32),
             vm((PAIRS, TP, 256), F32),
             vm((SLOTS, TP, C), F32),
@@ -738,7 +750,7 @@
                 vm((ysz // 2, n), BF16),
                 vm((ysz // 2, n), F32),
             ]
-        for n in (sum(cols[:4]), cols[4]):
+        for n in (sum(cols[:5]), cols[5]):
             scratch += [vm((nz, share, n), F32), vm((nz - 1, share, n), F32)]
         sm = (8, 384)
         scratch += [vm(sm, F32), vm(sm, F32), vm((ny,) + sm, F32), vm(sm, F32), vm(sm, F32), vm((nz,) + sm, F32)]

time: 67.1 us -> 72.8 us (1.085)
  the two profiles are of different devices: /device:TPU:4 before, /device:TPU:6 now
where the time goes in v5:
time: 72.8 us; the launch traced here: 72.6 us
  Pallas kernels  71.8 us (99%)
  between operations  0.8 us (1%)
    pallas_call x1, Pallas kernels, on_device(): pl.pallas_call(functools.partial(kernel, (ny, nx, nz), cols), out_shape=s...  69.4 us
    pallas_call x1, Pallas kernels, on_device(): pl.pallas_call(hand_over, out_shape=shapes, in_specs=[anywhere] * 6, out_...  2.49 us

profile of v5, /device:TPU:6, one launch (start us, length us, event | category | flops | bytes accessed | tf_op | source)
XLA Modules:
  0.0 72.6 jit_solution(11011340664369447834)
XLA Ops:
  0.6 69.4 %shard_map.154 = (bf16[18,48,512]{2,1,0:T(8,128)(2,1)}, bf16[18,48,512]{2,1,0:T(8,128)(2,1)}, f32[1,512]{1,0:T(1,128)}, f32[8,253]{1,0:T(8,128)}, f32[4,1536]{1,0:T(4,128)}, /*index=5*/f32[4,512]{1,0:T(4,128)}) custom-call(bf16[18,48,512]{2,1,0:T(8,128)(2,1)} %refs_0_.1, s32[18,48]{1,0:T(8,128)} %refs_1_.1, bf16[18,48,512]{2,1,0:T(8,128)(2,1)} %refs_2_.1, ...), custom_call_target="tpu_custom_call" | custom-call | tf_op jit(solution)/shard_map/pallas_call | solution.py:764
  70.0 2.5 %shard_map.155 = (bf16[18,48,512]{2,1,0:T(8,128)(2,1)}, bf16[18,48,512]{2,1,0:T(8,128)(2,1)}, f32[1,512]{1,0:T(1,128)}, f32[8,253]{1,0:T(8,128)}, f32[4,1536]{1,0:T(4,128)}, /*index=5*/f32[4,512]{1,0:T(4,128)}) custom-call(bf16[18,48,512]{2,1,0:T(8,128)(2,1)} %get-tuple-element.18.refs_0_, bf16[18,48,512]{2,1,0:T(8,128)(2,1)} %get-tuple-element.19.refs_1_, ...), custom_call_target="tpu_custom_call" | custom-call | tf_op jit(solution)/shard_map/pallas_call | solution.py:777

commit v6 on v4

--- a/solution.py
+++ b/solution.py
@@ -287,30 +287,30 @@
     def own_head(v):
         return jnp.transpose(jnp.concatenate([v[0:64, 0:128], v[64:128, 128:256]], axis=0))[0:TP]
 
-    def attend(k, carry):
-        rows = rows_of(k)
-        add = madd[k]
-        add2 = jnp.concatenate([add, add], axis=1)
+    def attend(i, carry):
+        chains = [(3 * i + j, p) for j in range(3) for p in range(PAIRS)]
         scores = []
-        for p in range(PAIRS):
+        for k, p in chains:
+            rows = rows_of(k)
             q2 = both_heads(packed[rows, 128 * p : 128 * p + 128], q_lo, q_hi)
+            add = madd[k]
+            add2 = jnp.concatenate([add, add], axis=1)
             scores.append(nt(packed[rows, C + 128 * p : C + 128 * p + 128], q2) + bias2[p] + add2)
         mixes = []
-        for p in range(PAIRS):
-            s = scores[p]
+        for (k, p), s in zip(chains, scores):
             e = jnp.exp(s - jnp.max(s, axis=0, keepdims=True))
             pr = e * (1.0 / jnp.sum(e, axis=0, keepdims=True))
             probs[k * PAIRS + p] = pr
-            mixes.append(tn(packed[rows, 2 * C + 128 * p : 2 * C + 128 * p + 128], pr.astype(BF16)))
-        for p in range(PAIRS):
-            mixed[rows, 128 * p : 128 * p + 128] = own_head(mixes[p]).astype(BF16)
+            mixes.append(tn(packed[rows_of(k), 2 * C + 128 * p : 2 * C + 128 * p + 128], pr.astype(BF16)))
+        for (k, p), mix in zip(chains, mixes):
+            mixed[rows_of(k), 128 * p : 128 * p + 128] = own_head(mix).astype(BF16)
         return carry
 
     def forward(first, last):
         lax.fori_loop(first // 3, last // 3, by_three(ln_step), 0)
         rows = slice(first * TP, last * TP)
         packed[rows, :] = nn(normed[rows, :], wqkv[...]).astype(BF16)
-        lax.fori_loop(first, last, attend, 0)
+        lax.fori_loop(first // 3, last // 3, attend, 0)
 
     for w in inner:
         cut(w, slice(0, FW))
@@ -491,35 +491,29 @@
     out_copies = [window_back(0, X0), None]
 
     def backward(p):
-        bacc[p] = jnp.zeros((TP, 256), F32)
-
-        def step(i, carry):
-            ks = [3 * i + j for j in range(3)]
-            d2s, dps = [], []
-            for k in ks:
-                rows = rows_of(k)
-                d2s.append(both_heads(gm[rows, 128 * p : 128 * p + 128], one_lo, one_hi))
-                dps.append(nt(packed[rows, 2 * C + 128 * p : 2 * C + 128 * p + 128], d2s[-1]))
-            dss, dvs = [], []
-            for j, k in enumerate(ks):
-                pr = probs[k * PAIRS + p]
-                t = pr * dps[j]
-                dss.append(t - pr * jnp.sum(t, axis=0, keepdims=True))
-                dvs.append(nn(pr.astype(BF16), d2s[j]))
-            bacc[p] += dss[0] + dss[1] + dss[2]
-            dqs = []
-            for j, k in enumerate(ks):
-                rows = rows_of(k)
-                ds = dss[j].astype(BF16)
-                q2 = both_heads(packed[rows, 128 * p : 128 * p + 128], q_lo, q_hi)
-                dqs.append(tn(packed[rows, C + 128 * p : C + 128 * p + 128], ds))
-                dp3[p, rows, 128:256] = nn(ds, q2).astype(BF16)
-                dp3[p, rows, 256:384] = dvs[j].astype(BF16)
-            for j, k in enumerate(ks):
-                dp3[p, rows_of(k), 0:128] = (own_head(dqs[j]) * 0.125).astype(BF16)
-            return carry
-
-        lax.fori_loop(0, SLOTS // 3, step, 0)
+        ks = list(range(SLOTS))
+        d2s, dps = [], []
+        for k in ks:
+            rows = slice(TP * k, TP * k + TP)
+            d2s.append(both_heads(gm[rows, 128 * p : 128 * p + 128], one_lo, one_hi))
+            dps.append(nt(packed[rows, 2 * C + 128 * p : 2 * C + 128 * p + 128], d2s[-1]))
+        dss, dvs = [], []
+        for k in ks:
+            pr = probs[k * PAIRS + p]
+            t = pr * dps[k]
+            dss.append(t - pr * jnp.sum(t, axis=0, keepdims=True))
+            dvs.append(nn(pr.astype(BF16), d2s[k]))
+        bacc[p] = functools.reduce(lambda a, b: a + b, dss)
+        dqs = []
+        for k in ks:
+            rows = slice(TP * k, TP * k + TP)
+            ds = dss[k].astype(BF16)
+            q2 = both_heads(packed[rows, 128 * p : 128 * p + 128], q_lo, q_hi)
+            dqs.append(tn(packed[rows, C + 128 * p : C + 128 * p + 128], ds))
+            dp3[p, rows, 128:256] = nn(ds, q2).astype(BF16)
+            dp3[p, rows, 256:384] = dvs[k].astype(BF16)
+        for k in ks:
+            dp3[p, TP * k : TP * k + TP, 0:128] = (own_head(dqs[k]) * 0.125).astype(BF16)
 
     def weight_pair(p):
         return jnp.concatenate([wqkv[:, C * part + 128 * p : C * part + 128 * p + 128] for part in range(3)], axis=1)

time: 67.1 us -> 65.2 us (0.972)
  Pallas kernels: 65.6 us -> 64.3 us
    pallas_call x1, Pallas kernels: 63.1 us -> 61.8 us  [on_device(): pl.pallas_call(functools.partial(kernel, (ny, nx, nz), cols), out_shape=s...]
where the time goes in v6:
time: 65.2 us; the launch traced here: 65.1 us
  Pallas kernels  64.3 us (99%)
  between operations  0.8 us (1%)
    pallas_call x1, Pallas kernels, on_device(): pl.pallas_call(functools.partial(kernel, (ny, nx, nz), cols), out_shape=s...  61.8 us
    pallas_call x1, Pallas kernels, on_device(): pl.pallas_call(hand_over, out_shape=shapes, in_specs=[anywhere] * 6, out_...  2.49 us

profile of v6, /device:TPU:4, one launch (start us, length us, event | category | flops | bytes accessed | tf_op | source)
XLA Modules:
  0.0 65.1 jit_solution(8623222273777154442)
XLA Ops:
  0.6 61.8 %shard_map.154 = (bf16[18,48,512]{2,1,0:T(8,128)(2,1)}, bf16[18,48,512]{2,1,0:T(8,128)(2,1)}, f32[1,512]{1,0:T(1,128)}, f32[8,253]{1,0:T(8,128)}, f32[4,1536]{1,0:T(4,128)}, /*index=5*/f32[4,512]{1,0:T(4,128)}) custom-call(bf16[18,48,512]{2,1,0:T(8,128)(2,1)} %refs_0_.1, s32[18,48]{1,0:T(8,128)} %refs_1_.1, bf16[18,48,512]{2,1,0:T(8,128)(2,1)} %refs_2_.1, ...), custom_call_target="tpu_custom_call" | custom-call | tf_op jit(solution)/shard_map/pallas_call | solution.py:746
  62.4 2.5 %shard_map.155 = (bf16[18,48,512]{2,1,0:T(8,128)(2,1)}, bf16[18,48,512]{2,1,0:T(8,128)(2,1)}, f32[1,512]{1,0:T(1,128)}, f32[8,253]{1,0:T(8,128)}, f32[4,1536]{1,0:T(4,128)}, /*index=5*/f32[4,512]{1,0:T(4,128)}) custom-call(bf16[18,48,512]{2,1,0:T(8,128)(2,1)} %get-tuple-element.18.refs_0_, bf16[18,48,512]{2,1,0:T(8,128)(2,1)} %get-tuple-element.19.refs_1_, ...), custom_call_target="tpu_custom_call" | custom-call | tf_op jit(solution)/shard_map/pallas_call | solution.py:759

commit v7 on v6

--- a/solution.py
+++ b/solution.py
@@ -71,9 +71,8 @@
     idx = take()
     tb, bias2, madd, xhat, invd, normed, gz, gm, packed, mixed, ntp, mtp, probs, dp3, gnacc, bacc = take(16)
     res, of = take(2)
-    ocs, ors, ocr, orr, occ = take(5)
-    chunks = [take(8) for _ in range(nchunk)]
-    groups = [take(2) for _ in range(2)]
+    ocs, ors, occs, ocr, orr, occ = take(6)
+    chunks = [take(11) for _ in range(nchunk)]
     sums = take(6)
     hs, hr, ms, mr, os_, or_, as_, ar, ys, yr, xs, xr, zs, zr, ss, sr = take(16)
     ins, outs = take(2)
@@ -392,39 +391,32 @@
         return [send(xsend, xrecv, xs.at[c], xr.at[c], xpeer)]
 
     def chunk_z(c, copies):
-        xsend, xrecv, xown = chunks[c][5:8]
-        zsend = groups[0 if c < 4 else 1][0]
-        start = sum(cols[:c]) if c < 4 else 0
+        xsend, xrecv, xown, zown, zsend, zrecv = chunks[c][5:11]
         copies[0].wait_recv()
         s = xown[...] + xrecv[...].astype(F32)
+        blocks = cols[c] // 128
         for j in range(nz):
-            zsend[j, :, start : start + cols[c]] = s[share * j : share * j + share]
-
-    def group_send(g):
-        zsend, zrecv = groups[g]
+            part = s[share * j : share * j + share]
+            piece = jnp.concatenate([part[:, 128 * min(q, blocks - 1) :][:, 0:128] for q in range(4)], axis=0)
+            zown[j] = piece
+            zsend[j] = piece.astype(BF16)
         return [
-            send(zsend.at[(z + d) % nz], zrecv.at[d - 1], zs.at[g, d - 1], zr.at[g, d - 1], zpeer[d - 1])
+            send(zsend.at[(z + d) % nz], zrecv.at[d - 1], zs.at[c, d - 1], zr.at[c, d - 1], zpeer[d - 1])
             for d in range(1, nz)
         ]
 
-    def group_end(g, copies):
-        zsend, zrecv = groups[g]
-        s = zsend[z]
+    def chunk_end(c, copies):
+        zown, zsend, zrecv = chunks[c][8:11]
+        s = zown[z]
         for i, copy in enumerate(copies):
             copy.wait_recv()
-            s = s + zrecv[i]
-        start = 0
-        for c in range(nchunk):
-            if (c < 4) != (g == 0):
-                continue
+            s = s + zrecv[i].astype(F32)
+        for q in range(cols[c] // 128):
+            block = s[share * q : share * q + share]
             if c == 0:
-                gproj[...] = s[:, 0:C]
+                gproj[:, 128 * q : 128 * q + 128] = block
             else:
-                p = c - 1
-                for part in range(3):
-                    at = start + 128 * part
-                    gqkv[:, C * part + 128 * p : C * part + 128 * p + 128] = s[:, at : at + 128]
-            start += cols[c]
+                gqkv[:, C * q + 128 * (c - 1) : C * q + 128 * c] = block
 
     def window_back(o, lane0):
         def place_window(w):
@@ -439,16 +431,20 @@
 
         for w in range(wcols - 1, nwin, wcols):
             place_window(w)
-        colf[0 : 6 * HALF_LAT, 0:C] = jnp.zeros((6 * HALF_LAT, C), F32)
+        colf[88:96, 0:C] = jnp.zeros((8, C), F32)
         for r in range(HALF_LAT, lat_dev):
-            colf[6 * r : 6 * r + 6, 0:C] = of[o, r, lon_dev : lon_dev + HALF_LON, :]
-        ocs[o, 0:112] = colf[0:112, 0:C].astype(BF16)
+            at = 6 * (r - HALF_LAT)
+            colf[at : at + 6, 0:C] = of[o, r, lon_dev : lon_dev + HALF_LON, :]
+        ocs[o] = colf[0:96, 0:C].astype(BF16)
         for r in range(HALF_LAT):
             colf[6 * r : 6 * r + 6, 0:C] = of[o, lat_dev + r, lon_dev : lon_dev + HALF_LON, :]
-        ocs[o, 112:144] = colf[0:32, 0:C].astype(BF16)
+        colf[8:16, C : C + 128] = jnp.zeros((8, 128), F32)
+        for j in range(8):
+            colf[j : j + 1, C : C + 128] = colf[16 + j // 4 : 17 + j // 4, 128 * (j % 4) : 128 * (j % 4) + 128]
+        occs[o] = colf[0:16, 0 : C + 128].astype(BF16)
         copies = [
-            send(ocs.at[o, 0:112], ocr.at[o], os_.at[o, 0], or_.at[o, 0], forth[0]),
-            send(ocs.at[o, 112:144], occ.at[o], os_.at[o, 2], or_.at[o, 2], forth[2]),
+            send(ocs.at[o], ocr.at[o], os_.at[o, 0], or_.at[o, 0], forth[0]),
+            send(occs.at[o], occ.at[o], os_.at[o, 2], or_.at[o, 2], forth[2]),
         ]
         for w in range(nwin - wcols, nwin - 1):
             place_window(w)
@@ -465,11 +461,14 @@
         for r in range(HALF_LAT):
             of[o, r, 0:lon_dev, :] = orr[o, r].astype(F32)
         copies[0].wait_recv()
-        colf[0:112, 0:C] = ocr[o].astype(F32)
+        colf[0:96, 0:C] = ocr[o].astype(F32)
         for r in range(HALF_LAT, lat_dev):
-            of[o, r, 0:HALF_LON, :] = colf[6 * r : 6 * r + 6, 0:C]
+            at = 6 * (r - HALF_LAT)
+            of[o, r, 0:HALF_LON, :] = colf[at : at + 6, 0:C]
         copies[2].wait_recv()
-        colf[0:32, 0:C] = occ[o].astype(F32)
+        colf[0:16, 0 : C + 128] = occ[o].astype(F32)
+        for j in range(8):
+            colf[16 + j // 4 : 17 + j // 4, 128 * (j % 4) : 128 * (j % 4) + 128] = colf[j : j + 1, C : C + 128]
         for r in range(HALF_LAT):
             of[o, r, 0:HALF_LON, :] = colf[6 * r : 6 * r + 6, 0:C]
         for r in range(lat_dev):
@@ -522,16 +521,14 @@
         g = nt(dp3[p, 0:ROWS, :], weight_pair(p))
         gnacc[...] = g if p == 0 else gnacc[...] + g
 
+    st[0] = chunk_y(0, st[0])
     for p in range(PAIRS):
         backward(p)
+        st[p] = chunk_x(p, st[p])
         st[p + 1] = chunk_start(p + 1, ntp, dp3.at[p])
-        st[p] = chunk_y(p, st[p])
-        if p >= 1:
-            st[p - 1] = chunk_x(p - 1, st[p - 1])
-        if p >= 2:
-            chunk_z(p - 2, st[p - 2])
         grad_normed(p)
-    st[4] = chunk_y(4, st[4])
+        st[p] = chunk_z(p, st[p])
+        st[p + 1] = chunk_y(p + 1, st[p + 1])
 
     def norm_back(k, total):
         w = idx[k]
@@ -547,7 +544,6 @@
 
     gsum = lax.fori_loop(0, SLOTS // 3, by_three(norm_back), jnp.zeros((1, C), F32))
     out_copies[1] = window_back(1, D0)
-    st[3] = chunk_x(3, st[3])
 
     stacked = jnp.concatenate([bacc[h // 2, :, 128 * (h % 2) : 128 * (h % 2) + 128] for h in range(HEADS)], axis=0)
     by_place = sum(nn(v, self_[...]) for v in pieces(stacked, 2))
@@ -561,17 +557,13 @@
     for j in range(4):
         sm[j : j + 1, 256:384] = gsum[:, 128 * j : 128 * j + 128]
     copy = send(sm, smc, ss.at[0], sr.at[0], partner)
-    chunk_z(2, st[2])
-    chunk_z(3, st[3])
-    group0 = group_send(0)
     st[4] = chunk_x(4, st[4])
     copy.wait_recv()
     smy[y] = sm[...] + smc[...]
     copies = [send(smy.at[y], smy.at[y], ss.at[d], sr.at[d], ypeer[d - 1]) for d in range(1, ny)]
     finish(0, out_copies[0], upd)
     stores[0].start()
-    chunk_z(4, st[4])
-    group1 = group_send(1)
+    st[4] = chunk_z(4, st[4])
     for copy in copies:
         copy.wait_recv()
     acc = smy[0]
@@ -579,13 +571,14 @@
         acc = acc + smy[j]
     sma[...] = acc
     copy = send(sma, smx, ss.at[ny], sr.at[ny], xpeer)
-    group_end(0, group0)
+    for c in range(nchunk - 1):
+        chunk_end(c, st[c])
     copy.wait_recv()
     smz[z] = sma[...] + smx[...]
     copies = [send(smz.at[z], smz.at[z], ss.at[ny + d], sr.at[ny + d], zpeer[d - 1]) for d in range(1, nz)]
     finish(1, out_copies[1], gin)
     stores[1].start()
-    group_end(1, group1)
+    chunk_end(nchunk - 1, st[nchunk - 1])
     for copy in copies:
         copy.wait_recv()
     acc = smz[0]
@@ -715,11 +708,12 @@
             vm((PAIRS, TP, 256), F32),
             vm((SLOTS, TP, C), F32),
             vm((2, lat_dev + 3, 56, C), F32),
-            vm((2, 144, C), BF16),
+            vm((2, 96, C), BF16),
             vm((2, 3, lon_dev, C), BF16),
-            vm((2, 112, C), BF16),
+            vm((2, 16, C + 128), BF16),
+            vm((2, 96, C), BF16),
             vm((2, 3, lon_dev, C), BF16),
-            vm((2, 32, C), BF16),
+            vm((2, 16, C + 128), BF16),
         ]
         for n in cols:
             scratch += [
@@ -731,16 +725,17 @@
                 vm((ysz // 2, n), BF16),
                 vm((ysz // 2, n), BF16),
                 vm((ysz // 2, n), F32),
+                vm((nz, 4 * share, 128), F32),
+                vm((nz, 4 * share, 128), BF16),
+                vm((nz - 1, 4 * share, 128), BF16),
             ]
-        for n in (sum(cols[:4]), cols[4]):
-            scratch += [vm((nz, share, n), F32), vm((nz - 1, share, n), F32)]
         sm = (8, 384)
         scratch += [vm(sm, F32), vm(sm, F32), vm((ny,) + sm, F32), vm(sm, F32), vm(sm, F32), vm((nz,) + sm, F32)]
         nc = len(cols)
         small = ny + nz
         scratch += [
             dma(2, 3), dma(2, 3), dma(3), dma(3), dma(2, 3), dma(2, 3), dma(nc), dma(nc), dma(nc, ny - 1),
-            dma(nc, ny - 1), dma(nc), dma(nc), dma(2, nz - 1), dma(2, nz - 1), dma(small), dma(small), dma(11), dma(6),
+            dma(nc, ny - 1), dma(nc), dma(nc), dma(nc, nz - 1), dma(nc, nz - 1), dma(small), dma(small), dma(11), dma(6),
         ]
         anywhere = pl.BlockSpec(memory_space=pl.ANY)
         outs = pl.pallas_call(

time: 65.2 us -> 83.3 us (1.28); the launches traced: 65.1 us -> 81.8 us
  Pallas kernels: 64.3 us -> 81 us
    pallas_call x1, Pallas kernels: 61.8 us -> 78.5 us  [on_device(): pl.pallas_call(functools.partial(kernel, (ny, nx, nz), cols), out_shape=s...]
where the time goes in v7:
time: 83.3 us; the launch traced here: 81.8 us
  Pallas kernels  81 us (97%)
    pallas_call x1, Pallas kernels, on_device(): pl.pallas_call(functools.partial(kernel, (ny, nx, nz), cols), out_shape=s...  78.5 us
    pallas_call x1, Pallas kernels, on_device(): pl.pallas_call(hand_over, out_shape=shapes, in_specs=[anywhere] * 6, out_...  2.49 us

profile of v7, /device:TPU:4, one launch (start us, length us, event | category | flops | bytes accessed | tf_op | source)
XLA Modules:
  0.0 81.8 jit_solution(824438807103129877)
XLA Ops:
  0.6 78.5 %shard_map.154 = (bf16[18,48,512]{2,1,0:T(8,128)(2,1)}, bf16[18,48,512]{2,1,0:T(8,128)(2,1)}, f32[1,512]{1,0:T(1,128)}, f32[8,253]{1,0:T(8,128)}, f32[4,1536]{1,0:T(4,128)}, /*index=5*/f32[4,512]{1,0:T(4,128)}) custom-call(bf16[18,48,512]{2,1,0:T(8,128)(2,1)} %refs_0_.1, s32[18,48]{1,0:T(8,128)} %refs_1_.1, bf16[18,48,512]{2,1,0:T(8,128)(2,1)} %refs_2_.1, ...), custom_call_target="tpu_custom_call" | custom-call | tf_op jit(solution)/shard_map/pallas_call | solution.py:741
  79.1 2.5 %shard_map.155 = (bf16[18,48,512]{2,1,0:T(8,128)(2,1)}, bf16[18,48,512]{2,1,0:T(8,128)(2,1)}, f32[1,512]{1,0:T(1,128)}, f32[8,253]{1,0:T(8,128)}, f32[4,1536]{1,0:T(4,128)}, /*index=5*/f32[4,512]{1,0:T(4,128)}) custom-call(bf16[18,48,512]{2,1,0:T(8,128)(2,1)} %get-tuple-element.18.refs_0_, bf16[18,48,512]{2,1,0:T(8,128)(2,1)} %get-tuple-element.19.refs_1_, ...), custom_call_target="tpu_custom_call" | custom-call | tf_op jit(solution)/shard_map/pallas_call | solution.py:754

commit v8 on v7

--- a/solution.py
+++ b/solution.py
@@ -25,6 +25,7 @@
 RP = 768
 REL = 253
 X0, M0, D0, FW = 0, 512, 640, 1152
+GROUPS = ((0, 1, 2), (3, 4))
 EARLY = 3
 EPS = 1e-5
 
@@ -69,10 +70,11 @@
     halos = [take(5) for _ in range(2)]
     masks = take(3)
     idx = take()
-    tb, bias2, madd, xhat, invd, normed, gz, gm, packed, mixed, ntp, mtp, probs, dp3, gnacc, bacc = take(16)
+    tb, bias2, madd, xhat, invd, normed, gz, gm, packed, mixed, ntp, mtp, probs, dp3, gnacc, bacc, wperm, gacc = take(18)
     res, of = take(2)
     ocs, ors, occs, ocr, orr, occ = take(6)
-    chunks = [take(11) for _ in range(nchunk)]
+    chunks = [take(8) for _ in range(nchunk)]
+    groups = [take(3) for _ in range(len(GROUPS))]
     sums = take(6)
     hs, hr, ms, mr, os_, or_, as_, ar, ys, yr, xs, xr, zs, zr, ss, sr = take(16)
     ins, outs = take(2)
@@ -192,6 +194,10 @@
     for p in range(PAIRS):
         bias2[p] = whole_bias[:, 256 * p : 256 * p + 256]
 
+    wperm[...] = nn(perm[...], wqkv[...]).astype(BF16)
+    gacc[...] = jnp.zeros_like(gacc)
+    for g in range(len(GROUPS)):
+        groups[g][0][...] = jnp.zeros_like(groups[g][0])
     zero_tail = jnp.zeros((RP - ROWS, C), BF16)
     normed[ROWS:RP, :] = zero_tail
     gz[ROWS:RP, :] = zero_tail
@@ -347,77 +353,6 @@
         slot_window(k, list(enumerate(place)))
     forward(EARLY, SLOTS)
 
-    halo_land(1, dlanes, dcopies)
-    for w in outer:
-        cut(w, dlanes)
-    lax.fori_loop(0, SLOTS // 3, by_three(dy_step), 0)
-    gm[...] = nt(gz[0:ROWS, :], wproj[...]).astype(BF16)
-    ntp[...] = nt(perm[...], normed[...]).astype(BF16)
-
-    def chunk_start(c, lhs, rhs):
-        asend, arecv, own = chunks[c][0:3]
-        right = rhs[...]
-        other = pl.multiple_of((1 - core) * half, half)
-        mine = pl.multiple_of(core * half, half)
-        asend[...] = nn(lhs[pl.ds(other, half), :], right).astype(BF16)
-        copy = send(asend, arecv, as_.at[c], ar.at[c], partner)
-        own[...] = nn(lhs[pl.ds(mine, half), :], right)
-        return [copy]
-
-    def chunk_y(c, copies):
-        asend, arecv, own, ysend, yrecv = chunks[c][0:5]
-        copies[0].wait_recv()
-        s = own[...] + arecv[...].astype(F32)
-        own[...] = s
-        ysend[...] = s.astype(BF16)
-        out = []
-        for d in range(1, ny):
-            start = pl.multiple_of(((y + d) % ny) * ysz, ysz)
-            out.append(
-                send(ysend.at[pl.ds(start, ysz)], yrecv.at[d - 1], ys.at[c, d - 1], yr.at[c, d - 1], ypeer[d - 1])
-            )
-        return out
-
-    def chunk_x(c, copies):
-        own, ysend, yrecv, xsend, xrecv, xown = chunks[c][2:8]
-        s = own[pl.ds(pl.multiple_of(y * ysz, ysz), ysz), :]
-        for d in range(1, ny):
-            copies[d - 1].wait_recv()
-            s = s + yrecv[d - 1].astype(F32)
-        top, low_half = s[0 : ysz // 2], s[ysz // 2 : ysz]
-        first = xh == 0
-        xsend[...] = jnp.where(first, low_half, top).astype(BF16)
-        xown[...] = jnp.where(first, top, low_half)
-        return [send(xsend, xrecv, xs.at[c], xr.at[c], xpeer)]
-
-    def chunk_z(c, copies):
-        xsend, xrecv, xown, zown, zsend, zrecv = chunks[c][5:11]
-        copies[0].wait_recv()
-        s = xown[...] + xrecv[...].astype(F32)
-        blocks = cols[c] // 128
-        for j in range(nz):
-            part = s[share * j : share * j + share]
-            piece = jnp.concatenate([part[:, 128 * min(q, blocks - 1) :][:, 0:128] for q in range(4)], axis=0)
-            zown[j] = piece
-            zsend[j] = piece.astype(BF16)
-        return [
-            send(zsend.at[(z + d) % nz], zrecv.at[d - 1], zs.at[c, d - 1], zr.at[c, d - 1], zpeer[d - 1])
-            for d in range(1, nz)
-        ]
-
-    def chunk_end(c, copies):
-        zown, zsend, zrecv = chunks[c][8:11]
-        s = zown[z]
-        for i, copy in enumerate(copies):
-            copy.wait_recv()
-            s = s + zrecv[i].astype(F32)
-        for q in range(cols[c] // 128):
-            block = s[share * q : share * q + share]
-            if c == 0:
-                gproj[:, 128 * q : 128 * q + 128] = block
-            else:
-                gqkv[:, C * q + 128 * (c - 1) : C * q + 128 * c] = block
-
     def window_back(o, lane0):
         def place_window(w):
             wr, wc = w // wcols, w % wcols
@@ -474,10 +409,6 @@
         for r in range(lat_dev):
             out[r] = of[o, r, 0:lon_dev, :].astype(BF16)
 
-    mtp[...] = nt(perm[...], mixed[...]).astype(BF16)
-    st = {}
-    st[0] = chunk_start(0, mtp, gz)
-
     gnacc[...] = nn(mixed[0:ROWS, :], wproj[...])
 
     def updated_step(k, carry):
@@ -487,7 +418,104 @@
         return carry
 
     lax.fori_loop(0, SLOTS // 3, by_three(updated_step), 0)
-    out_copies = [window_back(0, X0), None]
+    out_copies = [window_back(0, X0)]
+
+    halo_land(1, dlanes, dcopies)
+    for w in outer:
+        cut(w, dlanes)
+    lax.fori_loop(0, SLOTS // 3, by_three(dy_step), 0)
+    gm[...] = nt(gz[0:ROWS, :], wproj[...]).astype(BF16)
+    ntp[...] = nt(perm[...], normed[...]).astype(BF16)
+
+    def gain_part(c, rows, product):
+        weight = [wperm[rows, C * i + 128 * (c - 1) : C * i + 128 * c].astype(F32) for i in range(3)]
+        gacc[rows, :] += sum(product[:, 128 * i : 128 * i + 128] * weight[i] for i in range(3))
+
+    def chunk_start(c, lhs, rhs):
+        asend, arecv, own = chunks[c][0:3]
+        right = rhs[...]
+        other = pl.ds(pl.multiple_of((1 - core) * half, half), half)
+        mine = pl.ds(pl.multiple_of(core * half, half), half)
+        product = nn(lhs[other, :], right)
+        asend[...] = product.astype(BF16)
+        copy = send(asend, arecv, as_.at[c], ar.at[c], partner)
+        if c > 0:
+            gain_part(c, other, product)
+        product = nn(lhs[mine, :], right)
+        own[...] = product
+        if c > 0:
+            gain_part(c, mine, product)
+        return [copy]
+
+    def chunk_y(c, copies):
+        asend, arecv, own, ysend, yrecv = chunks[c][0:5]
+        copies[0].wait_recv()
+        s = own[...] + arecv[...].astype(F32)
+        own[...] = s
+        ysend[...] = s.astype(BF16)
+        out = []
+        for d in range(1, ny):
+            start = pl.multiple_of(((y + d) % ny) * ysz, ysz)
+            out.append(
+                send(ysend.at[pl.ds(start, ysz)], yrecv.at[d - 1], ys.at[c, d - 1], yr.at[c, d - 1], ypeer[d - 1])
+            )
+        return out
+
+    def chunk_x(c, copies):
+        own, ysend, yrecv, xsend, xrecv, xown = chunks[c][2:8]
+        s = own[pl.ds(pl.multiple_of(y * ysz, ysz), ysz), :]
+        for d in range(1, ny):
+            copies[d - 1].wait_recv()
+            s = s + yrecv[d - 1].astype(F32)
+        top, low_half = s[0 : ysz // 2], s[ysz // 2 : ysz]
+        first = xh == 0
+        xsend[...] = jnp.where(first, low_half, top).astype(BF16)
+        xown[...] = jnp.where(first, top, low_half)
+        return [send(xsend, xrecv, xs.at[c], xr.at[c], xpeer)]
+
+    def blocks_before(c):
+        g = next(i for i, members in enumerate(GROUPS) if c in members)
+        return g, sum(cols[m] // 128 for m in GROUPS[g] if m < c)
+
+    def chunk_z(c, copies):
+        xsend, xrecv, xown = chunks[c][5:8]
+        g, first = blocks_before(c)
+        zown = groups[g][0]
+        copies[0].wait_recv()
+        s = xown[...] + xrecv[...].astype(F32)
+        for j in range(nz):
+            part = s[share * j : share * j + share]
+            for q in range(cols[c] // 128):
+                at = share * (first + q)
+                zown[j, at : at + share, :] = part[:, 128 * q : 128 * q + 128]
+
+    def group_send(g):
+        zown, zsend, zrecv = groups[g]
+        zsend[...] = zown[...].astype(BF16)
+        return [
+            send(zsend.at[(z + d) % nz], zrecv.at[d - 1], zs.at[g, d - 1], zr.at[g, d - 1], zpeer[d - 1])
+            for d in range(1, nz)
+        ]
+
+    def group_end(g, copies):
+        zown, zsend, zrecv = groups[g]
+        s = zown[z]
+        for i, copy in enumerate(copies):
+            copy.wait_recv()
+            s = s + zrecv[i].astype(F32)
+        for c in GROUPS[g]:
+            first = blocks_before(c)[1]
+            for q in range(cols[c] // 128):
+                at = share * (first + q)
+                block = s[at : at + share]
+                if c == 0:
+                    gproj[:, 128 * q : 128 * q + 128] = block
+                else:
+                    gqkv[:, C * q + 128 * (c - 1) : C * q + 128 * c] = block
+
+    mtp[...] = nt(perm[...], mixed[...]).astype(BF16)
+    st = {}
+    st[0] = chunk_start(0, mtp, gz)
 
     def backward(p):
         ks = list(range(SLOTS))
@@ -517,20 +545,42 @@
     def weight_pair(p):
         return jnp.concatenate([wqkv[:, C * part + 128 * p : C * part + 128 * p + 128] for part in range(3)], axis=1)
 
-    def grad_normed(p):
-        g = nt(dp3[p, 0:ROWS, :], weight_pair(p))
-        gnacc[...] = g if p == 0 else gnacc[...] + g
-
-    st[0] = chunk_y(0, st[0])
+    def grad_normed(p, q):
+        return nt(dp3[p, 0:ROWS, :], weight_pair(p)) + nt(dp3[q, 0:ROWS, :], weight_pair(q))
+
     for p in range(PAIRS):
         backward(p)
-        st[p] = chunk_x(p, st[p])
         st[p + 1] = chunk_start(p + 1, ntp, dp3.at[p])
-        grad_normed(p)
-        st[p] = chunk_z(p, st[p])
-        st[p + 1] = chunk_y(p + 1, st[p + 1])
-
-    def norm_back(k, total):
+        st[p] = chunk_y(p, st[p])
+        if p >= 2:
+            st[p - 2] = chunk_x(p - 2, st[p - 2])
+        if p >= 3:
+            chunk_z(p - 3, st[p - 3])
+
+    stacked = jnp.concatenate([bacc[h // 2, :, 128 * (h % 2) : 128 * (h % 2) + 128] for h in range(HEADS)], axis=0)
+    by_place = sum(nn(v, self_[...]) for v in pieces(stacked, 2))
+    by_place = jnp.concatenate([by_place[TP * h : TP * h + TP] for h in range(HEADS)], axis=1)
+    spread = sum(nn(selrt[:, 0:TP], v) for v in pieces(by_place, 2))
+    for h in range(HEADS):
+        wide = jnp.concatenate([spread[:, 128 * h : 128 * h + 128], jnp.zeros((128, 128), F32)], axis=1)
+        sums[0][h : h + 1, 0:256] = jnp.sum(pltpu.roll(wide, 0, 1, stride=1, stride_axis=0), axis=0, keepdims=True)
+    gain_row = sum(tn(v, perm[...]) for v in pieces(gacc[...], 2))
+    gain_row = jnp.sum(gain_row, axis=0, keepdims=True) / gain
+    sm, smc, smy, sma, smx, smz = sums
+    sm[4:8, 256:384] = jnp.zeros((4, 128), F32)
+    for j in range(4):
+        sm[j : j + 1, 256:384] = gain_row[:, 128 * j : 128 * j + 128]
+    copy = send(sm, smc, ss.at[0], sr.at[0], partner)
+
+    gnacc[...] = grad_normed(0, 1)
+    st[4] = chunk_y(4, st[4])
+    st[2] = chunk_x(2, st[2])
+    gnacc[...] += grad_normed(2, 3)
+    copy.wait_recv()
+    smy[y] = sm[...] + smc[...]
+    copies = [send(smy.at[y], smy.at[y], ss.at[d], sr.at[d], ypeer[d - 1]) for d in range(1, ny)]
+
+    def norm_back(k, carry):
         w = idx[k]
         rows = rows_of(k)
         gn = gnacc[rows, :]
@@ -540,30 +590,12 @@
         mid = g - jnp.mean(g, axis=1, keepdims=True) - hat * jnp.mean(prod, axis=1, keepdims=True)
         inv = jnp.concatenate([invd[rows, :]] * 4, axis=1)
         res[k] = win[w, :, D0 : D0 + C] + inv * mid
-        return total + jnp.sum(gn * hat, axis=0, keepdims=True)
-
-    gsum = lax.fori_loop(0, SLOTS // 3, by_three(norm_back), jnp.zeros((1, C), F32))
-    out_copies[1] = window_back(1, D0)
-
-    stacked = jnp.concatenate([bacc[h // 2, :, 128 * (h % 2) : 128 * (h % 2) + 128] for h in range(HEADS)], axis=0)
-    by_place = sum(nn(v, self_[...]) for v in pieces(stacked, 2))
-    by_place = jnp.concatenate([by_place[TP * h : TP * h + TP] for h in range(HEADS)], axis=1)
-    spread = sum(nn(selrt[:, 0:TP], v) for v in pieces(by_place, 2))
-    for h in range(HEADS):
-        wide = jnp.concatenate([spread[:, 128 * h : 128 * h + 128], jnp.zeros((128, 128), F32)], axis=1)
-        sums[0][h : h + 1, 0:256] = jnp.sum(pltpu.roll(wide, 0, 1, stride=1, stride_axis=0), axis=0, keepdims=True)
-    sm, smc, smy, sma, smx, smz = sums
-    sm[4:8, 256:384] = jnp.zeros((4, 128), F32)
-    for j in range(4):
-        sm[j : j + 1, 256:384] = gsum[:, 128 * j : 128 * j + 128]
-    copy = send(sm, smc, ss.at[0], sr.at[0], partner)
-    st[4] = chunk_x(4, st[4])
-    copy.wait_recv()
-    smy[y] = sm[...] + smc[...]
-    copies = [send(smy.at[y], smy.at[y], ss.at[d], sr.at[d], ypeer[d - 1]) for d in range(1, ny)]
-    finish(0, out_copies[0], upd)
-    stores[0].start()
-    st[4] = chunk_z(4, st[4])
+        return carry
+
+    lax.fori_loop(0, SLOTS // 3, by_three(norm_back), 0)
+    chunk_z(1, st[1])
+    st[3] = chunk_x(3, st[3])
+    out_copies.append(window_back(1, D0))
     for copy in copies:
         copy.wait_recv()
     acc = smy[0]
@@ -571,14 +603,20 @@
         acc = acc + smy[j]
     sma[...] = acc
     copy = send(sma, smx, ss.at[ny], sr.at[ny], xpeer)
-    for c in range(nchunk - 1):
-        chunk_end(c, st[c])
+    st[4] = chunk_x(4, st[4])
+    chunk_z(2, st[2])
+    group0 = group_send(0)
+    finish(0, out_copies[0], upd)
+    stores[0].start()
     copy.wait_recv()
     smz[z] = sma[...] + smx[...]
     copies = [send(smz.at[z], smz.at[z], ss.at[ny + d], sr.at[ny + d], zpeer[d - 1]) for d in range(1, nz)]
+    chunk_z(3, st[3])
+    chunk_z(4, st[4])
+    group1 = group_send(1)
     finish(1, out_copies[1], gin)
     stores[1].start()
-    chunk_end(nchunk - 1, st[nchunk - 1])
+    group_end(0, group0)
     for copy in copies:
         copy.wait_recv()
     acc = smz[0]
@@ -587,6 +625,7 @@
     bias_out[...] = acc[:, 0:REL]
     for j in range(4):
         gain_out[:, 128 * j : 128 * j + 128] = acc[j : j + 1, 256:384]
+    group_end(1, group1)
     for store in stores[2:]:
         store.start()
     for copy in sends:
@@ -706,6 +745,8 @@
             vm((PAIRS, RP, 384), BF16),
             vm((ROWS, C), F32),
             vm((PAIRS, TP, 256), F32),
+            vm((C, 3 * C), BF16),
+            vm((C, 128), F32),
             vm((SLOTS, TP, C), F32),
             vm((2, lat_dev + 3, 56, C), F32),
             vm((2, 96, C), BF16),
@@ -725,10 +766,10 @@
                 vm((ysz // 2, n), BF16),
                 vm((ysz // 2, n), BF16),
                 vm((ysz // 2, n), F32),
-                vm((nz, 4 * share, 128), F32),
-                vm((nz, 4 * share, 128), BF16),
-                vm((nz - 1, 4 * share, 128), BF16),
             ]
+        for members in GROUPS:
+            rows = -(-share * sum(cols[c] // 128 for c in members) // 16) * 16
+            scratch += [vm((nz, rows, 128), F32), vm((nz, rows, 128), BF16), vm((nz - 1, rows, 128), BF16)]
         sm = (8, 384)
         scratch += [vm(sm, F32), vm(sm, F32), vm((ny,) + sm, F32), vm(sm, F32), vm(sm, F32), vm((nz,) + sm, F32)]
         nc = len(cols)

time: 83.3 us -> 57.3 us (0.69); the launches traced: 81.8 us -> 57.1 us
  Pallas kernels: 81 us -> 56.3 us
    pallas_call x1, Pallas kernels: 78.5 us -> 53.8 us  [on_device(): pl.pallas_call(functools.partial(kernel, (ny, nx, nz), cols), out_shape=s...]
where the time goes in v8:
time: 57.3 us; the launch traced here: 57.1 us
  Pallas kernels  56.3 us (98%)
  between operations  0.8 us (1%)
    pallas_call x1, Pallas kernels, on_device(): pl.pallas_call(functools.partial(kernel, (ny, nx, nz), cols), out_shape=s...  53.8 us
    pallas_call x1, Pallas kernels, on_device(): pl.pallas_call(hand_over, out_shape=shapes, in_specs=[anywhere] * 6, out_...  2.49 us

profile of v8, /device:TPU:4, one launch (start us, length us, event | category | flops | bytes accessed | tf_op | source)
XLA Modules:
  0.0 57.1 jit_solution(15898383530194673045)
XLA Ops:
  0.6 53.8 %shard_map.154 = (bf16[18,48,512]{2,1,0:T(8,128)(2,1)}, bf16[18,48,512]{2,1,0:T(8,128)(2,1)}, f32[1,512]{1,0:T(1,128)}, f32[8,253]{1,0:T(8,128)}, f32[4,1536]{1,0:T(4,128)}, /*index=5*/f32[4,512]{1,0:T(4,128)}) custom-call(bf16[18,48,512]{2,1,0:T(8,128)(2,1)} %refs_0_.1, s32[18,48]{1,0:T(8,128)} %refs_1_.1, bf16[18,48,512]{2,1,0:T(8,128)(2,1)} %refs_2_.1, ...), custom_call_target="tpu_custom_call" | custom-call | tf_op jit(solution)/shard_map/pallas_call | solution.py:782
  54.4 2.5 %shard_map.155 = (bf16[18,48,512]{2,1,0:T(8,128)(2,1)}, bf16[18,48,512]{2,1,0:T(8,128)(2,1)}, f32[1,512]{1,0:T(1,128)}, f32[8,253]{1,0:T(8,128)}, f32[4,1536]{1,0:T(4,128)}, /*index=5*/f32[4,512]{1,0:T(4,128)}) custom-call(bf16[18,48,512]{2,1,0:T(8,128)(2,1)} %get-tuple-element.18.refs_0_, bf16[18,48,512]{2,1,0:T(8,128)(2,1)} %get-tuple-element.19.refs_1_, ...), custom_call_target="tpu_custom_call" | custom-call | tf_op jit(solution)/shard_map/pallas_call | solution.py:795

commit v9 on v8

--- a/solution.py
+++ b/solution.py
@@ -25,7 +25,8 @@
 RP = 768
 REL = 253
 X0, M0, D0, FW = 0, 512, 640, 1152
-GROUPS = ((0, 1, 2), (3, 4))
+GROUPS = ((0, 1, 2),)
+LAST = (3, 4)
 EARLY = 3
 EPS = 1e-5
 
@@ -67,7 +68,7 @@
     staged = take(6)
     upd, gin, gain_out, bias_out, gqkv, gproj = staged
     frame, win, colf = take(3)
-    halos = [take(5) for _ in range(2)]
+    halos = [take(4) for _ in range(2)]
     masks = take(3)
     idx = take()
     tb, bias2, madd, xhat, invd, normed, gz, gm, packed, mixed, ntp, mtp, probs, dp3, gnacc, bacc, wperm, gacc = take(18)
@@ -75,8 +76,9 @@
     ocs, ors, occs, ocr, orr, occ = take(6)
     chunks = [take(8) for _ in range(nchunk)]
     groups = [take(3) for _ in range(len(GROUPS))]
-    sums = take(6)
-    hs, hr, ms, mr, os_, or_, as_, ar, ys, yr, xs, xr, zs, zr, ss, sr = take(16)
+    lastown, lastsend, lastrecv = take(3)
+    sums = take(4)
+    hs, hr, ms, mr, os_, or_, as_, ar, ys, yr, xs, xr, zs, zr, ss, sr, ls, lr = take(18)
     ins, outs = take(2)
 
     lon = lax.axis_index("lon")
@@ -91,17 +93,24 @@
     ypeer = [dev(((y + d) % ny) * nx + xh, lat) for d in range(1, ny)]
     xpeer = dev(y * nx + (1 - xh), lat)
     zpeer = [dev(lon, ((z + d) % nz) * 2 + core) for d in range(1, nz)]
+    crossy = [dev(((y + d) % ny) * nx + xh, z * 2 + (1 - core)) for d in range(1, ny)]
+    crossz = [dev(y * nx + (1 - xh), ((z + d) % nz) * 2 + core) for d in range(1, nz)]
     west, east = (lon + nlon - 1) % nlon, (lon + 1) % nlon
     north, south = (lat + nlat - 1) % nlat, (lat + 1) % nlat
     back = [dev(west, lat), dev(lon, north), dev(west, north)]
     forth = [dev(east, lat), dev(lon, south), dev(east, south)]
 
     barrier = pltpu.get_barrier_semaphore()
-    everyone = [partner, xpeer] + ypeer + zpeer + back + forth
+    everyone = [partner, xpeer] + ypeer + zpeer + crossy + crossz + back + forth
     for d in everyone:
         pl.semaphore_signal(barrier, inc=1, device_id=d, device_id_type=MESH)
 
-    loads = [pltpu.make_async_copy(a, b, ins.at[i]) for i, (a, b) in enumerate(zip(given, held))]
+    loads = [pltpu.make_async_copy(a, b, ins.at[i]) for i, (a, b) in enumerate(zip(given, held)) if i != 8]
+    for p in range(PAIRS):
+        for i in range(3):
+            src = given[8].at[:, C * i + 128 * p : C * i + 128 * p + 128]
+            dst = wqkv.at[:, 384 * p + 128 * i : 384 * p + 128 * i + 128]
+            loads.append(pltpu.make_async_copy(src, dst, ins.at[11 + 3 * p + i]))
     for load in loads:
         load.start()
 
@@ -122,28 +131,23 @@
     def spread_mask(ref):
         return tn(ref[...].astype(F32), pick)
 
-    loads[1].wait()
-    sea = spread_mask(mask_ref)
     colf[96:112, :] = jnp.zeros((16, FW), F32)
 
-    def halo_pack(h, lanes):
-        colsend, colrecv, rowsend, rowrecv, cornrecv = halos[h]
+    def halo_send(h, block, source):
+        colsend, colrecv, rowrecv, cornrecv = halos[h]
         for r in range(lat_dev):
-            colf[6 * r : 6 * r + 6, lanes] = frame[r, 0:HALF_LON, lanes]
-        colsend[...] = colf[:, lanes].astype(BF16)
-        for r in range(HALF_LAT):
-            rowsend[r] = frame[r, 0:lon_dev, lanes].astype(BF16)
-
-    def halo_send(h):
-        colsend, colrecv, rowsend, rowrecv, cornrecv = halos[h]
+            colf[6 * r : 6 * r + 6, 0:C] = block[r, 0:16, :].astype(F32)[0:HALF_LON]
+        colsend[...] = colf[:, 0:C].astype(BF16)
+        if h == 0:
+            pl.semaphore_wait(barrier, len(everyone))
         return [
             send(colsend, colrecv, hs.at[h, 0], hr.at[h, 0], back[0]),
-            send(rowsend, rowrecv, hs.at[h, 1], hr.at[h, 1], back[1]),
+            send(source.at[0:HALF_LAT], rowrecv, hs.at[h, 1], hr.at[h, 1], back[1]),
             send(colsend.at[0:32], cornrecv, hs.at[h, 2], hr.at[h, 2], back[2]),
         ]
 
     def halo_land(h, lanes, copies):
-        colsend, colrecv, rowsend, rowrecv, cornrecv = halos[h]
+        colsend, colrecv, rowrecv, cornrecv = halos[h]
         copies[1].wait_recv()
         for r in range(HALF_LAT):
             frame[lat_dev + r, 0:lon_dev, lanes] = rowrecv[r].astype(F32)
@@ -158,18 +162,16 @@
 
     xlanes, dlanes = slice(X0, X0 + C), slice(D0, D0 + C)
     loads[0].wait()
+    xcopies = halo_send(0, x_ref, given[0])
+    loads[1].wait()
+    mcopies = [send(mask_ref, masks[i], ms.at[i], mr.at[i], back[i]) for i in range(3)]
+    loads[2].wait()
+    dcopies = halo_send(1, dy_ref, given[2])
+    sea = spread_mask(mask_ref)
     for r in range(lat_dev):
         frame[r, 0:lon_dev, X0 : X0 + C] = x_ref[r].astype(F32)
         frame[r, 0:lon_dev, M0 : M0 + 128] = sea[:, 128 * r : 128 * r + 128]
-    halo_pack(0, xlanes)
-    pl.semaphore_wait(barrier, len(everyone))
-    mcopies = [send(mask_ref, masks[i], ms.at[i], mr.at[i], back[i]) for i in range(3)]
-    xcopies = halo_send(0)
-    loads[2].wait()
-    for r in range(lat_dev):
         frame[r, 0:lon_dev, D0 : D0 + C] = dy_ref[r].astype(F32)
-    halo_pack(1, dlanes)
-    dcopies = halo_send(1)
 
     def pieces(v, n):
         out = []
@@ -180,8 +182,8 @@
                 v = v - part.astype(F32)
         return out
 
-    for i in range(3, 11):
-        loads[i].wait()
+    for load in loads[3:]:
+        load.wait()
     tb[...] = jnp.zeros_like(tb)
     tb[:, 0:REL] = table[...]
     shifted = []
@@ -202,8 +204,7 @@
     normed[ROWS:RP, :] = zero_tail
     gz[ROWS:RP, :] = zero_tail
     mixed[ROWS:RP, :] = zero_tail
-    for p in range(PAIRS):
-        dp3[p, ROWS:RP, :] = jnp.zeros((RP - ROWS, 384), BF16)
+    dp3[ROWS:RP, :] = jnp.zeros((RP - ROWS, 3 * C), BF16)
     for w in range(nwin):
         win[w, T:TP, :] = jnp.zeros((TP - T, FW), F32)
 
@@ -297,16 +298,16 @@
         scores = []
         for k, p in chains:
             rows = rows_of(k)
-            q2 = both_heads(packed[rows, 128 * p : 128 * p + 128], q_lo, q_hi)
+            q2 = both_heads(packed[rows, 384 * p : 384 * p + 128], q_lo, q_hi)
             add = madd[k]
             add2 = jnp.concatenate([add, add], axis=1)
-            scores.append(nt(packed[rows, C + 128 * p : C + 128 * p + 128], q2) + bias2[p] + add2)
+            scores.append(nt(packed[rows, 384 * p + 128 : 384 * p + 256], q2) + bias2[p] + add2)
         mixes = []
         for (k, p), s in zip(chains, scores):
             e = jnp.exp(s - jnp.max(s, axis=0, keepdims=True))
             pr = e * (1.0 / jnp.sum(e, axis=0, keepdims=True))
             probs[k * PAIRS + p] = pr
-            mixes.append(tn(packed[rows_of(k), 2 * C + 128 * p : 2 * C + 128 * p + 128], pr.astype(BF16)))
+            mixes.append(tn(packed[rows_of(k), 384 * p + 256 : 384 * p + 384], pr.astype(BF16)))
         for (k, p), mix in zip(chains, mixes):
             mixed[rows_of(k), 128 * p : 128 * p + 128] = own_head(mix).astype(BF16)
         return carry
@@ -428,12 +429,12 @@
     ntp[...] = nt(perm[...], normed[...]).astype(BF16)
 
     def gain_part(c, rows, product):
-        weight = [wperm[rows, C * i + 128 * (c - 1) : C * i + 128 * c].astype(F32) for i in range(3)]
+        weight = [wperm[rows, 384 * (c - 1) + 128 * i : 384 * (c - 1) + 128 * i + 128].astype(F32) for i in range(3)]
         gacc[rows, :] += sum(product[:, 128 * i : 128 * i + 128] * weight[i] for i in range(3))
 
     def chunk_start(c, lhs, rhs):
         asend, arecv, own = chunks[c][0:3]
-        right = rhs[...]
+        right = rhs[...] if c == 0 else rhs[:, 384 * (c - 1) : 384 * c]
         other = pl.ds(pl.multiple_of((1 - core) * half, half), half)
         mine = pl.ds(pl.multiple_of(core * half, half), half)
         product = nn(lhs[other, :], right)
@@ -496,6 +497,45 @@
             send(zsend.at[(z + d) % nz], zrecv.at[d - 1], zs.at[g, d - 1], zr.at[g, d - 1], zpeer[d - 1])
             for d in range(1, nz)
         ]
+
+    def last_send(copies):
+        lastown[...] = jnp.zeros_like(lastown)
+        first = 0
+        for c in LAST:
+            own, ysend, yrecv = chunks[c][2:5]
+            s = own[pl.ds(pl.multiple_of(y * ysz, ysz), ysz), :]
+            for d in range(1, ny):
+                copies[c][d - 1].wait_recv()
+                s = s + yrecv[d - 1].astype(F32)
+            for j in range(nxz):
+                part = s[share * j : share * j + share]
+                for q in range(cols[c] // 128):
+                    at = share * (first + q)
+                    lastown[j, at : at + share, :] = part[:, 128 * q : 128 * q + 128]
+            first += cols[c] // 128
+        lastsend[...] = lastown[...].astype(BF16)
+        out = []
+        for a in range(nx):
+            for d in range(nz):
+                if (a, d) == (0, 0):
+                    continue
+                to = (xpeer if d == 0 else crossz[d - 1]) if a else zpeer[d - 1]
+                j = ((xh + a) % nx) * nz + (z + d) % nz
+                i = a * nz + d - 1
+                out.append(send(lastsend.at[j], lastrecv.at[i], ls.at[i], lr.at[i], to))
+        return out
+
+    def last_end(copies):
+        s = lastown[xh * nz + z]
+        for i, copy in enumerate(copies):
+            copy.wait_recv()
+            s = s + lastrecv[i].astype(F32)
+        first = 0
+        for c in LAST:
+            for q in range(cols[c] // 128):
+                at = share * (first + q)
+                gqkv[:, C * q + 128 * (c - 1) : C * q + 128 * c] = s[at : at + share]
+            first += cols[c] // 128
 
     def group_end(g, copies):
         zown, zsend, zrecv = groups[g]
@@ -523,7 +563,7 @@
         for k in ks:
             rows = slice(TP * k, TP * k + TP)
             d2s.append(both_heads(gm[rows, 128 * p : 128 * p + 128], one_lo, one_hi))
-            dps.append(nt(packed[rows, 2 * C + 128 * p : 2 * C + 128 * p + 128], d2s[-1]))
+            dps.append(nt(packed[rows, 384 * p + 256 : 384 * p + 384], d2s[-1]))
         dss, dvs = [], []
         for k in ks:
             pr = probs[k * PAIRS + p]
@@ -535,27 +575,19 @@
         for k in ks:
             rows = slice(TP * k, TP * k + TP)
             ds = dss[k].astype(BF16)
-            q2 = both_heads(packed[rows, 128 * p : 128 * p + 128], q_lo, q_hi)
-            dqs.append(tn(packed[rows, C + 128 * p : C + 128 * p + 128], ds))
-            dp3[p, rows, 128:256] = nn(ds, q2).astype(BF16)
-            dp3[p, rows, 256:384] = dvs[k].astype(BF16)
+            q2 = both_heads(packed[rows, 384 * p : 384 * p + 128], q_lo, q_hi)
+            dqs.append(tn(packed[rows, 384 * p + 128 : 384 * p + 256], ds))
+            dp3[rows, 384 * p + 128 : 384 * p + 256] = nn(ds, q2).astype(BF16)
+            dp3[rows, 384 * p + 256 : 384 * p + 384] = dvs[k].astype(BF16)
         for k in ks:
-            dp3[p, TP * k : TP * k + TP, 0:128] = (own_head(dqs[k]) * 0.125).astype(BF16)
-
-    def weight_pair(p):
-        return jnp.concatenate([wqkv[:, C * part + 128 * p : C * part + 128 * p + 128] for part in range(3)], axis=1)
-
-    def grad_normed(p, q):
-        return nt(dp3[p, 0:ROWS, :], weight_pair(p)) + nt(dp3[q, 0:ROWS, :], weight_pair(q))
+            dp3[TP * k : TP * k + TP, 384 * p : 384 * p + 128] = (own_head(dqs[k]) * 0.125).astype(BF16)
 
     for p in range(PAIRS):
         backward(p)
-        st[p + 1] = chunk_start(p + 1, ntp, dp3.at[p])
+        st[p + 1] = chunk_start(p + 1, ntp, dp3)
         st[p] = chunk_y(p, st[p])
         if p >= 2:
             st[p - 2] = chunk_x(p - 2, st[p - 2])
-        if p >= 3:
-            chunk_z(p - 3, st[p - 3])
 
     stacked = jnp.concatenate([bacc[h // 2, :, 128 * (h % 2) : 128 * (h % 2) + 128] for h in range(HEADS)], axis=0)
     by_place = sum(nn(v, self_[...]) for v in pieces(stacked, 2))
@@ -563,22 +595,23 @@
     spread = sum(nn(selrt[:, 0:TP], v) for v in pieces(by_place, 2))
     for h in range(HEADS):
         wide = jnp.concatenate([spread[:, 128 * h : 128 * h + 128], jnp.zeros((128, 128), F32)], axis=1)
-        sums[0][h : h + 1, 0:256] = jnp.sum(pltpu.roll(wide, 0, 1, stride=1, stride_axis=0), axis=0, keepdims=True)
+        sums[0][core * ny + y, h : h + 1, 0:256] = jnp.sum(pltpu.roll(wide, 0, 1, stride=1, stride_axis=0), axis=0, keepdims=True)
     gain_row = sum(tn(v, perm[...]) for v in pieces(gacc[...], 2))
     gain_row = jnp.sum(gain_row, axis=0, keepdims=True) / gain
-    sm, smc, smy, sma, smx, smz = sums
+    smy, sma, smx, smz = sums
+    slot = core * ny + y
+    sm = smy.at[slot]
     sm[4:8, 256:384] = jnp.zeros((4, 128), F32)
     for j in range(4):
         sm[j : j + 1, 256:384] = gain_row[:, 128 * j : 128 * j + 128]
-    copy = send(sm, smc, ss.at[0], sr.at[0], partner)
-
-    gnacc[...] = grad_normed(0, 1)
+    copies = [
+        send(sm, sm, ss.at[i], sr.at[i], to) for i, to in enumerate([partner] + ypeer + crossy)
+    ]
     st[4] = chunk_y(4, st[4])
     st[2] = chunk_x(2, st[2])
-    gnacc[...] += grad_normed(2, 3)
-    copy.wait_recv()
-    smy[y] = sm[...] + smc[...]
-    copies = [send(smy.at[y], smy.at[y], ss.at[d], sr.at[d], ypeer[d - 1]) for d in range(1, ny)]
+    for part in range(2):
+        rows = slice(part * ROWS // 2, (part + 1) * ROWS // 2)
+        gnacc[rows, :] = nt(dp3[rows, :], wqkv[...])
 
     def norm_back(k, carry):
         w = idx[k]
@@ -593,30 +626,29 @@
         return carry
 
     lax.fori_loop(0, SLOTS // 3, by_three(norm_back), 0)
-    chunk_z(1, st[1])
-    st[3] = chunk_x(3, st[3])
     out_copies.append(window_back(1, D0))
     for copy in copies:
         copy.wait_recv()
     acc = smy[0]
-    for j in range(1, ny):
+    for j in range(1, 2 * ny):
         acc = acc + smy[j]
     sma[...] = acc
-    copy = send(sma, smx, ss.at[ny], sr.at[ny], xpeer)
-    st[4] = chunk_x(4, st[4])
-    chunk_z(2, st[2])
+    copy = send(sma, smx, ss.at[2 * ny - 1], sr.at[2 * ny - 1], xpeer)
+    last = last_send(st)
+    for c in GROUPS[0]:
+        chunk_z(c, st[c])
     group0 = group_send(0)
     finish(0, out_copies[0], upd)
     stores[0].start()
     copy.wait_recv()
     smz[z] = sma[...] + smx[...]
-    copies = [send(smz.at[z], smz.at[z], ss.at[ny + d], sr.at[ny + d], zpeer[d - 1]) for d in range(1, nz)]
-    chunk_z(3, st[3])
-    chunk_z(4, st[4])
-    group1 = group_send(1)
+    copies = [
+        send(smz.at[z], smz.at[z], ss.at[2 * ny + d - 1], sr.at[2 * ny + d - 1], zpeer[d - 1]) for d in range(1, nz)
+    ]
+    group_end(0, group0)
     finish(1, out_copies[1], gin)
     stores[1].start()
-    group_end(0, group0)
+    last_end(last)
     for copy in copies:
         copy.wait_recv()
     acc = smz[0]
@@ -625,7 +657,6 @@
     bias_out[...] = acc[:, 0:REL]
     for j in range(4):
         gain_out[:, 128 * j : 128 * j + 128] = acc[j : j + 1, 256:384]
-    group_end(1, group1)
     for store in stores[2:]:
         store.start()
     for copy in sends:
@@ -723,7 +754,6 @@
                 vm((112, wide), BF16),
                 vm((112, wide), BF16),
                 vm((3, lon_dev, wide), BF16),
-                vm((3, lon_dev, wide), BF16),
                 vm((32, wide), BF16),
             ]
         scratch += [vm((lat_dev, lon_dev), jnp.int32)] * 3
@@ -742,7 +772,7 @@
             vm((C, RP), BF16),
             vm((C, RP), BF16),
             vm((SLOTS * PAIRS, TP, 256), F32),
-            vm((PAIRS, RP, 384), BF16),
+            vm((RP, 3 * C), BF16),
             vm((ROWS, C), F32),
             vm((PAIRS, TP, 256), F32),
             vm((C, 3 * C), BF16),
@@ -770,13 +800,15 @@
         for members in GROUPS:
             rows = -(-share * sum(cols[c] // 128 for c in members) // 16) * 16
             scratch += [vm((nz, rows, 128), F32), vm((nz, rows, 128), BF16), vm((nz - 1, rows, 128), BF16)]
+        rows = -(-share * sum(cols[c] // 128 for c in LAST) // 16) * 16
+        scratch += [vm((nxz, rows, 128), F32), vm((nxz, rows, 128), BF16), vm((nxz - 1, rows, 128), BF16)]
         sm = (8, 384)
-        scratch += [vm(sm, F32), vm(sm, F32), vm((ny,) + sm, F32), vm(sm, F32), vm(sm, F32), vm((nz,) + sm, F32)]
+        scratch += [vm((2 * ny,) + sm, F32), vm(sm, F32), vm(sm, F32), vm((nz,) + sm, F32)]
         nc = len(cols)
-        small = ny + nz
+        small = 2 * ny + nz
         scratch += [
             dma(2, 3), dma(2, 3), dma(3), dma(3), dma(2, 3), dma(2, 3), dma(nc), dma(nc), dma(nc, ny - 1),
-            dma(nc, ny - 1), dma(nc), dma(nc), dma(nc, nz - 1), dma(nc, nz - 1), dma(small), dma(small), dma(11), dma(6),
+            dma(nc, ny - 1), dma(nc), dma(nc), dma(nc, nz - 1), dma(nc, nz - 1), dma(small), dma(small), dma(nxz - 1), dma(nxz - 1), dma(23), dma(6),
         ]
         anywhere = pl.BlockSpec(memory_space=pl.ANY)
         outs = pl.pallas_call(

time: 57.3 us -> 58.4 us (1.019)
  the two profiles are of different devices: /device:TPU:4 before, /device:TPU:1 now
where the time goes in v9:
time: 58.4 us; the launch traced here: 58.3 us
  Pallas kernels  57.5 us (98%)
  between operations  0.8 us (1%)
    pallas_call x1, Pallas kernels, on_device(): pl.pallas_call(functools.partial(kernel, (ny, nx, nz), cols), out_shape=s...  55 us
    pallas_call x1, Pallas kernels, on_device(): pl.pallas_call(hand_over, out_shape=shapes, in_specs=[anywhere] * 6, out_...  2.49 us

profile of v9, /device:TPU:1, one launch (start us, length us, event | category | flops | bytes accessed | tf_op | source)
XLA Modules:
  0.0 58.3 jit_solution(4540131527760936923)
XLA Ops:
  0.6 55.0 %shard_map.154 = (bf16[18,48,512]{2,1,0:T(8,128)(2,1)}, bf16[18,48,512]{2,1,0:T(8,128)(2,1)}, f32[1,512]{1,0:T(1,128)}, f32[8,253]{1,0:T(8,128)}, f32[4,1536]{1,0:T(4,128)}, /*index=5*/f32[4,512]{1,0:T(4,128)}) custom-call(bf16[18,48,512]{2,1,0:T(8,128)(2,1)} %refs_0_.1, s32[18,48]{1,0:T(8,128)} %refs_1_.1, bf16[18,48,512]{2,1,0:T(8,128)(2,1)} %refs_2_.1, ...), custom_call_target="tpu_custom_call" | custom-call | tf_op jit(solution)/shard_map/pallas_call | solution.py:814
  55.6 2.5 %shard_map.155 = (bf16[18,48,512]{2,1,0:T(8,128)(2,1)}, bf16[18,48,512]{2,1,0:T(8,128)(2,1)}, f32[1,512]{1,0:T(1,128)}, f32[8,253]{1,0:T(8,128)}, f32[4,1536]{1,0:T(4,128)}, /*index=5*/f32[4,512]{1,0:T(4,128)}) custom-call(bf16[18,48,512]{2,1,0:T(8,128)(2,1)} %get-tuple-element.18.refs_0_, bf16[18,48,512]{2,1,0:T(8,128)(2,1)} %get-tuple-element.19.refs_1_, ...), custom_call_target="tpu_custom_call" | custom-call | tf_op jit(solution)/shard_map/pallas_call | solution.py:827

commit v10 on v9

--- a/solution.py
+++ b/solution.py
@@ -25,8 +25,7 @@
 RP = 768
 REL = 253
 X0, M0, D0, FW = 0, 512, 640, 1152
-GROUPS = ((0, 1, 2),)
-LAST = (3, 4)
+GROUPS = ((0, 1, 2), (3, 4))
 EARLY = 3
 EPS = 1e-5
 
@@ -71,14 +70,13 @@
     halos = [take(4) for _ in range(2)]
     masks = take(3)
     idx = take()
-    tb, bias2, madd, xhat, invd, normed, gz, gm, packed, mixed, ntp, mtp, probs, dp3, gnacc, bacc, wperm, gacc = take(18)
+    tb, bias2, madd, xhat, invd, normed, gz, gm, packed, mixed, ntp, mtp, probs, dp3, gnacc, bacc = take(16)
     res, of = take(2)
     ocs, ors, occs, ocr, orr, occ = take(6)
     chunks = [take(8) for _ in range(nchunk)]
     groups = [take(3) for _ in range(len(GROUPS))]
-    lastown, lastsend, lastrecv = take(3)
     sums = take(4)
-    hs, hr, ms, mr, os_, or_, as_, ar, ys, yr, xs, xr, zs, zr, ss, sr, ls, lr = take(18)
+    hs, hr, ms, mr, os_, or_, as_, ar, ys, yr, xs, xr, zs, zr, ss, sr = take(16)
     ins, outs = take(2)
 
     lon = lax.axis_index("lon")
@@ -94,14 +92,13 @@
     xpeer = dev(y * nx + (1 - xh), lat)
     zpeer = [dev(lon, ((z + d) % nz) * 2 + core) for d in range(1, nz)]
     crossy = [dev(((y + d) % ny) * nx + xh, z * 2 + (1 - core)) for d in range(1, ny)]
-    crossz = [dev(y * nx + (1 - xh), ((z + d) % nz) * 2 + core) for d in range(1, nz)]
     west, east = (lon + nlon - 1) % nlon, (lon + 1) % nlon
     north, south = (lat + nlat - 1) % nlat, (lat + 1) % nlat
     back = [dev(west, lat), dev(lon, north), dev(west, north)]
     forth = [dev(east, lat), dev(lon, south), dev(east, south)]
 
     barrier = pltpu.get_barrier_semaphore()
-    everyone = [partner, xpeer] + ypeer + zpeer + crossy + crossz + back + forth
+    everyone = [partner, xpeer] + ypeer + zpeer + crossy + back + forth
     for d in everyone:
         pl.semaphore_signal(barrier, inc=1, device_id=d, device_id_type=MESH)
 
@@ -196,8 +193,6 @@
     for p in range(PAIRS):
         bias2[p] = whole_bias[:, 256 * p : 256 * p + 256]
 
-    wperm[...] = nn(perm[...], wqkv[...]).astype(BF16)
-    gacc[...] = jnp.zeros_like(gacc)
     for g in range(len(GROUPS)):
         groups[g][0][...] = jnp.zeros_like(groups[g][0])
     zero_tail = jnp.zeros((RP - ROWS, C), BF16)
@@ -365,28 +360,26 @@
                     place[w] < SLOTS, res[slot, at, :], win[w, at, lane0 : lane0 + C]
                 )
 
-        for w in range(wcols - 1, nwin, wcols):
+        for w in range(nwin - wcols, nwin):
+            place_window(w)
+        for r in range(HALF_LAT):
+            ors[o, r] = of[o, lat_dev + r, 0:lon_dev, :].astype(BF16)
+        rows = send(ors.at[o], orr.at[o], os_.at[o, 1], or_.at[o, 1], forth[1])
+        for r in range(HALF_LAT):
+            colf[6 * r : 6 * r + 6, 0:C] = of[o, lat_dev + r, lon_dev : lon_dev + HALF_LON, :]
+        colf[8:16, C : C + 128] = jnp.zeros((8, 128), F32)
+        for j in range(8):
+            colf[j : j + 1, C : C + 128] = colf[16 + j // 4 : 17 + j // 4, 128 * (j % 4) : 128 * (j % 4) + 128]
+        occs[o] = colf[0:16, 0 : C + 128].astype(BF16)
+        corner = send(occs.at[o], occ.at[o], os_.at[o, 2], or_.at[o, 2], forth[2])
+        for w in range(wcols - 1, nwin - wcols, wcols):
             place_window(w)
         colf[88:96, 0:C] = jnp.zeros((8, C), F32)
         for r in range(HALF_LAT, lat_dev):
             at = 6 * (r - HALF_LAT)
             colf[at : at + 6, 0:C] = of[o, r, lon_dev : lon_dev + HALF_LON, :]
         ocs[o] = colf[0:96, 0:C].astype(BF16)
-        for r in range(HALF_LAT):
-            colf[6 * r : 6 * r + 6, 0:C] = of[o, lat_dev + r, lon_dev : lon_dev + HALF_LON, :]
-        colf[8:16, C : C + 128] = jnp.zeros((8, 128), F32)
-        for j in range(8):
-            colf[j : j + 1, C : C + 128] = colf[16 + j // 4 : 17 + j // 4, 128 * (j % 4) : 128 * (j % 4) + 128]
-        occs[o] = colf[0:16, 0 : C + 128].astype(BF16)
-        copies = [
-            send(ocs.at[o], ocr.at[o], os_.at[o, 0], or_.at[o, 0], forth[0]),
-            send(occs.at[o], occ.at[o], os_.at[o, 2], or_.at[o, 2], forth[2]),
-        ]
-        for w in range(nwin - wcols, nwin - 1):
-            place_window(w)
-        for r in range(HALF_LAT):
-            ors[o, r] = of[o, lat_dev + r, 0:lon_dev, :].astype(BF16)
-        copies.insert(1, send(ors.at[o], orr.at[o], os_.at[o, 1], or_.at[o, 1], forth[1]))
+        copies = [send(ocs.at[o], ocr.at[o], os_.at[o, 0], or_.at[o, 0], forth[0]), rows, corner]
         for w in range(nwin - wcols):
             if w % wcols < wcols - 1:
                 place_window(w)
@@ -428,24 +421,14 @@
     gm[...] = nt(gz[0:ROWS, :], wproj[...]).astype(BF16)
     ntp[...] = nt(perm[...], normed[...]).astype(BF16)
 
-    def gain_part(c, rows, product):
-        weight = [wperm[rows, 384 * (c - 1) + 128 * i : 384 * (c - 1) + 128 * i + 128].astype(F32) for i in range(3)]
-        gacc[rows, :] += sum(product[:, 128 * i : 128 * i + 128] * weight[i] for i in range(3))
-
     def chunk_start(c, lhs, rhs):
         asend, arecv, own = chunks[c][0:3]
         right = rhs[...] if c == 0 else rhs[:, 384 * (c - 1) : 384 * c]
         other = pl.ds(pl.multiple_of((1 - core) * half, half), half)
         mine = pl.ds(pl.multiple_of(core * half, half), half)
-        product = nn(lhs[other, :], right)
-        asend[...] = product.astype(BF16)
+        asend[...] = nn(lhs[other, :], right).astype(BF16)
         copy = send(asend, arecv, as_.at[c], ar.at[c], partner)
-        if c > 0:
-            gain_part(c, other, product)
-        product = nn(lhs[mine, :], right)
-        own[...] = product
-        if c > 0:
-            gain_part(c, mine, product)
+        own[...] = nn(lhs[mine, :], right)
         return [copy]
 
     def chunk_y(c, copies):
@@ -497,45 +480,6 @@
             send(zsend.at[(z + d) % nz], zrecv.at[d - 1], zs.at[g, d - 1], zr.at[g, d - 1], zpeer[d - 1])
             for d in range(1, nz)
         ]
-
-    def last_send(copies):
-        lastown[...] = jnp.zeros_like(lastown)
-        first = 0
-        for c in LAST:
-            own, ysend, yrecv = chunks[c][2:5]
-            s = own[pl.ds(pl.multiple_of(y * ysz, ysz), ysz), :]
-            for d in range(1, ny):
-                copies[c][d - 1].wait_recv()
-                s = s + yrecv[d - 1].astype(F32)
-            for j in range(nxz):
-                part = s[share * j : share * j + share]
-                for q in range(cols[c] // 128):
-                    at = share * (first + q)
-                    lastown[j, at : at + share, :] = part[:, 128 * q : 128 * q + 128]
-            first += cols[c] // 128
-        lastsend[...] = lastown[...].astype(BF16)
-        out = []
-        for a in range(nx):
-            for d in range(nz):
-                if (a, d) == (0, 0):
-                    continue
-                to = (xpeer if d == 0 else crossz[d - 1]) if a else zpeer[d - 1]
-                j = ((xh + a) % nx) * nz + (z + d) % nz
-                i = a * nz + d - 1
-                out.append(send(lastsend.at[j], lastrecv.at[i], ls.at[i], lr.at[i], to))
-        return out
-
-    def last_end(copies):
-        s = lastown[xh * nz + z]
-        for i, copy in enumerate(copies):
-            copy.wait_recv()
-            s = s + lastrecv[i].astype(F32)
-        first = 0
-        for c in LAST:
-            for q in range(cols[c] // 128):
-                at = share * (first + q)
-                gqkv[:, C * q + 128 * (c - 1) : C * q + 128 * c] = s[at : at + share]
-            first += cols[c] // 128
 
     def group_end(g, copies):
         zown, zsend, zrecv = groups[g]
@@ -589,6 +533,7 @@
         if p >= 2:
             st[p - 2] = chunk_x(p - 2, st[p - 2])
 
+    smy, sma, smx, smz = sums
     stacked = jnp.concatenate([bacc[h // 2, :, 128 * (h % 2) : 128 * (h % 2) + 128] for h in range(HEADS)], axis=0)
     by_place = sum(nn(v, self_[...]) for v in pieces(stacked, 2))
     by_place = jnp.concatenate([by_place[TP * h : TP * h + TP] for h in range(HEADS)], axis=1)
@@ -596,24 +541,14 @@
     for h in range(HEADS):
         wide = jnp.concatenate([spread[:, 128 * h : 128 * h + 128], jnp.zeros((128, 128), F32)], axis=1)
         sums[0][core * ny + y, h : h + 1, 0:256] = jnp.sum(pltpu.roll(wide, 0, 1, stride=1, stride_axis=0), axis=0, keepdims=True)
-    gain_row = sum(tn(v, perm[...]) for v in pieces(gacc[...], 2))
-    gain_row = jnp.sum(gain_row, axis=0, keepdims=True) / gain
-    smy, sma, smx, smz = sums
-    slot = core * ny + y
-    sm = smy.at[slot]
-    sm[4:8, 256:384] = jnp.zeros((4, 128), F32)
-    for j in range(4):
-        sm[j : j + 1, 256:384] = gain_row[:, 128 * j : 128 * j + 128]
-    copies = [
-        send(sm, sm, ss.at[i], sr.at[i], to) for i, to in enumerate([partner] + ypeer + crossy)
-    ]
-    st[4] = chunk_y(4, st[4])
-    st[2] = chunk_x(2, st[2])
     for part in range(2):
         rows = slice(part * ROWS // 2, (part + 1) * ROWS // 2)
         gnacc[rows, :] = nt(dp3[rows, :], wqkv[...])
-
-    def norm_back(k, carry):
+        if part == 0:
+            st[4] = chunk_y(4, st[4])
+            st[2] = chunk_x(2, st[2])
+
+    def norm_back(k, total):
         w = idx[k]
         rows = rows_of(k)
         gn = gnacc[rows, :]
@@ -623,10 +558,22 @@
         mid = g - jnp.mean(g, axis=1, keepdims=True) - hat * jnp.mean(prod, axis=1, keepdims=True)
         inv = jnp.concatenate([invd[rows, :]] * 4, axis=1)
         res[k] = win[w, :, D0 : D0 + C] + inv * mid
-        return carry
-
-    lax.fori_loop(0, SLOTS // 3, by_three(norm_back), 0)
+        return total + jnp.sum(gn * hat, axis=0, keepdims=True)
+
+    gsum = lax.fori_loop(0, SLOTS // 3, by_three(norm_back), jnp.zeros((1, C), F32))
+    slot = core * ny + y
+    smy[slot, 4:8, 256:384] = jnp.zeros((4, 128), F32)
+    for j in range(4):
+        smy[slot, j : j + 1, 256:384] = gsum[:, 128 * j : 128 * j + 128]
+    sm = smy.at[slot]
+    copies = [
+        send(sm, sm, ss.at[i], sr.at[i], to) for i, to in enumerate([partner] + ypeer + crossy)
+    ]
     out_copies.append(window_back(1, D0))
+    st[3] = chunk_x(3, st[3])
+    chunk_z(0, st[0])
+    chunk_z(1, st[1])
+    st[4] = chunk_x(4, st[4])
     for copy in copies:
         copy.wait_recv()
     acc = smy[0]
@@ -634,12 +581,13 @@
         acc = acc + smy[j]
     sma[...] = acc
     copy = send(sma, smx, ss.at[2 * ny - 1], sr.at[2 * ny - 1], xpeer)
-    last = last_send(st)
-    for c in GROUPS[0]:
-        chunk_z(c, st[c])
+    chunk_z(2, st[2])
     group0 = group_send(0)
     finish(0, out_copies[0], upd)
     stores[0].start()
+    chunk_z(3, st[3])
+    chunk_z(4, st[4])
+    group1 = group_send(1)
     copy.wait_recv()
     smz[z] = sma[...] + smx[...]
     copies = [
@@ -648,7 +596,7 @@
     group_end(0, group0)
     finish(1, out_copies[1], gin)
     stores[1].start()
-    last_end(last)
+    group_end(1, group1)
     for copy in copies:
         copy.wait_recv()
     acc = smz[0]
@@ -775,8 +723,6 @@
             vm((RP, 3 * C), BF16),
             vm((ROWS, C), F32),
             vm((PAIRS, TP, 256), F32),
-            vm((C, 3 * C), BF16),
-            vm((C, 128), F32),
             vm((SLOTS, TP, C), F32),
             vm((2, lat_dev + 3, 56, C), F32),
             vm((2, 96, C), BF16),
@@ -800,15 +746,13 @@
         for members in GROUPS:
             rows = -(-share * sum(cols[c] // 128 for c in members) // 16) * 16
             scratch += [vm((nz, rows, 128), F32), vm((nz, rows, 128), BF16), vm((nz - 1, rows, 128), BF16)]
-        rows = -(-share * sum(cols[c] // 128 for c in LAST) // 16) * 16
-        scratch += [vm((nxz, rows, 128), F32), vm((nxz, rows, 128), BF16), vm((nxz - 1, rows, 128), BF16)]
         sm = (8, 384)
         scratch += [vm((2 * ny,) + sm, F32), vm(sm, F32), vm(sm, F32), vm((nz,) + sm, F32)]
         nc = len(cols)
         small = 2 * ny + nz
         scratch += [
             dma(2, 3), dma(2, 3), dma(3), dma(3), dma(2, 3), dma(2, 3), dma(nc), dma(nc), dma(nc, ny - 1),
-            dma(nc, ny - 1), dma(nc), dma(nc), dma(nc, nz - 1), dma(nc, nz - 1), dma(small), dma(small), dma(nxz - 1), dma(nxz - 1), dma(23), dma(6),
+            dma(nc, ny - 1), dma(nc), dma(nc), dma(nc, nz - 1), dma(nc, nz - 1), dma(small), dma(small), dma(23), dma(6),
         ]
         anywhere = pl.BlockSpec(memory_space=pl.ANY)
         outs = pl.pallas_call(

time: 58.4 us -> 58.2 us (level)
  the two profiles are of different devices: /device:TPU:1 before, /device:TPU:4 now
where the time goes in v10:
time: 58.2 us; the launch traced here: 57.2 us
  Pallas kernels  56.4 us (97%)
  between operations  0.8 us (1%)
    pallas_call x1, Pallas kernels, on_device(): pl.pallas_call(functools.partial(kernel, (ny, nx, nz), cols), out_shape=s...  53.9 us
    pallas_call x1, Pallas kernels, on_device(): pl.pallas_call(hand_over, out_shape=shapes, in_specs=[anywhere] * 6, out_...  2.49 us

profile of v10, /device:TPU:4, one launch (start us, length us, event | category | flops | bytes accessed | tf_op | source)
XLA Modules:
  0.0 57.2 jit_solution(6232356348619885482)
XLA Ops:
  0.6 53.9 %shard_map.154 = (bf16[18,48,512]{2,1,0:T(8,128)(2,1)}, bf16[18,48,512]{2,1,0:T(8,128)(2,1)}, f32[1,512]{1,0:T(1,128)}, f32[8,253]{1,0:T(8,128)}, f32[4,1536]{1,0:T(4,128)}, /*index=5*/f32[4,512]{1,0:T(4,128)}) custom-call(bf16[18,48,512]{2,1,0:T(8,128)(2,1)} %refs_0_.1, s32[18,48]{1,0:T(8,128)} %refs_1_.1, bf16[18,48,512]{2,1,0:T(8,128)(2,1)} %refs_2_.1, ...), custom_call_target="tpu_custom_call" | custom-call | tf_op jit(solution)/shard_map/pallas_call | solution.py:758
  54.5 2.5 %shard_map.155 = (bf16[18,48,512]{2,1,0:T(8,128)(2,1)}, bf16[18,48,512]{2,1,0:T(8,128)(2,1)}, f32[1,512]{1,0:T(1,128)}, f32[8,253]{1,0:T(8,128)}, f32[4,1536]{1,0:T(4,128)}, /*index=5*/f32[4,512]{1,0:T(4,128)}) custom-call(bf16[18,48,512]{2,1,0:T(8,128)(2,1)} %get-tuple-element.18.refs_0_, bf16[18,48,512]{2,1,0:T(8,128)(2,1)} %get-tuple-element.19.refs_1_, ...), custom_call_target="tpu_custom_call" | custom-call | tf_op jit(solution)/shard_map/pallas_call | solution.py:771

commit v11 on v10

--- a/solution.py
+++ b/solution.py
@@ -97,19 +97,19 @@
     back = [dev(west, lat), dev(lon, north), dev(west, north)]
     forth = [dev(east, lat), dev(lon, south), dev(east, south)]
 
-    barrier = pltpu.get_barrier_semaphore()
-    everyone = [partner, xpeer] + ypeer + zpeer + crossy + back + forth
-    for d in everyone:
-        pl.semaphore_signal(barrier, inc=1, device_id=d, device_id_type=MESH)
-
     loads = [pltpu.make_async_copy(a, b, ins.at[i]) for i, (a, b) in enumerate(zip(given, held)) if i != 8]
     for p in range(PAIRS):
         for i in range(3):
             src = given[8].at[:, C * i + 128 * p : C * i + 128 * p + 128]
             dst = wqkv.at[:, 384 * p + 128 * i : 384 * p + 128 * i + 128]
             loads.append(pltpu.make_async_copy(src, dst, ins.at[11 + 3 * p + i]))
-    for load in loads:
-        load.start()
+    loads[0].start()
+    barrier = pltpu.get_barrier_semaphore()
+    everyone = back + forth + [partner, xpeer] + ypeer + zpeer + crossy
+    for d in everyone:
+        pl.semaphore_signal(barrier, inc=1, device_id=d, device_id_type=MESH)
+    loads[1].start()
+    loads[2].start()
 
     stores = [pltpu.make_async_copy(a, b, outs.at[i]) for i, (a, b) in enumerate(zip(staged, results))]
     sends = []
@@ -159,11 +159,13 @@
 
     xlanes, dlanes = slice(X0, X0 + C), slice(D0, D0 + C)
     loads[0].wait()
-    xcopies = halo_send(0, x_ref, given[0])
+    xcopies = halo_send(0, x_ref, x_ref)
     loads[1].wait()
     mcopies = [send(mask_ref, masks[i], ms.at[i], mr.at[i], back[i]) for i in range(3)]
+    for load in loads[3:]:
+        load.start()
     loads[2].wait()
-    dcopies = halo_send(1, dy_ref, given[2])
+    dcopies = halo_send(1, dy_ref, dy_ref)
     sea = spread_mask(mask_ref)
     for r in range(lat_dev):
         frame[r, 0:lon_dev, X0 : X0 + C] = x_ref[r].astype(F32)
@@ -414,12 +416,12 @@
     lax.fori_loop(0, SLOTS // 3, by_three(updated_step), 0)
     out_copies = [window_back(0, X0)]
 
+    ntp[...] = nt(perm[...], normed[...]).astype(BF16)
+    mtp[...] = nt(perm[...], mixed[...]).astype(BF16)
     halo_land(1, dlanes, dcopies)
     for w in outer:
         cut(w, dlanes)
     lax.fori_loop(0, SLOTS // 3, by_three(dy_step), 0)
-    gm[...] = nt(gz[0:ROWS, :], wproj[...]).astype(BF16)
-    ntp[...] = nt(perm[...], normed[...]).astype(BF16)
 
     def chunk_start(c, lhs, rhs):
         asend, arecv, own = chunks[c][0:3]
@@ -497,9 +499,9 @@
                 else:
                     gqkv[:, C * q + 128 * (c - 1) : C * q + 128 * c] = block
 
-    mtp[...] = nt(perm[...], mixed[...]).astype(BF16)
     st = {}
     st[0] = chunk_start(0, mtp, gz)
+    gm[...] = nt(gz[0:ROWS, :], wproj[...]).astype(BF16)
 
     def backward(p):
         ks = list(range(SLOTS))
@@ -528,8 +530,8 @@
 
     for p in range(PAIRS):
         backward(p)
+        st[p] = chunk_y(p, st[p])
         st[p + 1] = chunk_start(p + 1, ntp, dp3)
-        st[p] = chunk_y(p, st[p])
         if p >= 2:
             st[p - 2] = chunk_x(p - 2, st[p - 2])
 

time: 58.2 us -> 57.7 us (level)
  no operation moved by 1% of the time
where the time goes in v11:
time: 57.7 us; the launch traced here: 57 us
  Pallas kernels  56.2 us (97%)
  between operations  0.8 us (1%)
    pallas_call x1, Pallas kernels, on_device(): pl.pallas_call(functools.partial(kernel, (ny, nx, nz), cols), out_shape=s...  53.7 us
    pallas_call x1, Pallas kernels, on_device(): pl.pallas_call(hand_over, out_shape=shapes, in_specs=[anywhere] * 6, out_...  2.49 us

profile of v11, /device:TPU:4, one launch (start us, length us, event | category | flops | bytes accessed | tf_op | source)
XLA Modules:
  0.0 57.0 jit_solution(17300623047785318075)
XLA Ops:
  0.6 53.7 %shard_map.154 = (bf16[18,48,512]{2,1,0:T(8,128)(2,1)}, bf16[18,48,512]{2,1,0:T(8,128)(2,1)}, f32[1,512]{1,0:T(1,128)}, f32[8,253]{1,0:T(8,128)}, f32[4,1536]{1,0:T(4,128)}, /*index=5*/f32[4,512]{1,0:T(4,128)}) custom-call(bf16[18,48,512]{2,1,0:T(8,128)(2,1)} %refs_0_.1, s32[18,48]{1,0:T(8,128)} %refs_1_.1, bf16[18,48,512]{2,1,0:T(8,128)(2,1)} %refs_2_.1, ...), custom_call_target="tpu_custom_call" | custom-call | tf_op jit(solution)/shard_map/pallas_call | solution.py:760
  54.3 2.5 %shard_map.155 = (bf16[18,48,512]{2,1,0:T(8,128)(2,1)}, bf16[18,48,512]{2,1,0:T(8,128)(2,1)}, f32[1,512]{1,0:T(1,128)}, f32[8,253]{1,0:T(8,128)}, f32[4,1536]{1,0:T(4,128)}, /*index=5*/f32[4,512]{1,0:T(4,128)}) custom-call(bf16[18,48,512]{2,1,0:T(8,128)(2,1)} %get-tuple-element.18.refs_0_, bf16[18,48,512]{2,1,0:T(8,128)(2,1)} %get-tuple-element.19.refs_1_, ...), custom_call_target="tpu_custom_call" | custom-call | tf_op jit(solution)/shard_map/pallas_call | solution.py:773

commit v12 on v11

--- a/solution.py
+++ b/solution.py
@@ -73,7 +73,7 @@
     tb, bias2, madd, xhat, invd, normed, gz, gm, packed, mixed, ntp, mtp, probs, dp3, gnacc, bacc = take(16)
     res, of = take(2)
     ocs, ors, occs, ocr, orr, occ = take(6)
-    chunks = [take(8) for _ in range(nchunk)]
+    chunks = [take(10) for _ in range(nchunk)]
     groups = [take(3) for _ in range(len(GROUPS))]
     sums = take(4)
     hs, hr, ms, mr, os_, or_, as_, ar, ys, yr, xs, xr, zs, zr, ss, sr = take(16)
@@ -433,26 +433,40 @@
         own[...] = nn(lhs[mine, :], right)
         return [copy]
 
+    def y_piece(c, d):
+        return chunks[c][2][pl.ds(pl.multiple_of(((y + d) % ny) * ysz, ysz), ysz), :]
+
     def chunk_y(c, copies):
-        asend, arecv, own, ysend, yrecv = chunks[c][0:5]
+        asend, arecv, own, ysend, yvia = chunks[c][0:5]
         copies[0].wait_recv()
-        s = own[...] + arecv[...].astype(F32)
-        own[...] = s
-        ysend[...] = s.astype(BF16)
-        out = []
-        for d in range(1, ny):
-            start = pl.multiple_of(((y + d) % ny) * ysz, ysz)
-            out.append(
-                send(ysend.at[pl.ds(start, ysz)], yrecv.at[d - 1], ys.at[c, d - 1], yr.at[c, d - 1], ypeer[d - 1])
-            )
-        return out
+        own[...] += arecv[...].astype(F32)
+        ysend[...] = y_piece(c, 2).astype(BF16)
+        hy = ysz // 2
+        return [
+            send(ysend.at[0:hy], yvia.at[0], ys.at[c, 0], yr.at[c, 0], ypeer[ny - 2]),
+            send(ysend.at[hy:ysz], yvia.at[1], ys.at[c, 1], yr.at[c, 1], ypeer[0]),
+        ]
+
+    def chunk_near(c, copies):
+        yvia, nsend, nrecv = chunks[c][4:7]
+        hy = ysz // 2
+        copies[0].wait_recv()
+        before = y_piece(c, ny - 1)
+        nsend[0] = jnp.concatenate([before[0:hy] + yvia[0].astype(F32), before[hy:ysz]], axis=0).astype(BF16)
+        copies[1].wait_recv()
+        after = y_piece(c, 1)
+        nsend[1] = jnp.concatenate([after[0:hy], after[hy:ysz] + yvia[1].astype(F32)], axis=0).astype(BF16)
+        return [
+            send(nsend.at[0], nrecv.at[0], ys.at[c, 2], yr.at[c, 2], ypeer[ny - 2]),
+            send(nsend.at[1], nrecv.at[1], ys.at[c, 3], yr.at[c, 3], ypeer[0]),
+        ]
 
     def chunk_x(c, copies):
-        own, ysend, yrecv, xsend, xrecv, xown = chunks[c][2:8]
-        s = own[pl.ds(pl.multiple_of(y * ysz, ysz), ysz), :]
-        for d in range(1, ny):
-            copies[d - 1].wait_recv()
-            s = s + yrecv[d - 1].astype(F32)
+        nrecv, xsend, xrecv, xown = chunks[c][6:10]
+        s = y_piece(c, 0)
+        for d in range(2):
+            copies[d].wait_recv()
+            s = s + nrecv[d].astype(F32)
         top, low_half = s[0 : ysz // 2], s[ysz // 2 : ysz]
         first = xh == 0
         xsend[...] = jnp.where(first, low_half, top).astype(BF16)
@@ -464,7 +478,7 @@
         return g, sum(cols[m] // 128 for m in GROUPS[g] if m < c)
 
     def chunk_z(c, copies):
-        xsend, xrecv, xown = chunks[c][5:8]
+        xsend, xrecv, xown = chunks[c][7:10]
         g, first = blocks_before(c)
         zown = groups[g][0]
         copies[0].wait_recv()
@@ -531,9 +545,11 @@
     for p in range(PAIRS):
         backward(p)
         st[p] = chunk_y(p, st[p])
+        if p >= 1:
+            st[p - 1] = chunk_near(p - 1, st[p - 1])
         st[p + 1] = chunk_start(p + 1, ntp, dp3)
-        if p >= 2:
-            st[p - 2] = chunk_x(p - 2, st[p - 2])
+        if p >= 3:
+            st[p - 3] = chunk_x(p - 3, st[p - 3])
 
     smy, sma, smx, smz = sums
     stacked = jnp.concatenate([bacc[h // 2, :, 128 * (h % 2) : 128 * (h % 2) + 128] for h in range(HEADS)], axis=0)
@@ -548,7 +564,8 @@
         gnacc[rows, :] = nt(dp3[rows, :], wqkv[...])
         if part == 0:
             st[4] = chunk_y(4, st[4])
-            st[2] = chunk_x(2, st[2])
+            st[3] = chunk_near(3, st[3])
+            st[1] = chunk_x(1, st[1])
 
     def norm_back(k, total):
         w = idx[k]
@@ -571,11 +588,12 @@
     copies = [
         send(sm, sm, ss.at[i], sr.at[i], to) for i, to in enumerate([partner] + ypeer + crossy)
     ]
+    st[4] = chunk_near(4, st[4])
+    st[2] = chunk_x(2, st[2])
     out_copies.append(window_back(1, D0))
     st[3] = chunk_x(3, st[3])
     chunk_z(0, st[0])
     chunk_z(1, st[1])
-    st[4] = chunk_x(4, st[4])
     for copy in copies:
         copy.wait_recv()
     acc = smy[0]
@@ -585,6 +603,7 @@
     copy = send(sma, smx, ss.at[2 * ny - 1], sr.at[2 * ny - 1], xpeer)
     chunk_z(2, st[2])
     group0 = group_send(0)
+    st[4] = chunk_x(4, st[4])
     finish(0, out_copies[0], upd)
     stores[0].start()
     chunk_z(3, st[3])
@@ -739,22 +758,24 @@
                 vm((half, n), BF16),
                 vm((half, n), BF16),
                 vm((half, n), F32),
-                vm((half, n), BF16),
-                vm((ny - 1, ysz, n), BF16),
+                vm((ysz, n), BF16),
+                vm((2, ysz // 2, n), BF16),
+                vm((2, ysz, n), BF16),
+                vm((2, ysz, n), BF16),
                 vm((ysz // 2, n), BF16),
                 vm((ysz // 2, n), BF16),
                 vm((ysz // 2, n), F32),
             ]
         for members in GROUPS:
             rows = -(-share * sum(cols[c] // 128 for c in members) // 16) * 16
-            scratch += [vm((nz, rows, 128), F32), vm((nz, rows, 128), BF16), vm((nz - 1, rows, 128), BF16)]
+            scratch += [vm((nz, rows, 128), F32), vm((nz, rows, 128), BF16), vm((max(nz - 1, 1), rows, 128), BF16)]
         sm = (8, 384)
         scratch += [vm((2 * ny,) + sm, F32), vm(sm, F32), vm(sm, F32), vm((nz,) + sm, F32)]
         nc = len(cols)
         small = 2 * ny + nz
         scratch += [
-            dma(2, 3), dma(2, 3), dma(3), dma(3), dma(2, 3), dma(2, 3), dma(nc), dma(nc), dma(nc, ny - 1),
-            dma(nc, ny - 1), dma(nc), dma(nc), dma(nc, nz - 1), dma(nc, nz - 1), dma(small), dma(small), dma(23), dma(6),
+            dma(2, 3), dma(2, 3), dma(3), dma(3), dma(2, 3), dma(2, 3), dma(nc), dma(nc), dma(nc, 4),
+            dma(nc, 4), dma(nc), dma(nc), dma(nc, max(nz - 1, 1)), dma(nc, max(nz - 1, 1)), dma(small), dma(small), dma(23), dma(6),
         ]
         anywhere = pl.BlockSpec(memory_space=pl.ANY)
         outs = pl.pallas_call(

time: 57.7 us -> 59.3 us (1.028)
  Pallas kernels: 56.2 us -> 57.4 us
    pallas_call x1, Pallas kernels: 53.7 us -> 54.9 us  [on_device(): pl.pallas_call(functools.partial(kernel, (ny, nx, nz), cols), out_shape=s...]
where the time goes in v12:
time: 59.3 us; the launch traced here: 58.2 us
  Pallas kernels  57.4 us (97%)
  between operations  0.8 us (1%)
    pallas_call x1, Pallas kernels, on_device(): pl.pallas_call(functools.partial(kernel, (ny, nx, nz), cols), out_shape=s...  54.9 us
    pallas_call x1, Pallas kernels, on_device(): pl.pallas_call(hand_over, out_shape=shapes, in_specs=[anywhere] * 6, out_...  2.49 us

profile of v12, /device:TPU:4, one launch (start us, length us, event | category | flops | bytes accessed | tf_op | source)
XLA Modules:
  0.0 58.2 jit_solution(10493141574263207413)
XLA Ops:
  0.6 54.9 %shard_map.154 = (bf16[18,48,512]{2,1,0:T(8,128)(2,1)}, bf16[18,48,512]{2,1,0:T(8,128)(2,1)}, f32[1,512]{1,0:T(1,128)}, f32[8,253]{1,0:T(8,128)}, f32[4,1536]{1,0:T(4,128)}, /*index=5*/f32[4,512]{1,0:T(4,128)}) custom-call(bf16[18,48,512]{2,1,0:T(8,128)(2,1)} %refs_0_.1, s32[18,48]{1,0:T(8,128)} %refs_1_.1, bf16[18,48,512]{2,1,0:T(8,128)(2,1)} %refs_2_.1, ...), custom_call_target="tpu_custom_call" | custom-call | tf_op jit(solution)/shard_map/pallas_call | solution.py:781
  55.5 2.5 %shard_map.155 = (bf16[18,48,512]{2,1,0:T(8,128)(2,1)}, bf16[18,48,512]{2,1,0:T(8,128)(2,1)}, f32[1,512]{1,0:T(1,128)}, f32[8,253]{1,0:T(8,128)}, f32[4,1536]{1,0:T(4,128)}, /*index=5*/f32[4,512]{1,0:T(4,128)}) custom-call(bf16[18,48,512]{2,1,0:T(8,128)(2,1)} %get-tuple-element.18.refs_0_, bf16[18,48,512]{2,1,0:T(8,128)(2,1)} %get-tuple-element.19.refs_1_, ...), custom_call_target="tpu_custom_call" | custom-call | tf_op jit(solution)/shard_map/pallas_call | solution.py:794

commit v13 on v11

--- a/solution.py
+++ b/solution.py
@@ -315,6 +315,36 @@
         packed[rows, :] = nn(normed[rows, :], wqkv[...]).astype(BF16)
         lax.fori_loop(first // 3, last // 3, attend, 0)
 
+    def backward(chains):
+        d2s, dps = [], []
+        for k, p in chains:
+            rows = slice(TP * k, TP * k + TP)
+            d2s.append(both_heads(gm[rows, 128 * p : 128 * p + 128], one_lo, one_hi))
+            dps.append(nt(packed[rows, 384 * p + 256 : 384 * p + 384], d2s[-1]))
+        dss, dvs = [], []
+        for (k, p), d2, dp in zip(chains, d2s, dps):
+            pr = probs[k * PAIRS + p]
+            t = pr * dp
+            dss.append(t - pr * jnp.sum(t, axis=0, keepdims=True))
+            dvs.append(nn(pr.astype(BF16), d2))
+        for p in sorted({p for _, p in chains}):
+            bacc[p] += functools.reduce(lambda a, b: a + b, [ds for (_, q), ds in zip(chains, dss) if q == p])
+        dqs = []
+        for (k, p), ds, dv in zip(chains, dss, dvs):
+            rows = slice(TP * k, TP * k + TP)
+            ds = ds.astype(BF16)
+            q2 = both_heads(packed[rows, 384 * p : 384 * p + 128], q_lo, q_hi)
+            dqs.append(tn(packed[rows, 384 * p + 128 : 384 * p + 256], ds))
+            dp3[rows, 384 * p + 128 : 384 * p + 256] = nn(ds, q2).astype(BF16)
+            dp3[rows, 384 * p + 256 : 384 * p + 384] = dv.astype(BF16)
+        for (k, p), dq in zip(chains, dqs):
+            dp3[TP * k : TP * k + TP, 384 * p : 384 * p + 128] = (own_head(dq) * 0.125).astype(BF16)
+
+    def grad_mixed(first, last):
+        lax.fori_loop(first // 3, last // 3, by_three(dy_step), 0)
+        rows = slice(first * TP, last * TP)
+        gm[rows, :] = nt(gz[rows, :], wproj[...]).astype(BF16)
+
     for w in inner:
         cut(w, slice(0, FW))
         active[w] = holds_sea(w)
@@ -322,6 +352,9 @@
     for k in range(EARLY):
         slot_window(k, list(zip(inner, inner_rank)))
     forward(0, EARLY)
+    bacc[...] = jnp.zeros_like(bacc)
+    grad_mixed(0, EARLY)
+    backward([(k, p) for k in range(EARLY) for p in range(PAIRS)])
 
     mlanes = slice(M0, M0 + 128)
     for copy in mcopies:
@@ -421,7 +454,7 @@
     halo_land(1, dlanes, dcopies)
     for w in outer:
         cut(w, dlanes)
-    lax.fori_loop(0, SLOTS // 3, by_three(dy_step), 0)
+    grad_mixed(EARLY, SLOTS)
 
     def chunk_start(c, lhs, rhs):
         asend, arecv, own = chunks[c][0:3]
@@ -501,35 +534,9 @@
 
     st = {}
     st[0] = chunk_start(0, mtp, gz)
-    gm[...] = nt(gz[0:ROWS, :], wproj[...]).astype(BF16)
-
-    def backward(p):
-        ks = list(range(SLOTS))
-        d2s, dps = [], []
-        for k in ks:
-            rows = slice(TP * k, TP * k + TP)
-            d2s.append(both_heads(gm[rows, 128 * p : 128 * p + 128], one_lo, one_hi))
-            dps.append(nt(packed[rows, 384 * p + 256 : 384 * p + 384], d2s[-1]))
-        dss, dvs = [], []
-        for k in ks:
-            pr = probs[k * PAIRS + p]
-            t = pr * dps[k]
-            dss.append(t - pr * jnp.sum(t, axis=0, keepdims=True))
-            dvs.append(nn(pr.astype(BF16), d2s[k]))
-        bacc[p] = functools.reduce(lambda a, b: a + b, dss)
-        dqs = []
-        for k in ks:
-            rows = slice(TP * k, TP * k + TP)
-            ds = dss[k].astype(BF16)
-            q2 = both_heads(packed[rows, 384 * p : 384 * p + 128], q_lo, q_hi)
-            dqs.append(tn(packed[rows, 384 * p + 128 : 384 * p + 256], ds))
-            dp3[rows, 384 * p + 128 : 384 * p + 256] = nn(ds, q2).astype(BF16)
-            dp3[rows, 384 * p + 256 : 384 * p + 384] = dvs[k].astype(BF16)
-        for k in ks:
-            dp3[TP * k : TP * k + TP, 384 * p : 384 * p + 128] = (own_head(dqs[k]) * 0.125).astype(BF16)
 
     for p in range(PAIRS):
-        backward(p)
+        backward([(k, p) for k in range(EARLY, SLOTS)])
         st[p] = chunk_y(p, st[p])
         st[p + 1] = chunk_start(p + 1, ntp, dp3)
         if p >= 2:

time: 57.7 us -> 57.4 us (level)
  no operation moved by 1% of the time
where the time goes in v13:
time: 57.4 us; the launch traced here: 57 us
  Pallas kernels  56.2 us (98%)
  between operations  0.8 us (1%)
    pallas_call x1, Pallas kernels, on_device(): pl.pallas_call(functools.partial(kernel, (ny, nx, nz), cols), out_shape=s...  53.7 us
    pallas_call x1, Pallas kernels, on_device(): pl.pallas_call(hand_over, out_shape=shapes, in_specs=[anywhere] * 6, out_...  2.49 us

profile of v13, /device:TPU:4, one launch (start us, length us, event | category | flops | bytes accessed | tf_op | source)
XLA Modules:
  0.0 57.0 jit_solution(17382491420175903927)
XLA Ops:
  0.6 53.7 %shard_map.154 = (bf16[18,48,512]{2,1,0:T(8,128)(2,1)}, bf16[18,48,512]{2,1,0:T(8,128)(2,1)}, f32[1,512]{1,0:T(1,128)}, f32[8,253]{1,0:T(8,128)}, f32[4,1536]{1,0:T(4,128)}, /*index=5*/f32[4,512]{1,0:T(4,128)}) custom-call(bf16[18,48,512]{2,1,0:T(8,128)(2,1)} %refs_0_.1, s32[18,48]{1,0:T(8,128)} %refs_1_.1, bf16[18,48,512]{2,1,0:T(8,128)(2,1)} %refs_2_.1, ...), custom_call_target="tpu_custom_call" | custom-call | tf_op jit(solution)/shard_map/pallas_call | solution.py:767
  54.4 2.5 %shard_map.155 = (bf16[18,48,512]{2,1,0:T(8,128)(2,1)}, bf16[18,48,512]{2,1,0:T(8,128)(2,1)}, f32[1,512]{1,0:T(1,128)}, f32[8,253]{1,0:T(8,128)}, f32[4,1536]{1,0:T(4,128)}, /*index=5*/f32[4,512]{1,0:T(4,128)}) custom-call(bf16[18,48,512]{2,1,0:T(8,128)(2,1)} %get-tuple-element.18.refs_0_, bf16[18,48,512]{2,1,0:T(8,128)(2,1)} %get-tuple-element.19.refs_1_, ...), custom_call_target="tpu_custom_call" | custom-call | tf_op jit(solution)/shard_map/pallas_call | solution.py:780
